TPU v7x, 128 devices: a whole 4x4x4 slice. The times are simulated.
128 devices in a mesh: ctx: 16 (over z, x_lo, core), tp: 8 (over x_hi, y).
Axes of the slice: x: 4 (x_hi: 2, x_lo: 2; x = x_hi * 2 + x_lo), y: 4, z: 4, core: 2. Of those that a mesh axis runs over, the one named last changes fastest.
Arguments:
- tokens: bfloat16 [2, 2048, 2048], P(None, 'ctx', 'tp'), may hold values from -6 to 6
- norm1_gain: float32 [2048], replicated, may hold values from 0.5 to 1.5
- router_attn: bfloat16 [2048, 4], replicated, may hold values from -0.125 to 0.125
- w_query: bfloat16 [4, 2048, 2048], P(None, 'ctx', 'tp'), may hold values from -0.125 to 0.125
- w_key_value: bfloat16 [2048, 2, 2048], P('ctx', None, 'tp'), may hold values from -0.125 to 0.125
- w_out: bfloat16 [4, 2048, 2048], P(None, 'tp', 'ctx'), may hold values from -1 to 1
- norm2_gain: float32 [2048], replicated, may hold values from 0.5 to 1.5
- router_ffn: bfloat16 [2048, 4], replicated, may hold values from -0.125 to 0.125
- w_gate_up: bfloat16 [4, 2048, 2, 5632], P(None, 'ctx', None, 'tp'), may hold values from -0.125 to 0.125
- w_down: bfloat16 [4, 5632, 2048], P(None, 'tp', 'ctx'), may hold values from -0.078125 to 0.078125
- adapt_wide: float32 [2, 22, 16, 2048], P(None, None, None, ('ctx', 'tp'))
- adapt_heads: float32 [2, 10, 16, 2048], P(None, None, None, 'tp')
- adapt_ffn: float32 [2, 12, 16, 5632], P(None, None, None, 'tp')
- attention_routes: int32 [2, 2048, 2], P(None, 'ctx'), may hold values from 0 to 3, all different within a row
- feedforward_routes: int32 [2, 2048, 2], P(None, 'ctx'), may hold values from 0 to 3, all different within a row
- doc_lengths: int32 [2, 8], replicated, may hold values from 0 to 2048, as said below
- adapter_index: int32 [2], replicated, may hold values from 0 to 1, each once
- cotangent: bfloat16 [2, 2048, 2048], P(None, 'ctx', 'tp'), may hold values from -6 to 6
Outputs:
- mixed: bfloat16 [2, 2048, 2048], P(None, 'ctx', 'tp')
- grad_tokens: bfloat16 [2, 2048, 2048], P(None, 'ctx', 'tp')
- grad_wide: float32 [2, 22, 16, 2048], P(None, None, None, ('ctx', 'tp'))
- grad_heads: float32 [2, 10, 16, 2048], P(None, None, None, 'tp')
- grad_ffn: float32 [2, 12, 16, 5632], P(None, None, None, 'tp')
Inputs may be any that keep to these rules, and one draw needn't show every extreme that they name: `doc_lengths`: each row sums to at most 2048; positions past the sum are padding; in every draw one sequence, drawn from the seed, is a single document of 2048 positions. `attention_routes`: each token names 2 different attention experts. `feedforward_routes`: each token names 2 different feed-forward experts. `adapter_index`: each adapter set serves exactly one sequence.
All inputs are finite; a program needn't handle non-finite values.
Results may differ from a plain program's by a relative error of at most 0.03.
Values may be sent and summed in bfloat16 or wider, within the bound.
A program may use at most 384 MiB of HBM per device.

v0:
```python
import jax
import jax.numpy as jnp
from jax import lax
from jax.sharding import PartitionSpec as P

HEAD_DIM = 128
WINDOW = 1024


highest = lax.Precision.HIGHEST
eps = 1e-06
big_negative = -1e30


def rms_scale(values, gain):
    return values * lax.rsqrt(jnp.mean(values * values, axis=-1, keepdims=True) + eps) * gain


def norm_back(values, gain, grad_normed):
    inverse = lax.rsqrt(jnp.mean(values * values, axis=-1, keepdims=True) + eps)
    scaled = grad_normed * gain
    return inverse * scaled - values * inverse**3 * jnp.mean(
        scaled * values, axis=-1, keepdims=True
    )


def doc_layout(doc_lengths, positions):
    ends = jnp.cumsum(doc_lengths, axis=1)
    passed = positions[None, :, None] >= ends[:, None, :]
    doc_ids = jnp.sum(passed.astype(jnp.int32), axis=2)
    starting = jnp.sum(jnp.where(passed, doc_lengths[:, None, :], 0), axis=2)
    inside = positions[None, :] < ends[:, -1:]
    doc_ids = jnp.where(inside, doc_ids, -1 - positions[None, :])
    return (doc_ids, positions[None, :] - starting)


def rotate(values, offsets):
    half_dim = values.shape[-1] // 2
    frequency = 10000.0 ** (-2.0 * jnp.arange(half_dim, dtype=jnp.float32) / values.shape[-1])
    angles = offsets.astype(jnp.float32)[..., None] * frequency
    angles = angles.reshape(angles.shape[:2] + (1,) * (values.ndim - 3) + (half_dim,))
    cosine = jnp.cos(angles)
    sine_part = jnp.sin(angles)
    first_half = values[..., :half_dim]
    second_half = values[..., half_dim:]
    return jnp.concatenate(
        [
            first_half * cosine - second_half * sine_part,
            second_half * cosine + first_half * sine_part,
        ],
        axis=-1,
    )


def route_gates(logits, routes):
    return jax.nn.softmax(jnp.take_along_axis(logits, routes, axis=-1), axis=-1)


def gates_back(gates, grad_gates, routes, expert_count):
    inner_grad = gates * (grad_gates - jnp.sum(gates * grad_gates, axis=-1, keepdims=True))
    return jnp.sum(
        inner_grad[..., None] * jax.nn.one_hot(routes, expert_count, dtype=jnp.float32), axis=-2
    )


def arrange(routes, adapter_index, experts, adapters):
    seq_count, block_len, top_k = routes.shape
    group_key = routes.reshape(-1) * adapters + jnp.repeat(adapter_index, block_len * top_k)
    sort_order = jnp.argsort(group_key, stable=True)
    sorted_key = group_key[sort_order]
    onehot = (
        sorted_key[:, None] == jnp.arange(experts * adapters, dtype=jnp.int32)[None, :]
    ).astype(jnp.float32)
    counts = jnp.sum(onehot, axis=0).astype(jnp.int32)
    group_sizes = jnp.sum(counts.reshape(experts, adapters), axis=1)
    unsort = (
        jnp.zeros_like(sort_order)
        .at[sort_order]
        .set(jnp.arange(sort_order.shape[0], dtype=sort_order.dtype))
    )
    return (sort_order, sort_order // top_k, onehot, counts, group_sizes, unsort)


def ragged(left, right, group_sizes):
    return lax.ragged_dot(left, right, group_sizes, preferred_element_type=jnp.float32)


def ragged_exact(left, right, group_sizes):
    return lax.ragged_dot(
        left.astype(jnp.float32),
        right.astype(jnp.float32),
        group_sizes,
        precision=highest,
        preferred_element_type=jnp.float32,
    )


def groups_flat(factor, first_slot, slot_count):
    chosen = factor[:, first_slot : first_slot + slot_count]
    return jnp.swapaxes(chosen, 0, 1).reshape((slot_count * chosen.shape[0],) + chosen.shape[2:])


def ungroup(grouped, experts, adapters):
    return jnp.swapaxes(grouped.reshape((experts, adapters) + grouped.shape[1:]), 0, 1)


def group_outer(onehot, left_rows, right_rows):
    row_count, group_count = onehot.shape
    spread = (onehot[:, :, None] * left_rows[:, None, :]).reshape(
        row_count, group_count * left_rows.shape[1]
    )
    product = jnp.dot(spread.T, right_rows.astype(jnp.float32), precision=highest)
    return product.reshape(group_count, left_rows.shape[1], right_rows.shape[1])


def combine_pairs(sorted_rows, unsort, seq_count, block_len):
    unsorted = sorted_rows[unsort]
    return jnp.sum(unsorted.reshape(seq_count, block_len, -1, unsorted.shape[-1]), axis=2)


def own_slice(full_rows, part_width, tp_rank):
    return lax.dynamic_slice_in_dim(full_rows, tp_rank * part_width, part_width, 2)


def key_mask(query_pos, query_doc, key_pos, key_doc):
    same_doc = query_doc[:, :, None] == key_doc[:, None, :]
    near = (
        (key_pos[None, None, :] <= query_pos[None, :, None])
        & (query_pos[None, :, None] - key_pos[None, None, :] < WINDOW)
        & (key_pos[None, None, :] >= 0)
    )
    return (same_doc & near)[:, None]


def attend_add(carried, key_piece, key_pos, context):
    queries, query_pos, query_doc, doc_lengths = context
    seq_count, query_rows, width_here = queries.shape
    heads_here = carried[0].shape[1]
    head_dim = width_here // heads_here
    key_rows = key_piece.shape[1]
    key_doc = doc_layout(doc_lengths, jnp.maximum(key_pos, 0))[0]
    allowed = key_mask(query_pos, query_doc, key_pos, key_doc)

    def compute(running_state):
        running, peak, weight_sum = running_state
        query_split = queries.reshape(seq_count, query_rows, heads_here, head_dim)
        key_split = key_piece[:, :, :width_here].reshape(seq_count, key_rows, heads_here, head_dim)
        value_split = key_piece[:, :, width_here:].reshape(
            seq_count, key_rows, heads_here, head_dim
        )
        scores = jnp.einsum(
            "sqhd,skhd->shqk", query_split, key_split, preferred_element_type=jnp.float32
        ) * head_dim ** (-0.5)
        fresh = jnp.maximum(peak, jnp.max(jnp.where(allowed, scores, big_negative), axis=-1))
        weights = jnp.where(allowed, jnp.exp(scores - fresh[..., None]), 0.0)
        running = jnp.einsum(
            "shqk,skhd->shqd",
            weights.astype(jnp.bfloat16),
            value_split,
            preferred_element_type=jnp.float32,
        )
        return (running, fresh, jnp.sum(weights, axis=-1))

    def keep_state(running_state):
        return running_state

    return lax.cond(jnp.any(allowed), compute, keep_state, carried)


def attend_back(key_piece, key_pos, context, grad_pack):
    queries, query_pos, query_doc, doc_lengths = context
    grad_rows, log_total, delta = grad_pack
    seq_count, query_rows, width_here = queries.shape
    heads_here = log_total.shape[1]
    head_dim = width_here // heads_here
    key_rows = key_piece.shape[1]
    key_doc = doc_layout(doc_lengths, jnp.maximum(key_pos, 0))[0]
    allowed = key_mask(query_pos, query_doc, key_pos, key_doc)

    def compute(operand):
        scale_now = head_dim ** (-0.5)
        query_split = queries.reshape(seq_count, query_rows, heads_here, head_dim)
        grad_split = grad_rows.reshape(seq_count, query_rows, heads_here, head_dim)
        key_split = key_piece[:, :, :width_here].reshape(seq_count, key_rows, heads_here, head_dim)
        value_split = key_piece[:, :, width_here:].reshape(
            seq_count, key_rows, heads_here, head_dim
        )
        scores = (
            jnp.einsum(
                "sqhd,skhd->shqk", query_split, key_split, preferred_element_type=jnp.float32
            )
            * scale_now
        )
        probs = jnp.where(allowed, jnp.exp(scores - log_total[..., None]), 0.0)
        grad_probs = jnp.einsum(
            "sqhd,skhd->shqk", grad_split, value_split, preferred_element_type=jnp.float32
        )
        grad_scores = (probs * (grad_probs - delta[..., None])).astype(jnp.bfloat16)
        grad_query = (
            jnp.einsum(
                "shqk,skhd->sqhd", grad_scores, key_split, preferred_element_type=jnp.float32
            )
            * scale_now
        )
        grad_key = (
            jnp.einsum(
                "shqk,sqhd->skhd", grad_scores, query_split, preferred_element_type=jnp.float32
            )
            * scale_now
        )
        grad_value = jnp.einsum(
            "shqk,sqhd->skhd",
            probs.astype(jnp.bfloat16),
            grad_split,
            preferred_element_type=jnp.float32,
        )
        key_grads = jnp.concatenate(
            [
                grad_key.reshape(seq_count, key_rows, width_here),
                grad_value.reshape(seq_count, key_rows, width_here),
            ],
            axis=2,
        )
        return (grad_query.reshape(seq_count, query_rows, width_here), key_grads)

    def skipped(operand):
        return (
            jnp.zeros((seq_count, query_rows, width_here), jnp.float32),
            jnp.zeros((seq_count, key_rows, 2 * width_here), jnp.float32),
        )

    return lax.cond(jnp.any(allowed), compute, skipped, 0)


def shards(
    tokens,
    norm1_gain,
    router_attn,
    w_query,
    w_key_value,
    w_out,
    norm2_gain,
    router_ffn,
    w_gate_up,
    w_down,
    adapt_wide,
    adapt_heads,
    adapt_ffn,
    attention_routes,
    feedforward_routes,
    doc_lengths,
    adapter_index,
    cotangent,
):
    w_query, w_key_value, w_out, w_gate_up, w_down = (
        lax.all_gather(w_query, "ctx", axis=1, tiled=True),
        lax.all_gather(w_key_value, "ctx", axis=0, tiled=True),
        lax.all_gather(w_out, "ctx", axis=2, tiled=True),
        lax.all_gather(w_gate_up, "ctx", axis=1, tiled=True),
        lax.all_gather(w_down, "ctx", axis=2, tiled=True),
    )
    seq_count, block_len, part_width = tokens.shape
    width_here = w_query.shape[2]
    ff_here = w_down.shape[1]
    experts_a = w_query.shape[0]
    experts_f = w_down.shape[0]
    adapters = adapt_heads.shape[0]
    rank_dim = adapt_heads.shape[2]
    top_k = attention_routes.shape[2]
    heads_here = width_here // HEAD_DIM
    ctx_rank = lax.axis_index("ctx")
    tp_rank = lax.axis_index("tp")
    adapter_slot_gate = experts_a + 2
    adapter_slot_output = adapter_slot_gate + 2 * experts_f
    slot_down = adapter_slot_output + experts_a
    wide_all = lax.all_gather(adapt_wide.astype(jnp.bfloat16), ("ctx", "tp"), axis=3, tiled=True)
    heads_low = adapt_heads.astype(jnp.bfloat16)
    ffn_low = adapt_ffn.astype(jnp.bfloat16)
    wide_seq = wide_all[adapter_index]
    heads_seq = heads_low[adapter_index]
    model_width = wide_all.shape[3]
    whole_rows, grad_whole = (
        lax.all_gather(tokens, "tp", axis=2, tiled=True),
        lax.all_gather(cotangent, "tp", axis=2, tiled=True),
    )
    resid_in = whole_rows.astype(jnp.float32)
    positions = ctx_rank * block_len + jnp.arange(block_len, dtype=jnp.int32)
    doc_ids, offsets = doc_layout(doc_lengths, positions)
    first_normalized = rms_scale(resid_in, norm1_gain).astype(jnp.bfloat16)
    gate_attn = route_gates(
        jnp.einsum(
            "sbd,de->sbe", first_normalized, router_attn, preferred_element_type=jnp.float32
        ),
        attention_routes,
    )
    order_a, token_a, onehot_a, counts_a, sizes_a, unsort_a = arrange(
        attention_routes, adapter_index, experts_a, adapters
    )
    pairs_a = first_normalized.reshape(-1, model_width)[token_a]
    a_query = groups_flat(wide_all, 0, experts_a)
    b_query = groups_flat(heads_low, 0, experts_a)
    lowrank_query = ragged(pairs_a, jnp.swapaxes(a_query, 1, 2), counts_a)
    query_sorted = ragged(pairs_a, w_query, sizes_a) + ragged_exact(
        lowrank_query, b_query, counts_a
    )
    query_pre = query_sorted[unsort_a].reshape(seq_count, block_len, top_k, heads_here, HEAD_DIM)
    queries = (
        rotate(query_pre, offsets)
        .astype(jnp.bfloat16)
        .reshape(seq_count, block_len * top_k, width_here)
    )
    key_value_weight = w_key_value.reshape(model_width, 2 * width_here)
    kv_pre = jnp.einsum(
        "sbd,dc->sbc", first_normalized, key_value_weight, preferred_element_type=jnp.float32
    )
    lowrank_key_value = jnp.einsum(
        "sbd,scrd->sbcr",
        first_normalized,
        wide_seq[:, experts_a : experts_a + 2],
        preferred_element_type=jnp.float32,
    )
    kv_extra = jnp.einsum(
        "sbcr,scrh->sbch",
        lowrank_key_value,
        heads_seq[:, experts_a : experts_a + 2].astype(jnp.float32),
        precision=highest,
    )
    kv_pre = kv_pre + kv_extra.reshape(seq_count, block_len, 2 * width_here)
    keys_own = rotate(
        kv_pre[:, :, :width_here].reshape(seq_count, block_len, heads_here, HEAD_DIM), offsets
    )
    key_value_rows = jnp.concatenate(
        [keys_own.reshape(seq_count, block_len, width_here), kv_pre[:, :, width_here:]], axis=2
    ).astype(jnp.bfloat16)
    pair_pos = jnp.repeat(positions, top_k)
    pair_doc = jnp.repeat(doc_ids, top_k, axis=1)
    context = (queries, pair_pos, pair_doc, doc_lengths)
    query_rows = block_len * top_k
    start_state = (
        jnp.zeros((seq_count, heads_here, query_rows, HEAD_DIM), jnp.float32),
        jnp.full((seq_count, heads_here, query_rows), big_negative, jnp.float32),
        jnp.zeros((seq_count, heads_here, query_rows), jnp.float32),
    )
    key_piece = lax.all_gather(key_value_rows, "ctx", axis=1, tiled=True)
    carried = attend_add(
        start_state, key_piece, jnp.arange(key_piece.shape[1], dtype=jnp.int32), context
    )
    running, peak, weight_sum = carried
    log_total = peak + jnp.log(weight_sum)
    attended = running / weight_sum[..., None]
    attended_rows = jnp.transpose(attended, (0, 2, 1, 3)).reshape(seq_count, query_rows, width_here)
    out_low = attended_rows.astype(jnp.bfloat16)
    out_pairs = out_low.reshape(-1, width_here)[order_a]
    a_out = groups_flat(heads_low, experts_a + 2, experts_a)
    b_out = groups_flat(wide_all, adapter_slot_output, experts_a)
    low_out = ragged(out_pairs, jnp.swapaxes(a_out, 1, 2), counts_a)
    proj_out = ragged(out_pairs, w_out, sizes_a) + ragged_exact(low_out, b_out, counts_a)
    gate_pairs_a = gate_attn.reshape(-1)[order_a]
    attn_part = combine_pairs(proj_out * gate_pairs_a[:, None], unsort_a, seq_count, block_len)
    resid_mid = resid_in + lax.psum(attn_part.astype(jnp.bfloat16), "tp").astype(jnp.float32)
    second_normalized = rms_scale(resid_mid, norm2_gain).astype(jnp.bfloat16)
    gate_ffn = route_gates(
        jnp.einsum(
            "sbd,de->sbe", second_normalized, router_ffn, preferred_element_type=jnp.float32
        ),
        feedforward_routes,
    )
    order_f, token_f, onehot_f, counts_f, sizes_f, unsort_f = arrange(
        feedforward_routes, adapter_index, experts_f, adapters
    )
    pairs_f = second_normalized.reshape(-1, model_width)[token_f]
    a_gate_up = jnp.concatenate(
        [
            groups_flat(wide_all, adapter_slot_gate, experts_f),
            groups_flat(wide_all, adapter_slot_gate + experts_f, experts_f),
        ],
        axis=1,
    )
    b_gate = groups_flat(ffn_low, 0, experts_f)
    b_up = groups_flat(ffn_low, experts_f, experts_f)
    lowrank_gate_up = ragged(pairs_f, jnp.swapaxes(a_gate_up, 1, 2), counts_f)
    gate_up_matrix = w_gate_up.reshape(experts_f, model_width, 2 * ff_here)
    gate_up_pre = ragged(pairs_f, gate_up_matrix, sizes_f) + jnp.concatenate(
        [
            ragged_exact(lowrank_gate_up[:, :rank_dim], b_gate, counts_f),
            ragged_exact(lowrank_gate_up[:, rank_dim:], b_up, counts_f),
        ],
        axis=1,
    )
    gate_before_act = gate_up_pre[:, :ff_here]
    up_before_act = gate_up_pre[:, ff_here:]
    sigmoid_gate = jax.nn.sigmoid(gate_before_act)
    silu_gate = gate_before_act * sigmoid_gate
    hidden = (silu_gate * up_before_act).astype(jnp.bfloat16)
    a_down = groups_flat(ffn_low, 2 * experts_f, experts_f)
    b_down = groups_flat(wide_all, slot_down, experts_f)
    low_down = ragged(hidden, jnp.swapaxes(a_down, 1, 2), counts_f)
    proj_down = ragged(hidden, w_down, sizes_f) + ragged_exact(low_down, b_down, counts_f)
    gate_pairs_f = gate_ffn.reshape(-1)[order_f]
    ffn_part = combine_pairs(proj_down * gate_pairs_f[:, None], unsort_f, seq_count, block_len)
    mixed = (
        lax.psum_scatter(
            ffn_part.astype(jnp.bfloat16), "tp", scatter_dimension=2, tiled=True
        ).astype(jnp.float32)
        + own_slice(resid_mid, part_width, tp_rank)
    ).astype(jnp.bfloat16)
    grad_full = grad_whole.astype(jnp.float32)
    grad_rows_f = grad_full.reshape(-1, model_width)[token_f]
    grad_down = (gate_pairs_f[:, None] * grad_rows_f).astype(jnp.bfloat16)
    grad_gate_f = jnp.sum(proj_down * grad_rows_f, axis=1)
    dz_down = ragged(grad_down, jnp.swapaxes(b_down, 1, 2), counts_f)
    grad_hidden = ragged(grad_down, jnp.swapaxes(w_down, 1, 2), sizes_f) + ragged_exact(
        dz_down, a_down, counts_f
    )
    grad_gate = (
        grad_hidden * up_before_act * sigmoid_gate * (1.0 + gate_before_act * (1.0 - sigmoid_gate))
    ).astype(jnp.bfloat16)
    grad_up = (grad_hidden * silu_gate).astype(jnp.bfloat16)
    dz_gate_up = jnp.concatenate(
        [
            ragged(grad_gate, jnp.swapaxes(b_gate, 1, 2), counts_f),
            ragged(grad_up, jnp.swapaxes(b_up, 1, 2), counts_f),
        ],
        axis=1,
    )
    grad_gate_up = jnp.concatenate([grad_gate, grad_up], axis=1)
    grad_pairs_two = ragged(
        grad_gate_up, jnp.swapaxes(gate_up_matrix, 1, 2), sizes_f
    ) + ragged_exact(dz_gate_up, a_gate_up, counts_f)
    grad_logit_f = gates_back(
        gate_ffn,
        grad_gate_f[unsort_f].reshape(seq_count, block_len, top_k),
        feedforward_routes,
        experts_f,
    )
    grad_norm_two = combine_pairs(grad_pairs_two, unsort_f, seq_count, block_len) + jnp.einsum(
        "sbe,de->sbd", grad_logit_f, router_ffn.astype(jnp.float32), precision=highest
    )
    grad_mid = grad_full + lax.psum(
        norm_back(resid_mid, norm2_gain, grad_norm_two).astype(jnp.bfloat16), "tp"
    ).astype(jnp.float32)
    grad_a_gate_up = group_outer(onehot_f, dz_gate_up, pairs_f)
    grad_b_gate = group_outer(onehot_f, lowrank_gate_up[:, :rank_dim], grad_gate)
    grad_b_up = group_outer(onehot_f, lowrank_gate_up[:, rank_dim:], grad_up)
    grad_a_down = group_outer(onehot_f, dz_down, hidden)
    grad_b_down = group_outer(onehot_f, low_down, grad_down)
    grad_rows_a = grad_mid.reshape(-1, model_width)[token_a]
    grad_proj = (gate_pairs_a[:, None] * grad_rows_a).astype(jnp.bfloat16)
    grad_gate_a = jnp.sum(proj_out * grad_rows_a, axis=1)
    dz_out = ragged(grad_proj, jnp.swapaxes(b_out, 1, 2), counts_a)
    grad_out_sorted = ragged(grad_proj, jnp.swapaxes(w_out, 1, 2), sizes_a) + ragged_exact(
        dz_out, a_out, counts_a
    )
    grad_a_out = group_outer(onehot_a, dz_out, out_pairs)
    grad_b_out = group_outer(onehot_a, low_out, grad_proj)
    grad_attended = grad_out_sorted.astype(jnp.bfloat16)[unsort_a].reshape(
        seq_count, query_rows, width_here
    )
    delta = jnp.transpose(
        jnp.sum(
            (grad_attended.astype(jnp.float32) * attended_rows).reshape(
                seq_count, query_rows, heads_here, HEAD_DIM
            ),
            axis=-1,
        ),
        (0, 2, 1),
    )
    grad_pack = (grad_attended, log_total, delta)
    keys_all = lax.all_gather(key_value_rows, "ctx", axis=1, tiled=True)
    full_len = keys_all.shape[1]
    key_span = min(512, full_len)

    def back_block(grad_sum, block_number):
        first_pos = block_number * key_span
        key_piece = lax.dynamic_slice_in_dim(keys_all, first_pos, key_span, 1)
        query_part, kv_part = attend_back(
            key_piece, first_pos + jnp.arange(key_span, dtype=jnp.int32), context, grad_pack
        )
        return (grad_sum + query_part, kv_part)

    grad_query, kv_blocks = lax.scan(
        back_block,
        jnp.zeros((seq_count, query_rows, width_here), jnp.float32),
        jnp.arange(full_len // key_span, dtype=jnp.int32),
    )
    kv_whole = jnp.moveaxis(kv_blocks, 0, 1).reshape(seq_count, full_len, 2 * width_here)
    grad_kv = lax.psum_scatter(
        kv_whole.astype(jnp.bfloat16), "ctx", scatter_dimension=1, tiled=True
    ).astype(jnp.float32)
    grad_query_rot = rotate(
        grad_query.reshape(seq_count, block_len, top_k, heads_here, HEAD_DIM), -offsets
    )
    grad_query_pairs = grad_query_rot.astype(jnp.bfloat16).reshape(-1, width_here)[order_a]
    dz_query = ragged(grad_query_pairs, jnp.swapaxes(b_query, 1, 2), counts_a)
    grad_pairs_one = ragged(grad_query_pairs, jnp.swapaxes(w_query, 1, 2), sizes_a) + ragged_exact(
        dz_query, a_query, counts_a
    )
    grad_a_query = group_outer(onehot_a, dz_query, pairs_a)
    grad_b_query = group_outer(onehot_a, lowrank_query, grad_query_pairs)
    grad_key_rot = rotate(
        grad_kv[:, :, :width_here].reshape(seq_count, block_len, heads_here, HEAD_DIM), -offsets
    )
    grad_kv_pre = jnp.concatenate(
        [grad_key_rot.reshape(seq_count, block_len, width_here), grad_kv[:, :, width_here:]], axis=2
    ).astype(jnp.bfloat16)
    grad_kv_split = grad_kv_pre.reshape(seq_count, block_len, 2, width_here)
    dz_kv = jnp.einsum(
        "sbch,scrh->sbcr",
        grad_kv_split,
        heads_seq[:, experts_a : experts_a + 2],
        preferred_element_type=jnp.float32,
    )
    grad_norm_kv = jnp.einsum(
        "sbc,dc->sbd", grad_kv_pre, key_value_weight, preferred_element_type=jnp.float32
    ) + jnp.einsum(
        "sbcr,scrd->sbd",
        dz_kv,
        wide_seq[:, experts_a : experts_a + 2].astype(jnp.float32),
        precision=highest,
    )
    grad_a_kv = jnp.einsum(
        "sbcr,sbd->scrd", dz_kv, first_normalized.astype(jnp.float32), precision=highest
    )
    grad_b_kv = jnp.einsum(
        "sbcr,sbch->scrh", lowrank_key_value, grad_kv_split.astype(jnp.float32), precision=highest
    )
    grad_logit_a = gates_back(
        gate_attn,
        grad_gate_a[unsort_a].reshape(seq_count, block_len, top_k),
        attention_routes,
        experts_a,
    )
    grad_norm_one = (
        combine_pairs(grad_pairs_one, unsort_a, seq_count, block_len)
        + grad_norm_kv
        + jnp.einsum(
            "sbe,de->sbd", grad_logit_a, router_attn.astype(jnp.float32), precision=highest
        )
    )
    grad_tokens = (
        lax.psum_scatter(
            norm_back(resid_in, norm1_gain, grad_norm_one).astype(jnp.bfloat16),
            "tp",
            scatter_dimension=2,
            tiled=True,
        ).astype(jnp.float32)
        + own_slice(grad_mid, part_width, tp_rank)
    ).astype(jnp.bfloat16)
    kv_a_total = (
        jnp.zeros((adapters, 2, rank_dim, model_width), jnp.float32)
        .at[adapter_index]
        .add(grad_a_kv)
    )
    kv_b_total = (
        jnp.zeros((adapters, 2, rank_dim, width_here), jnp.float32).at[adapter_index].add(grad_b_kv)
    )
    wide_terms = jnp.concatenate(
        [
            ungroup(grad_a_query, experts_a, adapters),
            kv_a_total,
            ungroup(grad_a_gate_up[:, :rank_dim], experts_f, adapters),
            ungroup(grad_a_gate_up[:, rank_dim:], experts_f, adapters),
            ungroup(grad_b_out, experts_a, adapters),
            ungroup(grad_b_down, experts_f, adapters),
        ],
        axis=1,
    )
    head_terms = jnp.concatenate(
        [
            ungroup(grad_b_query, experts_a, adapters),
            kv_b_total,
            ungroup(grad_a_out, experts_a, adapters),
        ],
        axis=1,
    )
    ffn_terms = jnp.concatenate(
        [
            ungroup(grad_b_gate, experts_f, adapters),
            ungroup(grad_b_up, experts_f, adapters),
            ungroup(grad_a_down, experts_f, adapters),
        ],
        axis=1,
    )
    grad_wide = lax.psum_scatter(wide_terms, ("ctx", "tp"), scatter_dimension=3, tiled=True)
    grad_heads, grad_ffn = (
        lax.psum(head_terms.astype(jnp.bfloat16), "ctx").astype(jnp.float32),
        lax.psum(ffn_terms.astype(jnp.bfloat16), "ctx").astype(jnp.float32),
    )
    return (mixed, grad_tokens, grad_wide, grad_heads, grad_ffn)


def solution(mesh):
    placed = (
        P(None, "ctx", "tp"),
        P(),
        P(),
        P(None, "ctx", "tp"),
        P("ctx", None, "tp"),
        P(None, "tp", "ctx"),
        P(),
        P(),
        P(None, "ctx", None, "tp"),
        P(None, "tp", "ctx"),
        P(None, None, None, ("ctx", "tp")),
        P(None, None, None, "tp"),
        P(None, None, None, "tp"),
        P(None, "ctx", None),
        P(None, "ctx", None),
        P(),
        P(),
        P(None, "ctx", "tp"),
    )
    return jax.shard_map(
        shards,
        mesh=mesh,
        in_specs=placed,
        out_specs=(
            P(None, "ctx", "tp"),
            P(None, "ctx", "tp"),
            P(None, None, None, ("ctx", "tp")),
            P(None, None, None, "tp"),
            P(None, None, None, "tp"),
        ),
        check_vma=False,
    )
```

profile of v0, /device:TPU:1, one launch (start us, length us, event | category | flops | bytes accessed | tf_op | source)
XLA Modules:
  0.0 2553.9 jit_solution(3683813799447970405)
XLA Ops:
  17.7 40.1 %all-gather.10.cloned.1.call-done = bf16[2,128,2048]{2,1,0:T(8,128)(2,1)} async-done(((bf16[2,128,256]{2,1,0:T(8,128)(2,1)}), bf16[2,128,2048]{2,1,0:T(8,128)(2,1)}) %all-gather.10.cloned.1.call-update) | async-done | bytes 1048592 | tf_op jit(solution)/shard_map/all_gather | solution.py:283
  61.4 31.9 %all-gather.16.cloned.1.call-done = bf16[2048,2,256]{2,1,0:T(2,128)(2,1)} async-done(((bf16[128,2,256]{2,1,0:T(2,128)(2,1)}), bf16[2048,2,256]{2,1,0:T(2,128)(2,1)}) %all-gather.16.cloned.1.call-update) | async-done | bytes 2097168 | tf_op jit(solution)/shard_map/all_gather | solution.py:257
  96.4 325.7 %all-gather.14.cloned.1.call-done = bf16[2,22,16,2048]{1,2,0,3:T(8,128)(2,1)} async-done(((bf16[2,22,16,16]{1,2,0,3:T(8,128)(2,1)}), bf16[2,22,16,2048]{1,2,0,3:T(8,128)(2,1)}) %all-gather.14.cloned.1.call-update) | async-done | bytes 2883600 | tf_op jit(solution)/shard_map/all_gather | solution.py:276
  422.2 18.6 copy.367
  494.1 57.7 %slice_bitcast_fusion.1 = (bf16[4,2,16,2048]{0,2,1,3:T(8,128)(2,1)}, bf16[4,2,16,2048]{0,2,1,3:T(8,128)(2,1)}, bf16[4,2,16,2048]{0,2,1,3:T(8,128)(2,1)}, bf16[4,...) fusion(bf16[2,22,16,2048]{1,2,0,3:T(8,128)(2,1)} %all-gather.14.cloned.1.call-done), kind=kLoop, calls=%fused_computation.62 | loop fusion | bytes 5242880 | tf_op jit(solution)/shard_map/transpose | solution.py:100
  551.8 28.2 %copy.441 = bf16[4,2,16,2048]{2,3,1,0:T(8,128)(2,1)} copy(bf16[4,2,16,2048]{0,2,1,3:T(8,128)(2,1)} %get-tuple-element.511) | data formatting | bytes 1048576 | tf_op jit(solution)/shard_map/transpose | solution.py:302
  580.1 28.2 %copy.376 = bf16[4,2,16,2048]{2,3,1,0:T(8,128)(2,1)} copy(bf16[4,2,16,2048]{0,2,1,3:T(8,128)(2,1)} %get-tuple-element.510) | data formatting | bytes 1048576 | tf_op jit(solution)/shard_map/transpose | solution.py:100
  666.2 19.9 conditional.2
  697.7 20.4 ragged-dot-none.20
  792.3 17.3 copy.382
  809.6 17.3 copy.383
  831.6 28.3 %copy.393 = bf16[4,2,16,2048]{2,3,1,0:T(8,128)(2,1)} copy(bf16[4,2,16,2048]{0,2,1,3:T(8,128)(2,1)} %get-tuple-element.507) | data formatting | bytes 1048576 | tf_op jit(solution)/shard_map/transpose | solution.py:100
  933.8 115.2 %all-gather.22.cloned.1.call-done = bf16[4,2048,2,704]{1,3,2,0:T(8,128)(2,1)} async-done(((bf16[4,128,2,704]{1,3,2,0:T(8,128)(2,1)}), bf16[4,2048,2,704]{1,3,2,0:T(8,128)(2,1)}) %all-gather.22.cloned.1.call-update) | async-done | bytes 23068688 | tf_op jit(solution)/shard_map/all_gather | solution.py:259
  1049.1 28.9 %copy.381 = bf16[4,2048,1408]{2,1,0:T(8,128)(2,1)} copy(bf16[4,2048,1408]{1,2,0:T(8,128)(2,1)} %bitcast.322) | data formatting | bytes 46137344 | tf_op jit(solution)/shard_map/reshape | solution.py:382
  1121.8 20.5 ragged-dot-none.13
  1224.3 20.8 ragged-dot-none.6
  1304.1 76.4 %all-reduce.7.cloned.1.call-done = bf16[2,128,2048]{2,1,0:T(8,128)(2,1)} async-done(((bf16[2,128,2048]{2,1,0:T(8,128)(2,1)}), bf16[2,128,2048]{2,1,0:T(8,128)(2,1)}) %all-reduce.7.cloned.1.call-update) | async-done | bytes 1048592 | tf_op jit(solution)/shard_map/psum | solution.py:439
  1423.9 44.8 %while.15 = (s32[]{:T(128)}, f32[2,256,256]{1,2,0:T(8,128)}, bf16[4,2,512,512]{2,3,1,0:T(8,128)(2,1)}, s32[4]{0:T(128)S(1)}, s32[2,8]{0,1:T(8,128)S(1)}, /*index...) while((s32[]{:T(128)}, f32[2,256,256]{1,2,0:T(8,128)}, ...), condition=%wide.region_39.41_spmd.clone, body=%wide.region_34.40_spmd.clone.sunk | while | flops 679244288 | bytes 37017220 | solution.py:481
  1477.4 18.0 copy.361
  1550.1 20.4 ragged-dot-none
  1640.6 27.0 %copy.412 = f32[2,22,16,2048]{1,2,0,3:T(8,128)} copy(f32[2,22,16,2048]{3,2,0,1:T(8,128)} %fusion.23) | data formatting | bytes 11534336 | tf_op jit(solution)/shard_map/concatenate | solution.py:557
  1669.4 97.4 %all-reduce.9.cloned.1.call-done = (bf16[2,10,16,256]{3,2,0,1:T(8,128)(2,1)}, bf16[2,12,16,704]{3,2,0,1:T(8,128)(2,1)}) async-done(((bf16[2,10,16,256]{3,2,0,1:T(8,128)(2,1)}, bf16[2,12,16,704]{3,2,0,1:T(8,128)(2,1)}), (bf16[2,10,16,256]{3,2,0,1:T(8,128)(2,1)}, bf16[2,12,16,704]{3,2,0,1:T(8,128)(2,1)})) %all-reduce.9.cloned.1.call-update) | async-done | bytes 704528 | tf_op jit(solution)/shard_map/psum | solution.py:586
  1770.7 70.1 %reduce-scatter.9.cloned.1.call-done = bf16[2,128,256]{2,1,0:T(8,128)(2,1)} async-done(((bf16[2,128,2048]{2,1,0:T(8,128)(2,1)}), bf16[2,128,256]{2,1,0:T(8,128)(2,1)}) %reduce-scatter.9.cloned.1.call-update) | async-done | bytes 131088 | tf_op jit(solution)/shard_map/reduce_scatter | solution.py:541
  1842.3 702.8 %reduce-scatter.11.cloned.1.call-done = f32[2,22,16,16]{1,2,0,3:T(8,128)} async-done(((f32[2,22,16,2048]{1,2,0,3:T(8,128)}), f32[2,22,16,16]{1,2,0,3:T(8,128)}) %reduce-scatter.11.cloned.1.call-update) | async-done | bytes 45072 | tf_op jit(solution)/shard_map/reduce_scatter | solution.py:584
  (607 shorter events, 734.7 us)
Async XLA Ops:
  7.2 870.7 %copy-start = (bf16[2048,4]{0,1:T(4,128)(2,1)S(1)}, bf16[2048,4]{0,1:T(4,128)(2,1)}, u32[]{:S(2)}) copy-start(bf16[2048,4]{0,1:T(4,128)(2,1)} %param.33) | copy-start | bytes 49156
  7.2 50.6 %all-gather.10.cloned.1.call-start = ((), (), s32[]{:S(2)}) async-start(), calls=%async_computation.4 | async-start | bytes 1179648 | tf_op jit(solution)/shard_map/all_gather | solution.py:283
  7.9 85.3 %all-gather.16.cloned.1.call-start = ((), (), s32[]{:S(2)}) async-start(), calls=%async_computation.7 | async-start | bytes 2228224 | tf_op jit(solution)/shard_map/all_gather | solution.py:257
  8.7 413.5 %all-gather.14.cloned.1.call-start = ((), (), s32[]{:S(2)}) async-start(), calls=%async_computation.6 | async-start | bytes 16908288 | tf_op jit(solution)/shard_map/all_gather | solution.py:276
  10.5 628.5 %all-gather.12.cloned.1.call-start = ((), (), s32[]{:S(2)}) async-start(), calls=%async_computation.5 | async-start | bytes 4456448 | tf_op jit(solution)/shard_map/all_gather | solution.py:256
  12.3 644.6 %all-gather.20.cloned.1.call-start = ((), (), s32[]{:S(2)}) async-start(), calls=%async_computation.9 | async-start | bytes 4456448 | tf_op jit(solution)/shard_map/all_gather | solution.py:258
  14.2 652.0 %all-gather.18.cloned.1.call-start = ((), (), s32[]{:S(2)}) async-start(), calls=%async_computation.8 | async-start | bytes 4456448 | tf_op jit(solution)/shard_map/all_gather | solution.py:344
  15.8 460.1 %copy-start.69 = (s32[128]{0:T(128)}, s32[128]{0:T(128)S(1)}, u32[]{:S(2)}) copy-start(s32[128]{0:T(128)S(1)} %get-tuple-element.688) | copy-start | bytes 1540
  15.9 459.5 %copy-start.60 = (s32[2,128]{1,0:T(2,128)}, s32[2,128]{1,0:T(2,128)S(1)}, u32[]{:S(2)}) copy-start(s32[2,128]{1,0:T(2,128)S(1)} %get-tuple-element.687) | copy-start | bytes 3076
  61.4 429.4 %copy-start.2 = (bf16[2,128,2048]{2,1,0:T(8,128)(2,1)}, bf16[2,128,2048]{2,1,0:T(8,128)(2,1)S(1)}, u32[]{:S(2)}) copy-start(bf16[2,128,2048]{2,1,0:T(8,128)(2,1)S(1)} %fusion.28) | copy-start | bytes 3145732
  96.4 356.0 %copy-start.14 = (bf16[2048,512,1]{1,0,2:T(8,128)(2,1)}, bf16[2048,512,1]{1,0,2:T(8,128)(2,1)S(1)}, u32[]{:S(2)}) copy-start(bf16[2048,512,1]{1,0,2:T(8,128)(2,1)S(1)} %reshape.973) | copy-start | bytes 6291460
  457.1 330.2 %all-gather.26.cloned.1.call-start = ((), (), s32[]{:S(2)}) async-start(), calls=%async_computation.14 | async-start | bytes 1179648 | tf_op jit(solution)/shard_map/all_gather | solution.py:284
  457.8 414.5 %all-reduce.5.cloned.1.call-start = ((), (), s32[]{:S(2)}) async-start(), calls=%async_computation.10 | async-start | bytes 2097152 | tf_op jit(solution)/shard_map/psum | solution.py:360
  463.0 224.4 %copy-start.64 = (s32[1024]{0:T(1024)}, s32[1024]{0:T(1024)S(1)}, u32[]{:S(2)}) copy-start(s32[1024]{0:T(1024)S(1)} %pad_clamp_fusion.5) | copy-start | bytes 12292
  475.5 258.8 %copy-start.62 = (s32[1024]{0:T(1024)}, s32[1024]{0:T(1024)S(1)}, u32[]{:S(2)}) copy-start(s32[1024]{0:T(1024)S(1)} %pad_clamp_fusion.3) | copy-start | bytes 12292
  490.8 236.1 %copy-start.77 = (f32[512]{0:T(512)}, f32[512]{0:T(512)S(1)}, u32[]{:S(2)}) copy-start(f32[512]{0:T(512)S(1)} %gather_fusion.6) | copy-start | bytes 6148
  756.3 162.0 %all-gather.24.cloned.1.call-start = ((), (), s32[]{:S(2)}) async-start(), calls=%async_computation.12 | async-start | bytes 13369344 | tf_op jit(solution)/shard_map/all_gather | solution.py:260
  757.5 291.5 %all-gather.22.cloned.1.call-start = ((), (), s32[]{:S(2)}) async-start(), calls=%async_computation.11 | async-start | bytes 24510464 | tf_op jit(solution)/shard_map/all_gather | solution.py:259
  758.1 622.4 %all-reduce.7.cloned.1.call-start = ((), (), s32[]{:S(2)}) async-start(), calls=%async_computation.15 | async-start | bytes 2097152 | tf_op jit(solution)/shard_map/psum | solution.py:439
  1295.9 314.9 %reduce-scatter.7.cloned.1.call-start = ((), (), s32[]{:S(2)}) async-start(), calls=%async_computation.16 | async-start | bytes 4456448 | tf_op jit(solution)/shard_map/reduce_scatter | solution.py:487
  1476.0 191.7 %reduce-scatter.5.cloned.1.call-start = ((), (), s32[]{:S(2)}) async-start(), calls=%async_computation.13 | async-start | bytes 1179648 | tf_op jit(solution)/shard_map/reduce_scatter | solution.py:402
  1529.8 237.0 %all-reduce.9.cloned.1.call-start = ((), (), s32[]{:S(2)}) async-start(), calls=%async_computation.19 | async-start | bytes 1507328 | tf_op jit(solution)/shard_map/psum | solution.py:586
  1618.1 222.6 %reduce-scatter.9.cloned.1.call-start = ((), (), s32[]{:S(2)}) async-start(), calls=%async_computation.17 | async-start | bytes 1179648 | tf_op jit(solution)/shard_map/reduce_scatter | solution.py:541
  1625.2 919.9 %reduce-scatter.11.cloned.1.call-start = ((), (), s32[]{:S(2)}) async-start(), calls=%async_computation.18 | async-start | bytes 33816576 | tf_op jit(solution)/shard_map/reduce_scatter | solution.py:584
  (89 other events, 647.0 us)
Sparse Core Ops, SparseCore 0:
  10.2 47.5 all-gather.9
  59.5 33.7 all-gather.15
  95.5 326.5 all-gather.13
  424.2 46.8 all-gather.11
  472.6 37.7 all-gather.19
  511.9 37.3 all-gather.17
  551.5 43.9 all-gather.25
  756.4 83.5 all-reduce.4
  841.6 75.3 all-gather.23
  918.5 130.4 all-gather.21
  1296.0 84.4 all-reduce.6
  1476.1 92.3 reduce-scatter.6
  1572.7 70.8 reduce-scatter.4
  1646.8 119.9 all-reduce.8
  1770.2 70.4 reduce-scatter.8
  1843.1 701.9 reduce-scatter.10
where the time goes:
time: 2580 us; the launch traced here: 2550 us
  waiting for transfers between devices  1460 us (57%)
  local copies, waits for them, and re-layouts  524 us (20%)
  Pallas kernels  313 us (12%)
  other arithmetic  183 us (7%)
  matrix products  47 us (2%)
    reduce_scatter x1, waiting for transfers between devices, shards(): lax.psum_scatter(wide_terms, ('ctx', 'tp'), scatter_dimension=3, tiled=True)  703 us
    all_gather x1, waiting for transfers between devices, shards(): lax.all_gather(adapt_wide.astype(jnp.bfloat16), ('ctx', 'tp'), axis=3, ti...  326 us
    another operation x26, Pallas kernels  307 us
    transpose x13, local copies, waits for them, and re-layouts, groups_flat(): jnp.swapaxes(chosen, 0, 1)  169 us
    all_gather x1, waiting for transfers between devices, shards(): lax.all_gather(w_gate_up, 'ctx', axis=1, tiled=True)  115 us
    psum x1, waiting for transfers between devices, shards(): lax.psum(head_terms.astype(jnp.bfloat16), 'ctx').astype(jnp.float32)  97.4 us
    psum x1, waiting for transfers between devices, shards(): lax.psum(norm_back(resid_mid, norm2_gain, grad_norm_two).astype(jnp.bfloa...  76.4 us
    reduce_scatter x1, waiting for transfers between devices, shards(): lax.psum_scatter(norm_back(resid_in, norm1_gain, grad_norm_one).astype(jn...  70.1 us
  transfers between devices with their start and end apart: 16, of which 8 were waited for; matrix products, arithmetic and copies ran while one was open for 23% of the time, Pallas kernels for 5%

commit v1 on v0

v1 whole, which is shorter than its diff:
```python
import functools

import jax
import jax.numpy as jnp
from jax import lax
from jax.experimental import pallas as pl
from jax.experimental.pallas import tpu as pltpu
from jax.sharding import PartitionSpec as P

HEAD_DIM = 128
WINDOW = 1024
eps = 1e-06
big_negative = -1e30
bf16 = jnp.bfloat16
f32 = jnp.float32

MESH = pl.DeviceIdType.MESH
ANY = pl.BlockSpec(memory_space=pl.ANY)
VMEM = pl.BlockSpec(memory_space=pltpu.VMEM)
N_CTX, N_TP = 16, 8
PAST = 8


def region(kind, ref, owner, low, high):
    if kind == "rows":
        return ref.at[pl.ds(low, high - low), pl.ds(pl.multiple_of(owner * 128, 128), 128), :]
    if kind == "flat":
        return ref.at[pl.ds(pl.multiple_of(owner * 128 + 32 * low, 32), 32 * (high - low)), :]
    return ref.at[pl.ds(low, high - low), :, pl.ds(pl.multiple_of(owner * 128, 128), 128)]


def own_part(kind, ref, low, high):
    if kind == "flat":
        return ref.at[pl.ds(32 * low, 32 * (high - low)), :]
    return ref.at[pl.ds(low, high - low)]


def tp_part(kind, ref, rank, size):
    if kind == "cols":
        return ref.at[:, pl.ds(pl.multiple_of(rank * size, size), size)]
    return ref.at[pl.ds(pl.multiple_of(rank * size, size), size), :]


def gather_kernel(kinds, tp_kinds, *refs):
    n, m = len(kinds), len(tp_kinds)
    src, refs = list(refs[:n]), refs[n:]
    tp_src, refs = refs[:m], refs[m:]
    dst, refs = refs[:n], refs[n:]
    tp_dst, refs = refs[:m], refs[m:]
    send, recv, local, tp_send, tp_recv, tp_local = refs
    src = [tp_dst[m - 1] if r is None else r for r in src]
    me, tp = lax.axis_index("ctx"), lax.axis_index("tp")
    core, side = me ^ 1, me ^ 2
    up, down, far = lax.rem(me + 4, 16), lax.rem(me + 12, 16), lax.rem(me + 8, 16)
    barrier = pltpu.get_barrier_semaphore()
    for d in (core, side, up, down):
        pl.semaphore_signal(barrier, inc=1, device_id=(d, tp), device_id_type=MESH)
    for d in range(1, N_TP):
        pl.semaphore_signal(barrier, inc=1, device_id=(me, tp ^ d), device_id_type=MESH)
    pl.semaphore_wait(barrier, 4 + N_TP - 1)
    started, staying = [], []
    counter = [0] * n

    def tp_copy(i, d, rank):
        size = tp_src[i].shape[1 if tp_kinds[i] == "cols" else 0]
        return pltpu.make_async_remote_copy(
            src_ref=tp_src[i],
            dst_ref=tp_part(tp_kinds[i], tp_dst[i], rank, size),
            send_sem=tp_send.at[i, d],
            recv_sem=tp_recv.at[i, d],
            device_id=(me, tp ^ d),
            device_id_type=MESH,
        )

    for i in range(m):
        for d in range(1, N_TP):
            c = tp_copy(i, d, tp)
            c.start()
            started.append(c)
        size = tp_src[i].shape[1 if tp_kinds[i] == "cols" else 0]
        c = pltpu.make_async_copy(
            tp_src[i], tp_part(tp_kinds[i], tp_dst[i], tp, size), tp_local.at[i]
        )
        c.start()
        staying.append(c)

    def copy(t, item, owner, low, high, to, slot, own):
        there = region(kinds[t], dst[t], owner, low, high)
        return pltpu.make_async_remote_copy(
            src_ref=own_part(kinds[t], src[t], low, high) if own else there,
            dst_ref=there,
            send_sem=send.at[t, slot],
            recv_sem=recv.at[t, item],
            device_id=(to, tp),
            device_id_type=MESH,
        )

    def go(t, item, owner, low, high, to, own=False):
        c = copy(t, item, owner, low, high, to, counter[t], own)
        counter[t] += 1
        c.start()
        started.append(c)

    arrive = {
        0: (side, 0, 4),
        1: (down, 0, 4),
        2: (up, 0, 4),
        3: (down ^ 2, 0, 2),
        4: (up ^ 2, 0, 2),
        5: (far, 1, 3),
        6: (far, 0, 1),
        7: (far, 3, 4),
        8: (far ^ 2, 1, 2),
        9: (far ^ 2, 0, 1),
        10: (down ^ 2, 2, 4),
        11: (up ^ 2, 2, 4),
        12: (far ^ 2, 2, 4),
    }

    def got(t, item):
        owner, low, high = arrive[item]
        copy(t, item, owner, low, high, core, 0, False).wait_recv()
        go(t, 13 + item, owner, low, high, core)

    def first(t):
        go(t, 0, me, 0, 4, side, True)
        go(t, 2, me, 0, 4, down, True)
        go(t, 1, me, 0, 4, up, True)
        go(t, 26, me, 0, 4, core, True)
        c = pltpu.make_async_copy(src[t], region(kinds[t], dst[t], me, 0, 4), local.at[t])
        c.start()
        staying.append(c)

    for t in range(n - 1):
        first(t)
    for i in range(m):
        for d in range(1, N_TP):
            tp_copy(i, d, tp ^ d).wait_recv()
    staying[m - 1].wait()
    first(n - 1)
    for t in range(n):
        got(t, 0)
        go(t, 3, side, 0, 2, up)
        go(t, 4, side, 0, 2, down)
        got(t, 1)
        go(t, 5, down, 1, 3, up)
        go(t, 10, down, 2, 4, side)
        got(t, 2)
        go(t, 6, up, 0, 1, down)
        go(t, 7, up, 3, 4, down)
        go(t, 11, up, 2, 4, side)
    for t in range(n):
        got(t, 3)
        go(t, 8, down ^ 2, 1, 2, up)
        got(t, 4)
        go(t, 9, up ^ 2, 0, 1, down)
        got(t, 5)
        got(t, 6)
        got(t, 7)
        go(t, 12, far, 2, 4, side)
    for t in range(n):
        for item in range(8, 13):
            got(t, item)
    for t in range(n):
        for item in range(13):
            owner, low, high = arrive[item]
            copy(t, 13 + item, owner ^ 1, low, high, core, 0, False).wait_recv()
        copy(t, 26, core, 0, 4, core, 0, False).wait_recv()
    for c in started:
        c.wait_send()
    for i, c in enumerate(staying):
        if i != m - 1:
            c.wait()


def gather_all(shards, kinds, tp_shards, tp_kinds):
    n, m = len(kinds), len(tp_kinds)
    shapes, tp_shapes = [], []
    for s, k in zip(tp_shards, tp_kinds):
        shape = list(s.shape)
        shape[1 if k == "cols" else 0] *= N_TP
        tp_shapes.append(jax.ShapeDtypeStruct(tuple(shape), s.dtype))
    for s, k in zip(list(shards) + [tp_shapes[-1]], kinds):
        shape = list(s.shape)
        shape[{"rows": 1, "flat": 0, "cols": 2}[k]] *= N_CTX
        shapes.append(jax.ShapeDtypeStruct(tuple(shape), s.dtype))

    def body(*refs):
        gather_kernel(kinds, tp_kinds, *refs[: n - 1], None, *refs[n - 1 :])

    out = pl.pallas_call(
        body,
        out_shape=tuple(shapes + tp_shapes),
        in_specs=[ANY] * (n - 1 + m),
        out_specs=tuple([ANY] * (n + m)),
        scratch_shapes=[
            pltpu.SemaphoreType.DMA((n, 32)),
            pltpu.SemaphoreType.DMA((n, 27)),
            pltpu.SemaphoreType.DMA((n,)),
            pltpu.SemaphoreType.DMA((m, N_TP)),
            pltpu.SemaphoreType.DMA((m, N_TP)),
            pltpu.SemaphoreType.DMA((m,)),
        ],
        compiler_params=pltpu.CompilerParams(collective_id=0, has_side_effects=True),
        name="gather_all",
    )(*shards, *tp_shards)
    return out[:n], out[n : n + m - 1]


def exchange_kernel(kinds, *refs):
    n = len(kinds)
    src, refs = refs[:n], refs[n:]
    dst, refs = refs[:n], refs[n:]
    held, refs = refs[:n], refs[n:]
    send, recv = refs
    me, tp = lax.axis_index("ctx"), lax.axis_index("tp")
    barrier = pltpu.get_barrier_semaphore()
    for d in range(1, N_TP):
        pl.semaphore_signal(barrier, inc=1, device_id=(me, tp ^ d), device_id_type=MESH)
    pl.semaphore_wait(barrier, N_TP - 1)

    def part(i, ref, rank):
        if kinds[i].endswith("rows"):
            size = src[i].shape[0] // N_TP
            return ref.at[pl.ds(pl.multiple_of(rank * size, size), size), :]
        size = src[i].shape[1] // N_TP
        return ref.at[:, pl.ds(pl.multiple_of(rank * size, size), size)]

    def scatter(i, d):
        return pltpu.make_async_remote_copy(
            src_ref=part(i, src[i], tp ^ d),
            dst_ref=held[i].at[d],
            send_sem=send.at[i, d],
            recv_sem=recv.at[i, d],
            device_id=(me, tp ^ d),
            device_id_type=MESH,
        )

    def spread(i, d, rank):
        return pltpu.make_async_remote_copy(
            src_ref=part(i, dst[i], rank),
            dst_ref=part(i, dst[i], rank),
            send_sem=send.at[i, N_TP + d],
            recv_sem=recv.at[i, N_TP + d],
            device_id=(me, tp ^ d),
            device_id_type=MESH,
        )

    for i in range(n):
        for d in range(1, N_TP):
            scatter(i, d).start()
    for i in range(n):
        for d in range(1, N_TP):
            scatter(i, d).wait_recv()
        total = part(i, src[i], tp)[...].astype(f32)
        for d in range(1, N_TP):
            total = total + held[i][d].astype(f32)
        if kinds[i].startswith("ar"):
            part(i, dst[i], tp)[...] = total.astype(dst[i].dtype)
            for d in range(1, N_TP):
                spread(i, d, tp).start()
        else:
            dst[i][...] = total
    for i in range(n):
        for d in range(1, N_TP):
            scatter(i, d).wait_send()
            if kinds[i].startswith("ar"):
                spread(i, d, tp ^ d).wait_recv()
                spread(i, d, tp).wait_send()


def exchange(arrays, kinds, cid):
    outs, held = [], []
    for a, k in zip(arrays, kinds):
        if k == "rs_cols":
            outs.append(jax.ShapeDtypeStruct((a.shape[0], a.shape[1] // N_TP), f32))
        else:
            outs.append(jax.ShapeDtypeStruct(a.shape, a.dtype))
        r, c = a.shape
        held.append(
            pltpu.VMEM((N_TP, r // N_TP, c) if k == "ar_rows" else (N_TP, r, c // N_TP), a.dtype)
        )
    n = len(kinds)
    return pl.pallas_call(
        functools.partial(exchange_kernel, kinds),
        out_shape=tuple(outs),
        in_specs=[VMEM] * n,
        out_specs=tuple([VMEM] * n),
        scratch_shapes=held
        + [pltpu.SemaphoreType.DMA((n, 2 * N_TP)), pltpu.SemaphoreType.DMA((n, 2 * N_TP))],
        compiler_params=pltpu.CompilerParams(
            collective_id=cid, has_side_effects=True, vmem_limit_bytes=48 << 20
        ),
        name=f"exchange_{cid}",
    )(*arrays)


def halo_kernel(src, dst, send, recv, local):
    me, tp = lax.axis_index("ctx"), lax.axis_index("tp")
    block = src.shape[1]
    barrier = pltpu.get_barrier_semaphore()
    for d in range(1, N_CTX):
        pl.semaphore_signal(
            barrier, inc=1, device_id=(lax.rem(me + d, N_CTX), tp), device_id_type=MESH
        )
    pl.semaphore_wait(barrier, N_CTX - 1)

    def copy(d):
        return pltpu.make_async_remote_copy(
            src_ref=src,
            dst_ref=dst.at[:, pl.ds((PAST - d) * block, block), :],
            send_sem=send.at[d],
            recv_sem=recv.at[d],
            device_id=(lax.rem(me + d, N_CTX), tp),
            device_id_type=MESH,
        )

    own = pltpu.make_async_copy(src, dst.at[:, pl.ds(PAST * block, block), :], local)
    own.start()
    for d in range(1, PAST + 1):
        copy(d).start()
    own.wait()
    for d in range(1, PAST + 1):
        copy(d).wait()


def halo(kv_own):
    seqs, block, cols = kv_own.shape
    return pl.pallas_call(
        halo_kernel,
        out_shape=jax.ShapeDtypeStruct((seqs, (PAST + 1) * block, cols), kv_own.dtype),
        in_specs=[ANY],
        out_specs=ANY,
        scratch_shapes=[
            pltpu.SemaphoreType.DMA((PAST + 1,)),
            pltpu.SemaphoreType.DMA((PAST + 1,)),
            pltpu.SemaphoreType.DMA,
        ],
        compiler_params=pltpu.CompilerParams(collective_id=8, has_side_effects=True),
        name="halo",
    )(kv_own)


def halo_back_kernel(src, dst, held, send, recv):
    me, tp = lax.axis_index("ctx"), lax.axis_index("tp")
    block = dst.shape[1]
    barrier = pltpu.get_barrier_semaphore()
    for d in range(1, N_CTX):
        pl.semaphore_signal(
            barrier, inc=1, device_id=(lax.rem(me + d, N_CTX), tp), device_id_type=MESH
        )
    pl.semaphore_wait(barrier, N_CTX - 1)

    def copy(d):
        return pltpu.make_async_remote_copy(
            src_ref=src.at[:, pl.ds((PAST - d) * block, block), :],
            dst_ref=held.at[d],
            send_sem=send.at[d],
            recv_sem=recv.at[d],
            device_id=(lax.rem(me + N_CTX - d, N_CTX), tp),
            device_id_type=MESH,
        )

    for d in range(1, PAST + 1):
        copy(d).start()
    total = src[:, pl.ds(PAST * block, block), :].astype(f32)
    for d in range(1, PAST + 1):
        copy(d).wait_recv()
        total = total + held[d].astype(f32)
    dst[...] = total
    for d in range(1, PAST + 1):
        copy(d).wait_send()


def halo_back(partial):
    seqs, length, cols = partial.shape
    block = length // (PAST + 1)
    return pl.pallas_call(
        halo_back_kernel,
        out_shape=jax.ShapeDtypeStruct((seqs, block, cols), f32),
        in_specs=[VMEM],
        out_specs=VMEM,
        scratch_shapes=[
            pltpu.VMEM((PAST + 1, seqs, block, cols), partial.dtype),
            pltpu.SemaphoreType.DMA((PAST + 1,)),
            pltpu.SemaphoreType.DMA((PAST + 1,)),
        ],
        compiler_params=pltpu.CompilerParams(
            collective_id=9, has_side_effects=True, vmem_limit_bytes=48 << 20
        ),
        name="halo_back",
    )(partial)


def reduce_kernel(spread_too, *refs):
    n = len(spread_too)
    src, refs = refs[:n], refs[n:]
    dst, refs = refs[:n], refs[n:]
    held, refs = refs[:n], refs[n:]
    send, recv = refs
    me, tp = lax.axis_index("ctx"), lax.axis_index("tp")
    barrier = pltpu.get_barrier_semaphore()
    for d in range(1, N_CTX):
        pl.semaphore_signal(barrier, inc=1, device_id=(me ^ d, tp), device_id_type=MESH)
    pl.semaphore_wait(barrier, N_CTX - 1)

    def scatter(i, d):
        return pltpu.make_async_remote_copy(
            src_ref=src[i].at[me ^ d],
            dst_ref=held[i].at[d],
            send_sem=send.at[i, d],
            recv_sem=recv.at[i, d],
            device_id=(me ^ d, tp),
            device_id_type=MESH,
        )

    def spread(i, d, rank):
        return pltpu.make_async_remote_copy(
            src_ref=dst[i].at[rank],
            dst_ref=dst[i].at[rank],
            send_sem=send.at[i, N_CTX + d],
            recv_sem=recv.at[i, N_CTX + d],
            device_id=(me ^ d, tp),
            device_id_type=MESH,
        )

    for i in range(n):
        for d in range(1, N_CTX):
            scatter(i, d).start()
    for i in range(n):
        for d in range(1, N_CTX):
            scatter(i, d).wait_recv()
        total = src[i][me].astype(f32)
        for d in range(1, N_CTX):
            total = total + held[i][d].astype(f32)
        if spread_too[i]:
            dst[i][me] = total.astype(dst[i].dtype)
            for d in range(1, N_CTX):
                spread(i, d, me).start()
        else:
            dst[i][...] = total
    for i in range(n):
        for d in range(1, N_CTX):
            scatter(i, d).wait_send()
            if spread_too[i]:
                spread(i, d, me ^ d).wait_recv()
                spread(i, d, me).wait_send()


def reduce_ctx(arrays, spread_too):
    outs = [
        jax.ShapeDtypeStruct(a.shape if s else a.shape[1:], a.dtype if s else f32)
        for a, s in zip(arrays, spread_too)
    ]
    n = len(arrays)
    return pl.pallas_call(
        functools.partial(reduce_kernel, spread_too),
        out_shape=tuple(outs),
        in_specs=[VMEM] * n,
        out_specs=tuple([VMEM] * n),
        scratch_shapes=[pltpu.VMEM(a.shape, a.dtype) for a in arrays]
        + [pltpu.SemaphoreType.DMA((n, 2 * N_CTX)), pltpu.SemaphoreType.DMA((n, 2 * N_CTX))],
        compiler_params=pltpu.CompilerParams(
            collective_id=10, has_side_effects=True, vmem_limit_bytes=48 << 20
        ),
        name="reduce_ctx",
    )(*arrays)


def rms_scale(values, gain):
    return values * lax.rsqrt(jnp.mean(values * values, axis=-1, keepdims=True) + eps) * gain


def norm_back(values, gain, grad_normed):
    inverse = lax.rsqrt(jnp.mean(values * values, axis=-1, keepdims=True) + eps)
    scaled = grad_normed * gain
    return inverse * scaled - values * inverse**3 * jnp.mean(
        scaled * values, axis=-1, keepdims=True
    )


def doc_layout(doc_lengths, positions):
    ends = jnp.cumsum(doc_lengths, axis=1)
    passed = positions[None, :, None] >= ends[:, None, :]
    doc_ids = jnp.sum(passed.astype(jnp.int32), axis=2)
    starting = jnp.sum(jnp.where(passed, doc_lengths[:, None, :], 0), axis=2)
    inside = positions[None, :] < ends[:, -1:]
    doc_ids = jnp.where(inside, doc_ids, -1 - positions[None, :])
    return (doc_ids, positions[None, :] - starting)


def dot(a, b, ca=1, cb=0):
    return lax.dot_general(a, b, (((ca,), (cb,)), ((), ())), preferred_element_type=f32)


def rope(x, cosine, sine, sign):
    half = HEAD_DIM // 2
    x1, x2 = x[..., :half], x[..., half:]
    s = sine * sign
    return jnp.concatenate([x1 * cosine - x2 * s, x2 * cosine + x1 * s], axis=-1)


def gates_of(logits, onehot):
    chosen = jnp.sum(logits[:, None, :] * onehot, axis=-1)
    return jax.nn.softmax(chosen, axis=-1)


def gates_back(gates, grad_gates, onehot):
    inner = gates * (grad_gates - jnp.sum(gates * grad_gates, axis=-1, keepdims=True))
    return jnp.sum(inner[..., None] * onehot, axis=1)


def shards(
    tokens,
    norm1_gain,
    router_attn,
    w_query,
    w_key_value,
    w_out,
    norm2_gain,
    router_ffn,
    w_gate_up,
    w_down,
    adapt_wide,
    adapt_heads,
    adapt_ffn,
    attention_routes,
    feedforward_routes,
    doc_lengths,
    adapter_index,
    cotangent,
):
    seqs, block, part = tokens.shape
    rows = seqs * block
    n_ctx = lax.axis_size("ctx")
    n_tp = lax.axis_size("tp")
    model = part * n_tp
    experts = w_query.shape[0]
    width = w_query.shape[2]
    heads = width // HEAD_DIM
    hidden = w_down.shape[1]
    rank = adapt_heads.shape[2]
    wide_slots = adapt_wide.shape[1]
    ctx_rank = lax.axis_index("ctx")
    tp_rank = lax.axis_index("tp")

    def split(a):
        return a.reshape((seqs, block) + a.shape[1:])

    def merge(a):
        return a.reshape((rows,) + a.shape[2:])

    wide_own = adapt_wide.astype(bf16)[adapter_index]
    wide_cols = wide_own.reshape(seqs * wide_slots * rank, -1).T
    heads_low = adapt_heads.astype(bf16)[adapter_index]
    ffn_low = adapt_ffn.astype(bf16)[adapter_index]
    (w_query, w_key_value, w_out, w_gate_up, w_down, wide), (x0, dy) = gather_all(
        [
            w_query,
            w_key_value.reshape(-1, 2 * width),
            w_out,
            w_gate_up.reshape(experts, -1, 2 * hidden),
            w_down,
        ],
        ["rows", "flat", "cols", "rows", "cols", "flat"],
        [tokens.reshape(rows, part), cotangent.reshape(rows, part), wide_cols],
        ["cols", "cols", "rows"],
    )
    w_gate_up = w_gate_up.reshape(experts, model, 2, hidden)
    wide = wide.reshape(model, seqs, wide_slots, rank)
    xf = x0.astype(f32)
    n1 = rms_scale(xf, norm1_gain).astype(bf16)
    route_a = attention_routes.reshape(rows, -1)
    route_f = feedforward_routes.reshape(rows, -1)
    hot_a = jax.nn.one_hot(route_a, experts, dtype=f32)
    hot_f = jax.nn.one_hot(route_f, experts, dtype=f32)
    ga = gates_of(dot(n1, router_attn), hot_a)
    ga_e = jnp.sum(ga[..., None] * hot_a, axis=1)

    positions = ctx_rank * block + jnp.arange(block, dtype=jnp.int32)
    doc_ids, offsets = doc_layout(doc_lengths, positions)
    half = HEAD_DIM // 2
    frequency = 10000.0 ** (-2.0 * jnp.arange(half, dtype=f32) / HEAD_DIM)
    angles = offsets.astype(f32).reshape(rows)[:, None] * frequency
    cosine, sine = jnp.cos(angles), jnp.sin(angles)

    def low_in(v, first, count):
        return merge(
            jnp.einsum(
                "sbd,dscr->sbcr", split(v), wide[:, :, first : first + count],
                preferred_element_type=f32,
            )
        )

    def low_out(z, factor):
        return merge(
            jnp.einsum("sbcr,scrh->sbch", split(z).astype(bf16), factor, preferred_element_type=f32)
        )

    def low_sum(z, factor):
        return merge(
            jnp.einsum("sbcr,scrh->sbh", split(z).astype(bf16), factor, preferred_element_type=f32)
        )

    def low_back(dp, factor):
        return merge(
            jnp.einsum("sbch,scrh->sbcr", split(dp), factor, preferred_element_type=f32)
        )

    def low_grad(z, dp):
        return jnp.einsum(
            "sbcr,sbch->scrh", split(z).astype(bf16), split(dp), preferred_element_type=f32
        )

    z_q = low_in(n1, 0, experts)
    z_kv = low_in(n1, experts, 2)
    b_q, b_kv, a_o = heads_low[:, :experts], heads_low[:, experts : experts + 2], heads_low[:, experts + 2 :]
    q_all = jnp.stack([dot(n1, w_query[e]) for e in range(experts)], axis=1) + low_out(z_q, b_q)
    q_pre = jnp.einsum("rke,reh->rkh", hot_a, q_all, precision=lax.Precision.HIGHEST)
    q = rope(
        q_pre.reshape(rows, -1, heads, HEAD_DIM), cosine[:, None, None], sine[:, None, None], 1.0
    ).astype(bf16)
    kv = dot(n1, w_key_value.reshape(model, 2 * width)).reshape(rows, 2, width) + low_out(z_kv, b_kv)
    k_own = rope(
        kv[:, 0].reshape(rows, heads, HEAD_DIM), cosine[:, None], sine[:, None], 1.0
    ).astype(bf16)
    v_own = kv[:, 1].reshape(rows, heads, HEAD_DIM).astype(bf16)
    kv_own = jnp.concatenate([k_own, v_own], axis=1).reshape(seqs, block, 2 * width)
    kv_all = halo(kv_own)
    length = kv_all.shape[1]
    kv_all = kv_all.reshape(seqs, length, 2, heads, HEAD_DIM)
    key_pos = (ctx_rank - PAST) * block + jnp.arange(length, dtype=jnp.int32)
    key_doc = doc_layout(doc_lengths, jnp.maximum(key_pos, 0))[0]
    allowed = (
        (key_pos >= 0)[None, None, :] &
        (doc_ids[:, :, None] == key_doc[:, None, :])
        & (key_pos[None, None, :] <= positions[None, :, None])
        & (positions[None, :, None] - key_pos[None, None, :] < WINDOW)
    )[:, None, None]
    scale = HEAD_DIM ** (-0.5)
    q_s = q.reshape(seqs, block, -1, heads, HEAD_DIM)
    scores = jnp.einsum("sqthd,skhd->sthqk", q_s, kv_all[:, :, 0], preferred_element_type=f32) * scale
    scores = jnp.where(allowed, scores, big_negative)
    peak = jnp.max(scores, axis=-1, keepdims=True)
    weights = jnp.where(allowed, jnp.exp(scores - peak), 0.0)
    total = jnp.sum(weights, axis=-1, keepdims=True)
    probs = weights / total
    o = jnp.einsum(
        "sthqk,skhd->sqthd", probs.astype(bf16), kv_all[:, :, 1], preferred_element_type=f32
    )
    ob = o.astype(bf16).reshape(rows, -1, width)
    ob_e = jnp.einsum("rke,rkh->reh", hot_a.astype(bf16), ob, preferred_element_type=f32).astype(bf16)
    z_o = low_back(ob_e, a_o)
    b_o = jnp.transpose(wide[:, :, 14:18], (1, 2, 3, 0))
    part_out = sum(ga_e[:, e, None] * dot(ob_e[:, e], w_out[e]) for e in range(experts))
    part_out = part_out + low_sum(z_o * ga_e[..., None], b_o)
    (sum_out,) = exchange([part_out.astype(bf16)], ["ar_cols"], 1)
    sum_out = sum_out.astype(f32)
    x1 = xf + sum_out
    n2 = rms_scale(x1, norm2_gain).astype(bf16)
    gf = gates_of(dot(n2, router_ffn), hot_f)
    gf_e = jnp.sum(gf[..., None] * hot_f, axis=1)
    z_gu = low_in(n2, experts + 2, 2 * experts)
    b_gu, a_d = ffn_low[:, : 2 * experts], ffn_low[:, 2 * experts :]
    b_d = jnp.transpose(wide[:, :, 18:22], (1, 2, 3, 0))
    dz_d = low_in(dy, 18, experts)
    low_gu = low_out(z_gu, b_gu)
    low_dh = low_out(dz_d, a_d)
    h_all, dh_gate, dgp_all, dup_all = [], [], [], []
    for e in range(experts):
        gp = dot(n2, w_gate_up[e, :, 0]) + low_gu[:, e]
        up = dot(n2, w_gate_up[e, :, 1]) + low_gu[:, experts + e]
        sg = jax.nn.sigmoid(gp)
        silu = gp * sg
        h = (silu * up).astype(bf16)
        dh0 = dot(dy, w_down[e], 1, 1) + low_dh[:, e]
        dh_gate.append(jnp.sum(dh0 * h.astype(f32), axis=1))
        dh = dh0 * gf_e[:, e, None]
        dgp_all.append((dh * up * sg * (1.0 + gp * (1.0 - sg))).astype(bf16))
        dup_all.append((dh * silu).astype(bf16))
        h_all.append(h)
    h_all = jnp.stack(h_all, axis=1)
    d_gu = jnp.stack(dgp_all + dup_all, axis=1)
    z_d = low_back(h_all, a_d)
    part_ffn = sum(gf_e[:, e, None] * dot(h_all[:, e], w_down[e]) for e in range(experts))
    part_ffn = part_ffn + low_sum(z_d * gf_e[..., None], b_d)

    def own(a):
        return lax.dynamic_slice_in_dim(a, tp_rank * part, part, 1)

    dgf = jnp.sum(jnp.stack(dh_gate, axis=1)[:, None, :] * hot_f, axis=-1)
    dlf = gates_back(gf, dgf, hot_f)
    dz_gu = low_back(d_gu, b_gu)
    a_gu = jnp.transpose(wide[:, :, 6:14], (1, 2, 3, 0))
    dn2 = sum(
        dot(d_gu[:, e], w_gate_up[e, :, 0], 1, 1) + dot(d_gu[:, experts + e], w_gate_up[e, :, 1], 1, 1)
        for e in range(experts)
    )
    dn2 = dn2 + low_sum(dz_gu, a_gu) + dot(dlf.astype(bf16), router_ffn, 1, 1)
    back2 = norm_back(x1, norm2_gain, dn2)
    z_part = jnp.concatenate([z_o * ga_e[..., None], dz_gu, z_d * gf_e[..., None]], axis=1)
    z_part = jnp.pad(z_part.reshape(rows, -1).astype(bf16), ((0, 0), (0, 128)))
    sum_back, mixed_own, z_sum = exchange(
        [back2.astype(bf16), part_ffn.astype(bf16), z_part], ["ar_cols", "rs_cols", "ar_rows"], 2
    )
    z_sum = z_sum[:, :256].reshape(rows, 16, rank)
    dx1 = dy.astype(f32) + sum_back.astype(f32)
    mixed = (mixed_own + own(x1)).astype(bf16)
    dx1b = dx1.astype(bf16)
    dz_o = low_in(dx1b, 14, experts)
    g_e = jnp.stack([dot(dx1b, w_out[e], 1, 1) for e in range(experts)], axis=1) + low_out(dz_o, a_o)
    g_k = jnp.einsum("rke,reh->rkh", hot_a, g_e, precision=lax.Precision.HIGHEST)
    dga = jnp.sum(g_k * ob.astype(f32), axis=-1)
    dob = (g_k * ga[..., None]).astype(bf16)
    dob_s = dob.reshape(seqs, block, -1, heads, HEAD_DIM)
    delta = jnp.sum(dob_s.astype(f32) * o, axis=-1)
    delta = jnp.transpose(delta, (0, 2, 3, 1))[..., None]
    d_p = jnp.einsum("sqthd,skhd->sthqk", dob_s, kv_all[:, :, 1], preferred_element_type=f32)
    d_s = (probs * (d_p - delta)).astype(bf16)
    dqr = jnp.einsum("sthqk,skhd->sqthd", d_s, kv_all[:, :, 0], preferred_element_type=f32) * scale
    dkr = jnp.einsum("sthqk,sqthd->skhd", d_s, q_s, preferred_element_type=f32) * scale
    dvv = jnp.einsum("sthqk,sqthd->skhd", probs.astype(bf16), dob_s, preferred_element_type=f32)
    dkv = jnp.concatenate([dkr, dvv], axis=2).reshape(seqs, length, 2 * width).astype(bf16)
    dkv = halo_back(dkv)
    dkv = dkv.reshape(rows, 2, heads, HEAD_DIM)
    dkp = rope(dkv[:, 0], cosine[:, None], sine[:, None], -1.0).astype(bf16).reshape(rows, width)
    dvp = dkv[:, 1].astype(bf16).reshape(rows, width)
    dqp = rope(
        dqr.reshape(rows, -1, heads, HEAD_DIM), cosine[:, None, None], sine[:, None, None], -1.0
    ).astype(bf16).reshape(rows, -1, width)
    dq_e = jnp.einsum("rke,rkh->reh", hot_a.astype(bf16), dqp, preferred_element_type=f32).astype(bf16)
    dkv_p = jnp.stack([dkp, dvp], axis=1)
    dz_q = low_back(dq_e, b_q)
    dz_kv = low_back(dkv_p, b_kv)
    a_qkv = jnp.transpose(wide[:, :, :6], (1, 2, 3, 0))
    dz_qkv = jnp.concatenate([dz_q, dz_kv], axis=1)
    dla = gates_back(ga, dga, hot_a)
    dn1 = sum(dot(dq_e[:, e], w_query[e], 1, 1) for e in range(experts))
    dn1 = dn1 + dot(dkv_p.reshape(rows, 2 * width), w_key_value.reshape(model, 2 * width), 1, 1)
    dn1 = dn1 + low_sum(dz_qkv, a_qkv) + dot(dla.astype(bf16), router_attn, 1, 1)
    back1 = norm_back(xf, norm1_gain, dn1)
    dz_part = jnp.pad(dz_qkv.reshape(rows, -1).astype(bf16), ((0, 0), (0, 32)))
    back_own, dz_sum = exchange([back1.astype(bf16), dz_part], ["rs_cols", "ar_rows"], 3)
    dz_sum = dz_sum[:, :96].reshape(rows, 6, rank)
    grad_tokens = (back_own + own(dx1)).astype(bf16)
    grad_heads = jnp.concatenate(
        [low_grad(z_q, dq_e), low_grad(z_kv, dkv_p), low_grad(dz_o * ga_e[..., None], ob_e)], axis=1
    )
    grad_ffn = jnp.concatenate(
        [low_grad(z_gu, d_gu), low_grad(dz_d * gf_e[..., None], h_all)], axis=1
    )
    def strided(a):
        return lax.dynamic_slice_in_dim(
            a.reshape(rows, n_ctx, n_tp, model // (n_ctx * n_tp)), tp_rank, 1, 2
        ).reshape(seqs, block, -1)

    def wide_grad(z, v):
        return jnp.einsum("sbcr,sbm->mscr", split(z).astype(bf16), strided(v), preferred_element_type=f32)

    wide_terms = jnp.concatenate(
        [
            wide_grad(dz_sum, n1),
            wide_grad(z_sum[:, 4:12], n2),
            wide_grad(z_sum[:, :4], dx1b),
            wide_grad(z_sum[:, 12:], dy),
        ],
        axis=2,
    ).reshape(-1, seqs * wide_slots * rank)
    head_rows = seqs * grad_heads.shape[1] * rank // N_CTX
    head_terms = jnp.pad(
        grad_heads.reshape(N_CTX, head_rows, width).astype(bf16), ((0, 0), (0, 32 - head_rows), (0, 0))
    )
    grad_wide, head_sum = reduce_ctx(
        [wide_terms.reshape(N_CTX, -1, seqs * wide_slots * rank).astype(bf16), head_terms],
        [False, True],
    )
    grad_wide = grad_wide.T.reshape(seqs, wide_slots, rank, -1)[adapter_index]
    grad_heads = head_sum[:, :head_rows].astype(f32).reshape(grad_heads.shape)[adapter_index]
    grad_ffn = lax.psum(grad_ffn.astype(bf16), "ctx").astype(f32)[adapter_index]
    mixed = mixed.reshape(seqs, block, part)
    grad_tokens = grad_tokens.reshape(seqs, block, part)
    return (mixed, grad_tokens, grad_wide, grad_heads, grad_ffn)


def solution(mesh):
    placed = (
        P(None, "ctx", "tp"),
        P(),
        P(),
        P(None, "ctx", "tp"),
        P("ctx", None, "tp"),
        P(None, "tp", "ctx"),
        P(),
        P(),
        P(None, "ctx", None, "tp"),
        P(None, "tp", "ctx"),
        P(None, None, None, ("ctx", "tp")),
        P(None, None, None, "tp"),
        P(None, None, None, "tp"),
        P(None, "ctx", None),
        P(None, "ctx", None),
        P(),
        P(),
        P(None, "ctx", "tp"),
    )
    return jax.shard_map(
        shards,
        mesh=mesh,
        in_specs=placed,
        out_specs=(
            P(None, "ctx", "tp"),
            P(None, "ctx", "tp"),
            P(None, None, None, ("ctx", "tp")),
            P(None, None, None, "tp"),
            P(None, None, None, "tp"),
        ),
        check_vma=False,
    )
```

time: 2580 us -> 799 us (0.31)
  waiting for transfers between devices: 1460 us -> 0.02 us
  local copies, waits for them, and re-layouts: 524 us -> 165 us
  other arithmetic: 183 us -> 60 us
  Pallas kernels: 313 us -> 420 us
  matrix products: 47 us -> 124 us
    reduce_scatter x4 -> x0, waiting for transfers between devices: 773 us -> none  [the longest x1 703 us: shards(): lax.psum_scatter(wide_terms, ('ctx', 'tp'), scatter_dimension=3, tiled=True)]
    all_gather x9 -> x0, waiting for transfers between devices: 513 us -> none  [the longest x1 326 us: shards(): lax.all_gather(adapt_wide.astype(jnp.bfloat16), ('ctx', 'tp'), axis=3, ti...]
    pallas_call x0 -> x7, Pallas kernels: none -> 420 us  [the longest x1 200 us: gather_all(): pl.pallas_call(body, out_shape=tuple(shapes + tp_shapes), in_specs=[ANY]...]
    another operation x26 -> x0, Pallas kernels: 307 us -> none
    transpose x17 -> x3, local copies, waits for them, and re-layouts: 203 us -> 0.24 us  [low_out(): jnp.einsum('sbcr,scrh->sbch', split(z).astype(bf16), factor, preferred_el...]
    psum x3 -> x1, waiting for transfers between devices: 174 us -> 0.01 us  [shards(): grad_ffn = lax.psum(grad_ffn.astype(bf16), 'ctx').astype(f32)[adapter_index]]
    gather x30 -> x7, local copies, waits for them, and re-layouts: 90.4 us -> 6.72 us  [the longest x1 1.76 us: shards(): grad_ffn = lax.psum(grad_ffn.astype(bf16), 'ctx').astype(f32)[adapter_index]]
    dot_general x28 -> x74, matrix products: 47 us -> 113 us  [the longest x46 73.7 us: dot(): lax.dot_general(a, b, (((ca,), (cb,)), ((), ())), preferred_element_type=...]
  transfers between devices with their start and end apart: 16 -> 1, of which waited for: 8 -> 0; matrix products, arithmetic and copies ran while one was open for 23% -> 16% of each run, Pallas kernels for 5% -> 18%
where the time goes in v1:
time: 799 us; the launch traced here: 787 us
  Pallas kernels  420 us (53%)
  local copies, waits for them, and re-layouts  165 us (21%)
  matrix products  124 us (16%)
  other arithmetic  60 us (8%)
  between operations  16.8 us (2%)
    pallas_call x1, Pallas kernels, gather_all(): pl.pallas_call(body, out_shape=tuple(shapes + tp_shapes), in_specs=[ANY]...  200 us
    pallas_call x3, Pallas kernels, exchange(): pl.pallas_call(functools.partial(exchange_kernel, kinds), out_shape=tuple...  103 us
    dot_general x46, matrix products, dot(): lax.dot_general(a, b, (((ca,), (cb,)), ((), ())), preferred_element_type=...  73.7 us
    pallas_call x1, Pallas kernels, halo(): pl.pallas_call(halo_kernel, out_shape=jax.ShapeDtypeStruct((seqs, (PAST +...  49.7 us
    pallas_call x1, Pallas kernels, reduce_ctx(): pl.pallas_call(functools.partial(reduce_kernel, spread_too), out_shape=tu...  43.3 us
    pallas_call x3, local copies, waits for them, and re-layouts, gather_all(): pl.pallas_call(body, out_shape=tuple(shapes + tp_shapes), in_specs=[ANY]...  35 us
    unnamed x308, local copies, waits for them, and re-layouts  32.7 us
    pallas_call x1, Pallas kernels, halo_back(): pl.pallas_call(halo_back_kernel, out_shape=jax.ShapeDtypeStruct((seqs, bl...  24.9 us
  transfers between devices with their start and end apart: 1, of which 0 were waited for; matrix products, arithmetic and copies ran while one was open for 16% of the time, Pallas kernels for 18%

profile of v1, /device:TPU:1, one launch (start us, length us, event | category | flops | bytes accessed | tf_op | source)
XLA Modules:
  0.0 786.8 jit_solution(1181871758845308260)
XLA Ops:
  16.6 199.8 %gather_all.1 = (bf16[4,2048,256]{2,1,0:T(8,128)(2,1)}, bf16[2048,512]{1,0:T(8,128)(2,1)}, bf16[4,256,2048]{2,1,0:T(8,128)(2,1)}, bf16[4,2048,1408]{2,1,0:T(8,12...) custom-call(bf16[4,128,256]{2,1,0:T(8,128)(2,1)} %refs_0_.1, ...), custom_call_target="tpu_custom_call" | custom-call | tf_op jit(solution)/shard_map/gather_all/pallas_call | solution.py:191
  218.5 4.7 copy.255
  248.5 49.7 %halo.1 = bf16[2,1152,512]{2,1,0:T(8,128)(2,1)} custom-call(bf16[2,128,512]{2,1,0:T(8,128)(2,1)} %copy.361.src), custom_call_target="tpu_custom_call" | custom-call | tf_op jit(solution)/shard_map/halo/pallas_call | solution.py:329
  298.2 6.1 reshape.846
  304.3 4.1 fusion.250
  321.4 5.5 fusion.254
  339.1 31.5 %exchange_1.1 = bf16[256,2048]{1,0:T(8,128)(2,1)S(1)} custom-call(bf16[256,2048]{1,0:T(8,128)(2,1)S(1)} %fusion.64.refs_0_), custom_call_target="tpu_custom_call" | custom-call | tf_op jit(solution)/shard_map/exchange_1/pallas_call | solution.py:284
  373.7 28.9 %copy.282 = bf16[4,2048,1408]{1,2,0:T(8,128)(2,1)} copy(bf16[4,2048,1408]{2,1,0:T(8,128)(2,1)} %get-tuple-element.27) | data formatting | bytes 46137344 | tf_op jit(solution)/shard_map/gather_all/pallas_call | solution.py:191
  404.3 3.9 convolution_bitcast_fusion.2
  408.3 3.9 copy.509
  412.2 3.5 copy-done.1
  450.7 3.6 select_reduce_fusion.1
  511.4 3.0 fusion.66
  531.4 3.1 fusion.55
  544.6 4.4 fusion.61.refs_1_
  549.6 49.6 %exchange_2.1 = (bf16[256,2048]{1,0:T(8,128)(2,1)S(1)}, f32[256,256]{1,0:T(8,128)S(1)}, bf16[256,384]{1,0:T(8,128)(2,1)S(1)}) custom-call(bf16[256,2048]{1,0:T(8,128)(2,1)S(1)} %subtract_convert_fusion.refs_0_, bf16[256,2048]{1,0:T(8,128)(2,1)S(1)} %fusion.61.refs_1_, bf16[256,384]{1,0:T(8,128)(2,1)S(1)} %pad.12.refs_2_), custom_call_target="tpu_custom_call" | custom-call | tf_op jit(solution)/shard_map/exchange_2/pallas_call | solution.py:284
  606.5 4.4 multiply_reduce_fusion.6
  613.6 3.4 fusion.3
  622.5 24.9 %halo_back.1 = f32[2,128,512]{2,1,0:T(8,128)S(1)} custom-call(bf16[2,1152,512]{2,1,0:T(8,128)(2,1)S(1)} %copy.375.src), custom_call_target="tpu_custom_call" | custom-call | tf_op jit(solution)/shard_map/halo_back/pallas_call | solution.py:378
  648.0 3.9 fusion.115
  696.7 21.6 %exchange_3.1 = (f32[256,256]{1,0:T(8,128)S(1)}, bf16[256,128]{1,0:T(8,128)(2,1)S(1)}) custom-call(bf16[256,2048]{1,0:T(8,128)(2,1)S(1)} %fusion.92.refs_0_, bf16[256,128]{1,0:T(8,128)(2,1)S(1)} %pad.13.refs_1_), custom_call_target="tpu_custom_call" | custom-call | tf_op jit(solution)/shard_map/exchange_3/pallas_call | solution.py:284
  719.7 3.0 convert_element_type.340
  722.7 3.9 copy.343.refs_0_
  726.7 43.3 %reduce_ctx.1 = (f32[16,704]{1,0:T(8,128)S(1)}, bf16[16,32,256]{2,1,0:T(8,128)(2,1)S(1)}) custom-call(bf16[16,16,704]{2,1,0:T(8,128)(2,1)S(1)} %copy.343.refs_0_, bf16[16,32,256]{2,1,0:T(8,128)(2,1)S(1)} %pad.14.refs_1_), custom_call_target="tpu_custom_call" | custom-call | tf_op jit(solution)/shard_map/reduce_ctx/pallas_call | solution.py:456
  (562 shorter events, 256.2 us)
Async XLA Ops:
  7.2 436.5 %copy-start = (bf16[2048,4]{0,1:T(4,128)(2,1)S(1)}, bf16[2048,4]{0,1:T(4,128)(2,1)}, u32[]{:S(2)}) copy-start(bf16[2048,4]{0,1:T(4,128)(2,1)} %param.25) | copy-start | bytes 49156
  7.2 769.4 %all-reduce.5.cloned.1.call-start = ((), (), s32[]{:S(2)}) async-start(), calls=%async_computation | async-start | bytes 1179648 | tf_op jit(solution)/shard_map/psum | solution.py:779
  7.3 235.1 %copy-start.114 = (s32[1152]{0:T(1024)}, s32[1152]{0:T(1024)S(1)}, u32[]{:S(2)}) copy-start(s32[1152]{0:T(1024)S(1)} %get-tuple-element.122) | copy-start | bytes 13828
  14.8 211.2 %copy-start.36 = (bf16[2,10,16,256]{3,2,1,0:T(8,128)(2,1)}, bf16[2,10,16,256]{3,2,1,0:T(8,128)(2,1)S(1)}, u32[]{:S(2)}) copy-start(bf16[2,10,16,256]{3,2,1,0:T(8,128)(2,1)S(1)} %gather_fusion.1) | copy-start | bytes 491524
  224.7 83.7 %copy-start.8 = (bf16[256,2048]{1,0:T(8,128)(2,1)}, bf16[256,2048]{1,0:T(8,128)(2,1)S(1)}, u32[]{:S(2)}) copy-start(bf16[256,2048]{1,0:T(8,128)(2,1)S(1)} %fusion.89) | copy-start | bytes 3145732
  233.9 75.8 %copy-start.48 = (s32[256,2]{1,0:T(8,128)}, s32[256,2]{1,0:T(8,128)S(1)}, u32[]{:S(2)}) copy-start(s32[256,2]{1,0:T(8,128)S(1)} %copy.253) | copy-start | bytes 6148
  233.9 8.0 %copy-start.135 = (s32[2,8]{1,0:T(2,128)S(1)}, s32[2,8]{1,0:T(2,128)}, u32[]{:S(2)}) copy-start(s32[2,8]{1,0:T(2,128)} %param.33) | copy-start | bytes 196
  234.3 9.9 %slice-start.6 = ((f32[256,2,256]{2,0,1:T(8,128)}), f32[256,1,256]{2,0,1:T(8,128)S(1)}, s32[]{:S(2)}) async-start(f32[256,2,256]{2,0,1:T(8,128)} %copy-done.58), calls=%async_computation.7 | async-start | bytes 524288 | tf_op jit(solution)/shard_map/slice | solution.py:625
  235.3 9.1 %copy-start.26 = (f32[256,2]{1,0:T(8,128)}, f32[256,2]{1,0:T(8,128)S(1)}, u32[]{:S(2)}) copy-start(f32[256,2]{1,0:T(8,128)S(1)} %select_reduce_fusion.6) | copy-start | bytes 6148
  236.6 7.5 copy-start.91
  315.4 14.2 %copy-start.28 = (bf16[2,1152,1,2,128]{1,4,3,0,2:T(8,128)(2,1)}, bf16[2,1152,1,2,128]{1,4,3,0,2:T(8,128)(2,1)S(1)}, u32[]{:S(2)}) copy-start(bf16[2,1152,1,2,128]{1,4,3,0,2:T(8,128)(2,1)S(1)} %copy.388) | copy-start | bytes 3538948
  339.1 31.6 %copy-start.71 = (f32[2,12,16,704]{3,2,1,0:T(8,128)S(1)}, f32[2,12,16,704]{3,2,1,0:T(8,128)}, u32[]{:S(2)}) copy-start(f32[2,12,16,704]{3,2,1,0:T(8,128)} %param.30) | copy-start | bytes 3244036
  371.4 32.9 %copy-start.17 = (bf16[2,12,16,704]{3,2,1,0:T(8,128)(2,1)}, bf16[2,12,16,704]{3,2,1,0:T(8,128)(2,1)S(1)}, u32[]{:S(2)}) copy-start(bf16[2,12,16,704]{3,2,1,0:T(8,128)(2,1)S(1)} %gather_fusion.2) | copy-start | bytes 1622020
  373.7 29.0 %copy-start.128 = (f32[256]{0:T(256)}, f32[256]{0:T(256)S(1)}, u32[]{:S(2)}) copy-start(f32[256]{0:T(256)S(1)} %get-tuple-element.106) | copy-start | bytes 3076
  373.7 29.0 %copy-start.116 = (f32[2048]{0:T(1024)S(1)}, f32[2048]{0:T(1024)}, u32[]{:S(2)}) copy-start(f32[2048]{0:T(1024)} %param.24) | copy-start | bytes 24580
  403.2 25.4 %copy-start.15 = (bf16[256,2048]{1,0:T(8,128)(2,1)}, bf16[256,2048]{1,0:T(8,128)(2,1)S(1)}, u32[]{:S(2)}) copy-start(bf16[256,2048]{1,0:T(8,128)(2,1)S(1)} %multiply_convert_fusion) | copy-start | bytes 3145732
  404.3 11.4 %copy-start.1 = (bf16[4,2048,1408]{1,2,0:T(8,128)(2,1)S(1)}, bf16[4,2048,1408]{1,2,0:T(8,128)(2,1)}, u32[]{:S(2)}) copy-start(bf16[4,2048,1408]{1,2,0:T(8,128)(2,1)} %copy.282) | copy-start | bytes 69206016
  491.1 7.9 %copy-start.62 = (bf16[2,128,1,704]{1,0,3,2:T(2,128)(2,1)S(1)}, bf16[2,128,1,704]{1,0,3,2:T(2,128)(2,1)}, u32[]{:S(2)}) copy-start(bf16[2,128,1,704]{1,0,3,2:T(2,128)(2,1)} %stack.104) | copy-start | bytes 1081348
  491.1 8.7 %copy-start.97 = (f32[2,128,128]{1,2,0:S(1)}, f32[2,128,128]{1,2,0}, u32[]{:S(2)}) copy-start(f32[2,128,128]{1,2,0} %copy-done.96) | copy-start | bytes 393220
  508.4 12.4 %slice-start.3 = ((s8[11534336]{0:T(1024)(128)(4,1)}), s8[4194304]{0:T(1024)(128)(4,1)S(1)}, s32[]{:S(2)}) async-start(s8[11534336]{0:T(1024)(128)(4,1)} %bitcast.659), calls=%async_computation.4 | async-start | bytes 8388608
  511.4 9.4 %slice-start.4 = ((s8[11534336]{0:T(1024)(128)(4,1)}), s8[4194304]{0:T(1024)(128)(4,1)S(1)}, s32[]{:S(2)}) async-start(s8[11534336]{0:T(1024)(128)(4,1)} %bitcast.659), calls=%async_computation.5 | async-start | bytes 8388608
  696.7 22.9 %copy-start.94 = (bf16[256,2,8,16]{0,3,2,1:T(8,128)(2,1)S(1)}, bf16[256,2,8,16]{0,3,2,1:T(8,128)(2,1)}, u32[]{:S(2)}) copy-start(bf16[256,2,8,16]{0,3,2,1:T(8,128)(2,1)} %convert_bitcast_fusion) | copy-start | bytes 393220
  696.7 22.9 %copy-start.107 = (bf16[256,2,4,16]{0,3,2,1:T(8,128)(2,1)S(1)}, bf16[256,2,4,16]{0,3,2,1:T(8,128)(2,1)}, u32[]{:S(2)}) copy-start(bf16[256,2,4,16]{0,3,2,1:T(8,128)(2,1)} %convert_bitcast_fusion.2) | copy-start | bytes 196612
  696.7 22.9 %copy-start.108 = (bf16[256,2,4,16]{0,3,2,1:T(8,128)(2,1)S(1)}, bf16[256,2,4,16]{0,3,2,1:T(8,128)(2,1)}, u32[]{:S(2)}) copy-start(bf16[256,2,4,16]{0,3,2,1:T(8,128)(2,1)} %convert_bitcast_fusion.3) | copy-start | bytes 196612
  (125 other events, 352.8 us)
Sparse Core Ops, SparseCore 0:
  505.9 116.4 all-reduce.4

commit v2 on v1

--- a/solution.py
+++ b/solution.py
@@ -1,6 +1,7 @@
 import functools
 
 import jax
+import numpy as np
 import jax.numpy as jnp
 from jax import lax
 from jax.experimental import pallas as pl
@@ -510,6 +511,735 @@
     return jnp.sum(inner[..., None] * onehot, axis=1)
 
 
+def dot_nt(a, b):
+    return dot(a, b, 1, 1)
+
+
+def dot_tn(a, b):
+    return dot(a, b, 0, 0)
+
+
+def by_seq(rows, f):
+    half = rows.shape[0] // 2
+    return jnp.concatenate([f(0, rows[:half]), f(1, rows[half:])], axis=0)
+
+
+def column_of(values, lane, e):
+    return jnp.sum(jnp.where(lane == e, values, 0.0), axis=1, keepdims=True)
+
+
+def greet(targets):
+    barrier = pltpu.get_barrier_semaphore()
+    for device in targets:
+        pl.semaphore_signal(barrier, inc=1, device_id=device, device_id_type=MESH)
+    pl.semaphore_wait(barrier, len(targets))
+
+
+def masked_gates(logits, hot):
+    largest = jnp.max(jnp.where(hot > 0, logits, big_negative), axis=1, keepdims=True)
+    powers = jnp.where(hot > 0, jnp.exp(logits - largest), 0.0)
+    return powers / jnp.sum(powers, axis=1, keepdims=True)
+
+
+def ffn_kernel(
+    x0, attn, dy, gain, wide, router, hot, b_gu, a_d, z_o, w_gu_hbm, w_d_hbm,
+    mixed, dx1, dx1_own, n2, z_sum, g_gu, g_d,
+    w_gu, w_d, hg, dgu, dh_tmp, z_gu, dz_d, z_part, parts, own, held, z_held, dots, tails,
+    load, send, recv,
+):
+    me, tp = lax.axis_index("ctx"), lax.axis_index("tp")
+    rows, model = x0.shape
+    experts = w_gu.shape[0]
+    part = model // N_TP
+    greet([(me, tp ^ d) for d in range(1, N_TP)])
+
+    def fetch(e):
+        return (
+            pltpu.make_async_copy(w_gu_hbm.at[e], w_gu.at[e], load.at[0, e]),
+            pltpu.make_async_copy(w_d_hbm.at[e], w_d.at[e], load.at[1, e]),
+        )
+
+    for e in range(experts):
+        for c in fetch(e):
+            c.start()
+
+    step = 32
+
+    def normalize(i, carry):
+        at = pl.ds(pl.multiple_of(i * step, step), step)
+        x = x0[at, :].astype(f32) + attn[at, :].astype(f32)
+        n2[at, :] = rms_scale(x, gain[...]).astype(bf16)
+        return carry
+
+    lax.fori_loop(0, rows // step, normalize, 0)
+    lane = lax.broadcasted_iota(jnp.int32, (rows, 128), 1)
+    gates = masked_gates(dot(n2[...], router[...]), hot[...])
+    z_gu[...] = by_seq(n2[...], lambda s, v: dot(v, wide[:, 128 * s : 128 * s + 128])).astype(bf16)
+    dz_d[...] = by_seq(dy[...], lambda s, v: dot(v, wide[:, 256 + 128 * s : 384 + 128 * s])).astype(bf16)
+    g_gu[...] = jnp.zeros_like(g_gu)
+    g_d[...] = jnp.zeros_like(g_d)
+    zero = jnp.zeros((rows, 128), f32)
+
+    def expert(e, carry):
+        d_gates, dz_gu, z_d = carry
+        for c in fetch(e):
+            c.wait()
+        gate = column_of(gates, lane, e)
+        z_in = jnp.where(lane // 32 == e, z_gu[...].astype(f32), 0.0).astype(bf16)
+        dz_in = jnp.where(lane // 16 == 4 + e, dz_d[...].astype(f32), 0.0).astype(bf16)
+        dh_tmp[:, :704] = dot_nt(dy[...], w_d[e]) + by_seq(dz_in, lambda s, v: dot(v, a_d[s]))
+        pre = dot(n2[...], w_gu[e]) + by_seq(z_in, lambda s, v: dot(v, b_gu[s]))
+
+        def tile(g, u, d):
+            sg = jax.nn.sigmoid(g)
+            silu = g * sg
+            h = silu * u
+            dg = d * gate
+            return h, (dg * u * sg * (1.0 + g * (1.0 - sg))), dg * silu, h * d
+
+        h, dgp, dup, hd = tile(pre[:, :640], pre[:, 640:1280], dh_tmp[:, :640])
+        hg[e, :, :640] = (h * gate).astype(bf16)
+        dgu[e, :, :640] = dgp.astype(bf16)
+        dgu[e, :, 640:1280] = dup.astype(bf16)
+        dgf = jnp.sum(hd, axis=1, keepdims=True)
+        last = pre[:, 1280:]
+        h, dgp, dup, hd = tile(last, pltpu.roll(last, 64, 1), dh_tmp[:, 640:])
+        hg[e, :, 640:] = (h * gate).astype(bf16)[:, :64]
+        dgu[e, :, 1280:] = jnp.where(lane < 64, dgp, pltpu.roll(dup, 64, 1)).astype(bf16)
+        dgf = dgf + jnp.sum(jnp.where(lane < 64, hd, 0.0), axis=1, keepdims=True)
+        d_gates = d_gates + jnp.where(lane == e, dgf, 0.0)
+        back = by_seq(dgu[e], lambda s, v: dot_nt(v, b_gu[s]))
+        dz_gu = dz_gu + jnp.where(lane // 32 == e, back, 0.0)
+        low = by_seq(hg[e], lambda s, v: dot_nt(v, a_d[s]))
+        z_d = z_d + jnp.where(lane // 16 == 4 + e, low, 0.0)
+        half = rows // 2
+        for s in range(2):
+            at = slice(s * half, s * half + half)
+            g_gu[s] += dot_tn(z_in[at], dgu[e, at, :])
+            g_d[s] += dot_tn(dz_in[at], hg[e, at, :])
+        return d_gates, dz_gu, z_d
+
+    d_gates, dz_gu, z_d = lax.fori_loop(0, experts, expert, (zero, zero, zero))
+    d_logits = gates * (d_gates - jnp.sum(gates * d_gates, axis=1, keepdims=True))
+    d_logits = d_logits.astype(bf16)
+    dz_gu, z_d = dz_gu.astype(bf16), z_d.astype(bf16)
+    z_part[:, :128] = dz_gu
+    z_part[:, 128:] = z_o[...] + z_d
+
+    def scatter(i, d):
+        return pltpu.make_async_remote_copy(
+            src_ref=parts.at[i, d],
+            dst_ref=held.at[i, d],
+            send_sem=send.at[i, d],
+            recv_sem=recv.at[i, d],
+            device_id=(me, tp ^ d),
+            device_id_type=MESH,
+        )
+
+    def piece(j, carry):
+        d = lax.rem(j, N_TP)
+        peer = tp ^ d
+        at = pl.ds(pl.multiple_of(peer * part, part), part)
+        w_rows = wide[at, :]
+        dn = dot_nt(d_logits, router[at, :])
+        dn = dn + by_seq(dz_gu, lambda s, v: dot_nt(v, w_rows[:, 128 * s : 128 * s + 128]))
+        ff = by_seq(z_d, lambda s, v: dot_nt(v, w_rows[:, 256 + 128 * s : 384 + 128 * s]))
+        for e in range(experts):
+            dn = dn + dot_nt(dgu[e], w_gu[e, at, :])
+            ff = ff + dot(hg[e], w_d[e, :, at])
+
+        @pl.when(j < N_TP)
+        def _():
+            parts[0, d] = dn.astype(bf16)
+            parts[1, d] = ff.astype(bf16)
+            scatter(0, d).start()
+            scatter(1, d).start()
+
+        @pl.when(j == N_TP)
+        def _():
+            own[0] = dn
+            own[1] = ff
+
+        return carry
+
+    z_rows = rows // N_TP
+
+    def z_region(ref, rank):
+        return ref.at[pl.ds(pl.multiple_of(rank * z_rows, z_rows), z_rows), :]
+
+    def z_scatter(d):
+        return pltpu.make_async_remote_copy(
+            src_ref=z_region(z_part, tp ^ d),
+            dst_ref=z_held.at[d],
+            send_sem=send.at[2, d],
+            recv_sem=recv.at[2, d],
+            device_id=(me, tp ^ d),
+            device_id_type=MESH,
+        )
+
+    def z_spread(d, rank):
+        return pltpu.make_async_remote_copy(
+            src_ref=z_region(z_sum, rank),
+            dst_ref=z_region(z_sum, rank),
+            send_sem=send.at[3, d],
+            recv_sem=recv.at[3, d],
+            device_id=(me, tp ^ d),
+            device_id_type=MESH,
+        )
+
+    def columns(ref, rank):
+        return ref.at[:, pl.ds(pl.multiple_of(rank * part, part), part)]
+
+    def spread(d, rank):
+        return pltpu.make_async_remote_copy(
+            src_ref=columns(dx1, rank),
+            dst_ref=columns(dx1, rank),
+            send_sem=send.at[4, d],
+            recv_sem=recv.at[4, d],
+            device_id=(me, tp ^ d),
+            device_id_type=MESH,
+        )
+
+    def tail(d, rank):
+        return pltpu.make_async_remote_copy(
+            src_ref=tails.at[rank],
+            dst_ref=tails.at[rank],
+            send_sem=send.at[5, d],
+            recv_sem=recv.at[5, d],
+            device_id=(me, tp ^ d),
+            device_id_type=MESH,
+        )
+
+    def x_own():
+        return x0[:, at].astype(f32) + attn[:, at].astype(f32)
+
+    lax.fori_loop(1, N_TP + 1, piece, 0)
+    for d in range(1, N_TP):
+        z_scatter(d).start()
+    total = own[0]
+    for d in range(1, N_TP):
+        scatter(0, d).wait_recv()
+        total = total + held[0, d].astype(f32)
+    at = pl.ds(pl.multiple_of(tp * part, part), part)
+    total = total * gain[:, at]
+    own[0] = total
+    columns(dx1, tp)[...] = total.astype(bf16)
+    for d in range(1, N_TP):
+        spread(d, tp).start()
+    dots[...] = jnp.broadcast_to(jnp.sum(total * x_own(), axis=1, keepdims=True), dots.shape)
+    tails[tp] = jnp.transpose(dots[...])[:8, :]
+    for d in range(1, N_TP):
+        tail(d, tp).start()
+    total = own[1] + x_own()
+    for d in range(1, N_TP):
+        scatter(1, d).wait_recv()
+        total = total + held[1, d].astype(f32)
+    mixed[...] = total.astype(bf16)
+    total = z_region(z_part, tp)[...].astype(f32)
+    for d in range(1, N_TP):
+        z_scatter(d).wait_recv()
+        total = total + z_held[d].astype(f32)
+    z_region(z_sum, tp)[...] = total.astype(bf16)
+    for d in range(1, N_TP):
+        z_spread(d, tp).start()
+    for d in range(1, N_TP):
+        tail(d, tp ^ d).wait_recv()
+    whole = tails[0]
+    for d in range(1, N_TP):
+        whole = whole + tails[d]
+    dots[...] = jnp.transpose(jnp.broadcast_to(whole[:1], (128, rows)))
+    for d in range(1, N_TP):
+        spread(d, tp ^ d).wait_recv()
+        spread(d, tp).wait_send()
+
+    def back(i, carry):
+        rows_at = pl.ds(pl.multiple_of(i * step, step), step)
+        x = x0[rows_at, :].astype(f32) + attn[rows_at, :].astype(f32)
+        inverse = lax.rsqrt(jnp.mean(x * x, axis=1, keepdims=True) + eps)
+        mean = dots[rows_at, :1] * (1.0 / model)
+        got = dy[rows_at, :].astype(f32) + inverse * dx1[rows_at, :].astype(f32) - x * inverse**3 * mean
+        dx1[rows_at, :] = got.astype(bf16)
+        dx1_own[rows_at, :] = (
+            dy[rows_at, at].astype(f32) + inverse * own[0, rows_at, :]
+            - (x0[rows_at, at].astype(f32) + attn[rows_at, at].astype(f32)) * inverse**3 * mean
+        )
+        return carry
+
+    lax.fori_loop(0, rows // step, back, 0)
+    for d in range(1, N_TP):
+        scatter(0, d).wait_send()
+        scatter(1, d).wait_send()
+        z_scatter(d).wait_send()
+        z_spread(d, tp ^ d).wait_recv()
+        z_spread(d, tp).wait_send()
+        tail(d, tp).wait_send()
+
+
+def feed_forward(x0, attn, dy, gain, wide, router, hot, b_gu, a_d, z_o, w_gu, w_d):
+    rows, model = x0.shape
+    part = model // N_TP
+    experts, _, cols = w_gu.shape
+    hidden = w_d.shape[1]
+    shape = jax.ShapeDtypeStruct
+    return pl.pallas_call(
+        ffn_kernel,
+        out_shape=(
+            shape((rows, part), bf16),
+            shape((rows, model), bf16),
+            shape((rows, part), f32),
+            shape((rows, model), bf16),
+            shape((rows, 256), bf16),
+            shape(b_gu.shape, f32),
+            shape(a_d.shape, f32),
+        ),
+        in_specs=[VMEM] * 10 + [ANY] * 2,
+        out_specs=tuple([VMEM] * 7),
+        scratch_shapes=[
+            pltpu.VMEM(w_gu.shape, bf16),
+            pltpu.VMEM(w_d.shape, bf16),
+            pltpu.VMEM((experts, rows, hidden), bf16),
+            pltpu.VMEM((experts, rows, cols), bf16),
+            pltpu.VMEM((rows, 768), f32),
+            pltpu.VMEM((rows, 128), bf16),
+            pltpu.VMEM((rows, 128), bf16),
+            pltpu.VMEM((rows, 256), bf16),
+            pltpu.VMEM((2, N_TP, rows, part), bf16),
+            pltpu.VMEM((2, rows, part), f32),
+            pltpu.VMEM((2, N_TP, rows, part), bf16),
+            pltpu.VMEM((N_TP, rows // N_TP, 256), bf16),
+            pltpu.VMEM((rows, 128), f32),
+            pltpu.VMEM((N_TP, 8, rows), f32),
+            pltpu.SemaphoreType.DMA((2, experts)),
+            pltpu.SemaphoreType.DMA((6, N_TP)),
+            pltpu.SemaphoreType.DMA((6, N_TP)),
+        ],
+        compiler_params=pltpu.CompilerParams(
+            collective_id=2, has_side_effects=True, vmem_limit_bytes=62 << 20
+        ),
+        name="feed_forward",
+    )(x0, attn, dy, gain, wide, router, hot, b_gu, a_d, z_o, w_gu, w_d)
+
+
+def widen_routes(routes, experts):
+    lane = jnp.arange(128, dtype=jnp.int32)
+    return jnp.sum((routes[..., None] == lane).astype(f32), axis=1)
+
+
+def gate_up_columns(gate, up):
+    return jnp.concatenate([gate[..., :640], up[..., :640], gate[..., 640:], up[..., 640:]], axis=-1)
+
+
+def attention_kernel(
+    s_q, s_kv, s_o, s_gu, s_d, tokens, cotangent, s_wide,
+    gain, router, hot0, hot1, cosine, sine, q_doc, k_doc, b_q, b_kv, a_o,
+    g_q, g_kv, g_o, g_gu, g_d, g_wide, wide_mid, dy,
+    x0, attn, n1, kv_all, q_all, probs, ob, z_o, z_q, z_kv, gates,
+    w_q, w_kv, w_o, wide, parts, own, held,
+    send, recv, local, tp_send, tp_recv, tp_local, kv_send, kv_recv, load, sum_send, sum_recv,
+):
+    me, tp = lax.axis_index("ctx"), lax.axis_index("tp")
+    core, side = me ^ 1, me ^ 2
+    up, down, far = lax.rem(me + 4, 16), lax.rem(me + 12, 16), lax.rem(me + 8, 16)
+    on_core, on_side = lax.rem(me, 2), lax.rem(me // 2, 2)
+    rows, model = x0.shape
+    part = model // N_TP
+    half = rows // 2
+    experts = w_q.shape[0]
+    width = w_q.shape[2]
+    heads = width // HEAD_DIM
+    span = (PAST + 1) * half
+    greet([(d, tp) for d in (core, side, up, down, far)] + [(me, tp ^ d) for d in range(1, N_TP)])
+
+    kinds = ["flat", "flat", "rows", "cols", "rows", "cols"]
+    src = [s_kv, wide_mid, s_q, s_o, s_gu, s_d]
+    dst = [g_kv, g_wide, g_q, g_o, g_gu, g_d]
+    tp_src, tp_dst, tp_kinds = [tokens, s_wide, cotangent], [x0, wide_mid, dy], ["cols", "rows", "cols"]
+    started, staying = [], []
+    counter = [0] * len(kinds)
+
+    def tp_copy(i, d, rank):
+        size = tp_src[i].shape[1 if tp_kinds[i] == "cols" else 0]
+        return pltpu.make_async_remote_copy(
+            src_ref=tp_src[i],
+            dst_ref=tp_part(tp_kinds[i], tp_dst[i], rank, size),
+            send_sem=tp_send.at[i, d],
+            recv_sem=tp_recv.at[i, d],
+            device_id=(me, tp ^ d),
+            device_id_type=MESH,
+        )
+
+    def tp_own(i):
+        size = tp_src[i].shape[1 if tp_kinds[i] == "cols" else 0]
+        return pltpu.make_async_copy(
+            tp_src[i], tp_part(tp_kinds[i], tp_dst[i], tp, size), tp_local.at[i]
+        )
+
+    def tp_wait(i):
+        for d in range(1, N_TP):
+            tp_copy(i, d, tp ^ d).wait_recv()
+        tp_own(i).wait()
+
+    def copy(t, item, owner, low, high, to, slot, own_shard):
+        there = region(kinds[t], dst[t], owner, low, high)
+        return pltpu.make_async_remote_copy(
+            src_ref=own_part(kinds[t], src[t], low, high) if own_shard else there,
+            dst_ref=there,
+            send_sem=send.at[t, slot],
+            recv_sem=recv.at[t, item],
+            device_id=(to, tp),
+            device_id_type=MESH,
+        )
+
+    def go(t, item, owner, low, high, to, own_shard=False):
+        c = copy(t, item, owner, low, high, to, counter[t], own_shard)
+        counter[t] += 1
+        c.start()
+        started.append(c)
+
+    arrive = {
+        0: (side, 0, 4),
+        1: (down, 0, 4),
+        2: (up, 0, 4),
+        3: (down ^ 2, 0, 2),
+        4: (up ^ 2, 0, 2),
+        5: (far, 1, 3),
+        6: (far, 0, 1),
+        7: (far, 3, 4),
+        8: (far ^ 2, 1, 2),
+        9: (far ^ 2, 0, 1),
+        10: (down ^ 2, 2, 4),
+        11: (up ^ 2, 2, 4),
+        12: (far ^ 2, 2, 4),
+    }
+
+    def got(t, item):
+        owner, low, high = arrive[item]
+        copy(t, item, owner, low, high, core, 0, False).wait_recv()
+        go(t, 13 + item, owner, low, high, core)
+
+    def first(t):
+        go(t, 0, me, 0, 4, side, True)
+        go(t, 2, me, 0, 4, down, True)
+        go(t, 1, me, 0, 4, up, True)
+        go(t, 26, me, 0, 4, core, True)
+        c = pltpu.make_async_copy(src[t], region(kinds[t], dst[t], me, 0, 4), local.at[t])
+        c.start()
+        staying.append(c)
+
+    def second(t):
+        got(t, 0)
+        go(t, 3, side, 0, 2, up)
+        go(t, 4, side, 0, 2, down)
+        got(t, 1)
+        go(t, 5, down, 1, 3, up)
+        go(t, 10, down, 2, 4, side)
+        got(t, 2)
+        go(t, 6, up, 0, 1, down)
+        go(t, 7, up, 3, 4, down)
+        go(t, 11, up, 2, 4, side)
+
+    def third(t):
+        got(t, 3)
+        go(t, 8, down ^ 2, 1, 2, up)
+        got(t, 4)
+        go(t, 9, up ^ 2, 0, 1, down)
+        got(t, 5)
+        got(t, 6)
+        got(t, 7)
+        go(t, 12, far, 2, 4, side)
+
+    def fourth(t):
+        for item in range(8, 13):
+            got(t, item)
+
+    def finish(t):
+        for item in range(13):
+            owner, low, high = arrive[item]
+            copy(t, 13 + item, owner ^ 1, low, high, core, 0, False).wait_recv()
+        copy(t, 26, core, 0, 4, core, 0, False).wait_recv()
+
+    for i in range(3):
+        for d in range(1, N_TP):
+            c = tp_copy(i, d, tp)
+            c.start()
+            started.append(c)
+        tp_own(i).start()
+    for t in (0, 2, 3):
+        first(t)
+    tp_wait(1)
+    first(1)
+    tp_wait(0)
+    step = 32
+
+    def normalize(i, carry):
+        at = pl.ds(pl.multiple_of(i * step, step), step)
+        n1[at, :] = rms_scale(x0[at, :].astype(f32), gain[...]).astype(bf16)
+        return carry
+
+    lax.fori_loop(0, rows // step, normalize, 0)
+    gates[...] = masked_gates(dot(n1[...], router[...]), hot0[...] + hot1[...])
+    for t in (0, 2, 1, 3):
+        second(t)
+    for t in (0, 2, 1, 3):
+        third(t)
+    first(4)
+    first(5)
+    for t in (0, 2, 1, 3):
+        fourth(t)
+
+    for c in staying[:4]:
+        c.wait()
+    fetches = []
+    for i, (t, ref) in enumerate([(0, w_kv), (1, wide), (2, w_q), (3, w_o)]):
+        finish(t)
+        c = pltpu.make_async_copy(dst[t], ref, load.at[i])
+        c.start()
+        fetches.append(c)
+
+    lane = lax.broadcasted_iota(jnp.int32, (rows, 128), 1)
+    seq = lax.broadcasted_iota(jnp.int32, (rows, 128), 0) // half
+
+    def rotary(x):
+        return x * cosine[...] + pltpu.roll(x, HEAD_DIM // 2, 1) * sine[...]
+
+    fetches[0].wait()
+    fetches[1].wait()
+    z = dot(n1[...], wide[:, 512:640])
+    z_q[...] = jnp.where(lane // 64 == seq, z, 0.0).astype(bf16)
+    z = dot(n1[...], wide[:, 640:704])
+    z_kv[...] = jnp.where((lane // 16) % 2 == seq, jnp.pad(z, ((0, 0), (0, 64))), 0.0).astype(bf16)
+    kv = dot(n1[...], w_kv[...]) + dot(z_kv[:, :64], b_kv[...])
+    for h in range(heads):
+        at = slice(HEAD_DIM * h, HEAD_DIM * h + HEAD_DIM)
+        turned = rotary(kv[:, at]).astype(bf16)
+        kv_all[PAST, 0, :, at] = turned[:half]
+        kv_all[PAST, 1, :, at] = turned[half:]
+    for s in range(2):
+        kv_all[PAST, s, :, width:] = kv[half * s : half * s + half, width:].astype(bf16)
+
+    def kv_copy(slot, back, to, to_back):
+        return pltpu.make_async_remote_copy(
+            src_ref=kv_all.at[PAST - back],
+            dst_ref=kv_all.at[PAST - to_back],
+            send_sem=kv_send.at[slot],
+            recv_sem=kv_recv.at[to_back],
+            device_id=(to, tp),
+            device_id_type=MESH,
+        )
+
+    def kv_arrived(back):
+        kv_copy(0, back, core, back).wait_recv()
+
+    def when(condition, c):
+        if condition is None:
+            c.start()
+        else:
+            pl.when(condition)(c.start)
+        kv_started.append((condition, c))
+
+    kv_started = []
+    when(None, kv_copy(0, 0, up, 4))
+    when(None, kv_copy(1, 0, far, 8))
+    when(on_side == 0, kv_copy(2, 0, side, 2))
+    when(on_core == 0, kv_copy(3, 0, core, 1))
+
+    fetches[2].wait()
+    queries = [jnp.zeros((rows, width), f32), jnp.zeros((rows, width), f32)]
+    for e in range(experts):
+        z_e = jnp.where((lane % 64) // 16 == e, z_q[...].astype(f32), 0.0).astype(bf16)
+        q_e = dot(n1[...], w_q[e]) + dot(z_e, b_q[...])
+        for k, hot in enumerate((hot0, hot1)):
+            queries[k] = queries[k] + jnp.where(hot[:, e : e + 1] > 0, q_e, 0.0)
+    for k in range(2):
+        for h in range(heads):
+            turned = rotary(queries[k][:, HEAD_DIM * h : HEAD_DIM * h + HEAD_DIM]).astype(bf16)
+            for s in range(2):
+                q_all[s * heads + h, k * half : k * half + half, :] = turned[half * s : half * s + half]
+
+    kv_arrived(4)
+    when(on_side == 0, kv_copy(4, 4, side, 6))
+    when(on_side == 1, kv_copy(5, 4, side, 2))
+    when(on_core == 0, kv_copy(6, 4, core, 5))
+    when(on_core == 1, kv_copy(7, 4, core, 3))
+    kv_arrived(8)
+    when(on_side == 1, kv_copy(8, 8, side, 6))
+    when(on_core == 1, kv_copy(9, 8, core, 7))
+    kv_arrived(2)
+    when(on_core == 0, kv_copy(10, 2, core, 3))
+    when(on_core == 1, kv_copy(11, 2, core, 1))
+    kv_arrived(6)
+    when(on_core == 0, kv_copy(12, 6, core, 7))
+    when(on_core == 1, kv_copy(13, 6, core, 5))
+    for back in (1, 3, 5, 7):
+        kv_arrived(back)
+
+    row = lax.broadcasted_iota(jnp.int32, (half, span), 0)
+    key = lax.broadcasted_iota(jnp.int32, (half, span), 1)
+    near = (key > row) & (key <= row + PAST * half)
+
+    def attend(i, carry):
+        s = i // heads
+        h = lax.rem(i, heads)
+        at = pl.ds(pl.multiple_of(h * HEAD_DIM, HEAD_DIM), HEAD_DIM)
+        v_at = pl.ds(pl.multiple_of(width + h * HEAD_DIM, HEAD_DIM), HEAD_DIM)
+        keys = kv_all[:, s, :, at].reshape(span, HEAD_DIM)
+        values = kv_all[:, s, :, v_at].reshape(span, HEAD_DIM)
+        seq_rows = pl.ds(pl.multiple_of(s * half, half), half)
+        allowed = near & (q_doc[seq_rows, :1] == k_doc[s, :1, :])
+        for k in range(2):
+            q = q_all[i, k * half : k * half + half, :]
+            scores = dot_nt(q, keys) * HEAD_DIM**-0.5
+            scores = jnp.where(allowed, scores, big_negative)
+            peak = jnp.max(scores, axis=1, keepdims=True)
+            powers = jnp.exp(scores - peak)
+            p = (powers * (1.0 / jnp.sum(powers, axis=1, keepdims=True))).astype(bf16)
+            probs[i, k * half : k * half + half, :] = p
+            ob[k, seq_rows, at] = dot(p, values).astype(bf16)
+        return carry
+
+    lax.fori_loop(0, 2 * heads, attend, 0)
+    second(4)
+
+    fetches[3].wait()
+    z_acc = jnp.zeros((rows, 128), f32)
+    chosen = []
+    for e in range(experts):
+        o_e = jnp.where(hot0[:, e : e + 1] > 0, ob[0].astype(f32), 0.0)
+        o_e = o_e + jnp.where(hot1[:, e : e + 1] > 0, ob[1].astype(f32), 0.0)
+        o_e = o_e.astype(bf16)
+        chosen.append(o_e)
+        low = by_seq(o_e, lambda s, v: dot_nt(v, a_o[s]))
+        z_acc = z_acc + jnp.where(lane // 16 == e, low * gates[:, e : e + 1], 0.0)
+    z_o[...] = z_acc.astype(bf16)
+
+    def columns(ref, rank):
+        return ref.at[:, pl.ds(pl.multiple_of(rank * part, part), part)]
+
+    def scatter(d):
+        return pltpu.make_async_remote_copy(
+            src_ref=parts.at[d],
+            dst_ref=held.at[d],
+            send_sem=sum_send.at[0, d],
+            recv_sem=sum_recv.at[0, d],
+            device_id=(me, tp ^ d),
+            device_id_type=MESH,
+        )
+
+    def spread(d, rank):
+        return pltpu.make_async_remote_copy(
+            src_ref=columns(attn, rank),
+            dst_ref=columns(attn, rank),
+            send_sem=sum_send.at[1, d],
+            recv_sem=sum_recv.at[1, d],
+            device_id=(me, tp ^ d),
+            device_id_type=MESH,
+        )
+
+    for j in range(1, N_TP + 1):
+        d = j % N_TP
+        at = pl.ds(pl.multiple_of((tp ^ d) * part, part), part)
+        w_rows = wide[at, 256:512]
+        total = by_seq(z_o[...], lambda s, v: dot_nt(v, w_rows[:, 128 * s : 128 * s + 128]))
+        for e in range(experts):
+            total = total + dot(chosen[e], w_o[e, :, at]) * gates[:, e : e + 1]
+        if d:
+            parts[d] = total.astype(bf16)
+            scatter(d).start()
+        else:
+            own[...] = total
+    second(5)
+    total = own[...]
+    for d in range(1, N_TP):
+        scatter(d).wait_recv()
+        total = total + held[d].astype(f32)
+    columns(attn, tp)[...] = total.astype(bf16)
+    for d in range(1, N_TP):
+        spread(d, tp).start()
+    third(4)
+    third(5)
+    for d in range(1, N_TP):
+        spread(d, tp ^ d).wait_recv()
+    fourth(4)
+    fourth(5)
+    tp_wait(2)
+    for t in (4, 5):
+        finish(t)
+    for c in started:
+        c.wait_send()
+    for c in staying[4:]:
+        c.wait()
+    for condition, c in kv_started:
+        if condition is None:
+            c.wait_send()
+        else:
+            pl.when(condition)(c.wait_send)
+    for d in range(1, N_TP):
+        scatter(d).wait_send()
+        spread(d, tp).wait_send()
+
+
+def attention(shards_in, tp_shards, small):
+    s_q, s_kv, s_o, s_gu, s_d = shards_in
+    tokens, cotangent, s_wide = tp_shards
+    rows, part = tokens.shape
+    model = part * N_TP
+    experts, _, width = s_q.shape
+    half = rows // 2
+    heads = width // HEAD_DIM
+    shape = jax.ShapeDtypeStruct
+
+    def grown(a, d):
+        return shape(tuple(n * (N_CTX if i == d else 1) for i, n in enumerate(a.shape)), a.dtype)
+
+    gathered = (grown(s_q, 1), grown(s_kv, 0), grown(s_o, 2), grown(s_gu, 1), grown(s_d, 2))
+    wide_mid = shape((s_wide.shape[0] * N_TP, s_wide.shape[1]), bf16)
+    wide = grown(wide_mid, 0)
+    vmem_out = (
+        shape((rows, model), bf16),
+        shape((rows, model), bf16),
+        shape((rows, model), bf16),
+        shape((PAST + 1, 2, half, 2 * width), bf16),
+        shape((2 * heads, rows, HEAD_DIM), bf16),
+        shape((2 * heads, rows, (PAST + 1) * half), bf16),
+        shape((2, rows, width), bf16),
+        shape((rows, 128), bf16),
+        shape((rows, 128), bf16),
+        shape((rows, 128), bf16),
+        shape((rows, 128), f32),
+    )
+    any_out = gathered + (wide, wide_mid, shape((rows, model), bf16))
+    return pl.pallas_call(
+        attention_kernel,
+        out_shape=any_out + vmem_out,
+        in_specs=[ANY] * 8 + [VMEM] * len(small),
+        out_specs=tuple([ANY] * len(any_out) + [VMEM] * len(vmem_out)),
+        scratch_shapes=[
+            pltpu.VMEM(gathered[0].shape, bf16),
+            pltpu.VMEM(gathered[1].shape, bf16),
+            pltpu.VMEM(gathered[2].shape, bf16),
+            pltpu.VMEM(wide.shape, bf16),
+            pltpu.VMEM((N_TP, rows, part), bf16),
+            pltpu.VMEM((rows, part), f32),
+            pltpu.VMEM((N_TP, rows, part), bf16),
+            pltpu.SemaphoreType.DMA((6, 32)),
+            pltpu.SemaphoreType.DMA((6, 27)),
+            pltpu.SemaphoreType.DMA((6,)),
+            pltpu.SemaphoreType.DMA((3, N_TP)),
+            pltpu.SemaphoreType.DMA((3, N_TP)),
+            pltpu.SemaphoreType.DMA((3,)),
+            pltpu.SemaphoreType.DMA((14,)),
+            pltpu.SemaphoreType.DMA((PAST + 1,)),
+            pltpu.SemaphoreType.DMA((4,)),
+            pltpu.SemaphoreType.DMA((2, N_TP)),
+            pltpu.SemaphoreType.DMA((2, N_TP)),
+        ],
+        compiler_params=pltpu.CompilerParams(
+            collective_id=0, has_side_effects=True, vmem_limit_bytes=60 << 20
+        ),
+        name="attention",
+    )(*shards_in, *tp_shards, *small)
+
+
 def shards(
     tokens,
     norm1_gain,
@@ -551,31 +1281,18 @@
         return a.reshape((rows,) + a.shape[2:])
 
     wide_own = adapt_wide.astype(bf16)[adapter_index]
-    wide_cols = wide_own.reshape(seqs * wide_slots * rank, -1).T
+    groups = [[6, 10, 7, 11, 8, 12, 9, 13], list(range(14, 22)), [0, 1, 2, 3], [4, 5]]
+    order = [(q, s) for g in groups[:3] for q in range(seqs) for s in g]
+    order += [(q, s) for s in groups[3] for q in range(seqs)]
+    wide_cols = wide_own.reshape(seqs * wide_slots, rank, -1)[
+        np.array([q * wide_slots + s for q, s in order])
+    ].reshape(seqs * wide_slots * rank, -1).T
     heads_low = adapt_heads.astype(bf16)[adapter_index]
     ffn_low = adapt_ffn.astype(bf16)[adapter_index]
-    (w_query, w_key_value, w_out, w_gate_up, w_down, wide), (x0, dy) = gather_all(
-        [
-            w_query,
-            w_key_value.reshape(-1, 2 * width),
-            w_out,
-            w_gate_up.reshape(experts, -1, 2 * hidden),
-            w_down,
-        ],
-        ["rows", "flat", "cols", "rows", "cols", "flat"],
-        [tokens.reshape(rows, part), cotangent.reshape(rows, part), wide_cols],
-        ["cols", "cols", "rows"],
-    )
-    w_gate_up = w_gate_up.reshape(experts, model, 2, hidden)
-    wide = wide.reshape(model, seqs, wide_slots, rank)
-    xf = x0.astype(f32)
-    n1 = rms_scale(xf, norm1_gain).astype(bf16)
     route_a = attention_routes.reshape(rows, -1)
     route_f = feedforward_routes.reshape(rows, -1)
     hot_a = jax.nn.one_hot(route_a, experts, dtype=f32)
     hot_f = jax.nn.one_hot(route_f, experts, dtype=f32)
-    ga = gates_of(dot(n1, router_attn), hot_a)
-    ga_e = jnp.sum(ga[..., None] * hot_a, axis=1)
 
     positions = ctx_rank * block + jnp.arange(block, dtype=jnp.int32)
     doc_ids, offsets = doc_layout(doc_lengths, positions)
@@ -612,101 +1329,83 @@
             "sbcr,sbch->scrh", split(z).astype(bf16), split(dp), preferred_element_type=f32
         )
 
-    z_q = low_in(n1, 0, experts)
-    z_kv = low_in(n1, experts, 2)
     b_q, b_kv, a_o = heads_low[:, :experts], heads_low[:, experts : experts + 2], heads_low[:, experts + 2 :]
-    q_all = jnp.stack([dot(n1, w_query[e]) for e in range(experts)], axis=1) + low_out(z_q, b_q)
-    q_pre = jnp.einsum("rke,reh->rkh", hot_a, q_all, precision=lax.Precision.HIGHEST)
-    q = rope(
-        q_pre.reshape(rows, -1, heads, HEAD_DIM), cosine[:, None, None], sine[:, None, None], 1.0
-    ).astype(bf16)
-    kv = dot(n1, w_key_value.reshape(model, 2 * width)).reshape(rows, 2, width) + low_out(z_kv, b_kv)
-    k_own = rope(
-        kv[:, 0].reshape(rows, heads, HEAD_DIM), cosine[:, None], sine[:, None], 1.0
-    ).astype(bf16)
-    v_own = kv[:, 1].reshape(rows, heads, HEAD_DIM).astype(bf16)
-    kv_own = jnp.concatenate([k_own, v_own], axis=1).reshape(seqs, block, 2 * width)
-    kv_all = halo(kv_own)
-    length = kv_all.shape[1]
-    kv_all = kv_all.reshape(seqs, length, 2, heads, HEAD_DIM)
-    key_pos = (ctx_rank - PAST) * block + jnp.arange(length, dtype=jnp.int32)
+    key_pos = (ctx_rank - PAST) * block + jnp.arange((PAST + 1) * block, dtype=jnp.int32)
     key_doc = doc_layout(doc_lengths, jnp.maximum(key_pos, 0))[0]
-    allowed = (
-        (key_pos >= 0)[None, None, :] &
-        (doc_ids[:, :, None] == key_doc[:, None, :])
-        & (key_pos[None, None, :] <= positions[None, :, None])
-        & (positions[None, :, None] - key_pos[None, None, :] < WINDOW)
-    )[:, None, None]
+    key_doc = jnp.where(key_pos[None, :] >= 0, key_doc, -(1 << 20))
+    blank = jnp.zeros((seqs, rank, width), bf16)
+    b_kv_wide = jnp.concatenate(
+        [
+            jnp.concatenate([b_kv[:, 0], blank], axis=-1).reshape(seqs * rank, 2 * width),
+            jnp.concatenate([blank, b_kv[:, 1]], axis=-1).reshape(seqs * rank, 2 * width),
+        ],
+        axis=0,
+    )
+    a_o_wide = jnp.pad(a_o.reshape(seqs, experts * rank, width), ((0, 0), (0, 64), (0, 0)))
+    router_wide = jnp.pad(router_attn, ((0, 0), (0, 128 - experts)))
+    (
+        w_query, w_key_value, w_out, w_gate_up, w_down, wide, _, dy,
+        x0, sum_out, n1, kv_all, q_all, probs, ob, z_o_gated, z_q, z_kv, gates,
+    ) = attention(
+        [
+            w_query,
+            w_key_value.reshape(-1, 2 * width),
+            w_out,
+            gate_up_columns(w_gate_up[:, :, 0], w_gate_up[:, :, 1]),
+            w_down,
+        ],
+        [tokens.reshape(rows, part), cotangent.reshape(rows, part), wide_cols],
+        [
+            norm1_gain[None],
+            router_wide,
+            widen_routes(route_a[:, :1], experts),
+            widen_routes(route_a[:, 1:], experts),
+            jnp.concatenate([cosine, cosine], axis=1),
+            jnp.concatenate([-sine, sine], axis=1),
+            jnp.broadcast_to(doc_ids.reshape(rows, 1), (rows, 128)),
+            jnp.broadcast_to(key_doc[:, None, :], (seqs, 8, key_doc.shape[1])),
+            b_q.reshape(seqs * experts * rank, width),
+            b_kv_wide,
+            a_o_wide,
+        ],
+    )
+    wide_low = wide
+    place = {qs: rank * i for i, qs in enumerate(order)}
+    wide = jnp.stack([jnp.stack([wide[:, place[q, s] : place[q, s] + rank] for s in range(wide_slots)], axis=1) for q in range(seqs)], axis=1)
+    ga_e = gates[:, :experts]
+    ga = jnp.sum(ga_e[:, None, :] * hot_a, axis=-1)
     scale = HEAD_DIM ** (-0.5)
-    q_s = q.reshape(seqs, block, -1, heads, HEAD_DIM)
-    scores = jnp.einsum("sqthd,skhd->sthqk", q_s, kv_all[:, :, 0], preferred_element_type=f32) * scale
-    scores = jnp.where(allowed, scores, big_negative)
-    peak = jnp.max(scores, axis=-1, keepdims=True)
-    weights = jnp.where(allowed, jnp.exp(scores - peak), 0.0)
-    total = jnp.sum(weights, axis=-1, keepdims=True)
-    probs = weights / total
-    o = jnp.einsum(
-        "sthqk,skhd->sqthd", probs.astype(bf16), kv_all[:, :, 1], preferred_element_type=f32
+    length = (PAST + 1) * block
+    kv_all = jnp.swapaxes(kv_all, 0, 1).reshape(seqs, length, 2, heads, HEAD_DIM)
+    probs = jnp.swapaxes(probs.reshape(seqs, heads, 2, block, length), 1, 2).astype(f32)
+    q_s = jnp.transpose(q_all.reshape(seqs, heads, 2, block, HEAD_DIM), (0, 3, 2, 1, 4))
+    ob = jnp.swapaxes(ob, 0, 1)
+    o = ob.reshape(seqs, block, 2, heads, HEAD_DIM).astype(f32)
+    ob_e = jnp.einsum("rke,rkh->reh", hot_a.astype(bf16), ob, preferred_element_type=f32).astype(bf16)
+    xf = x0.astype(f32)
+    z_q = jnp.where(jnp.arange(rows)[:, None] < block, z_q[:, :64], z_q[:, 64:]).reshape(rows, experts, rank).astype(f32)
+    z_kv = z_kv[:, :64].reshape(rows, 2, 2, rank)
+    z_kv = jnp.where(jnp.arange(rows)[:, None, None] < block, z_kv[:, :, 0], z_kv[:, :, 1]).astype(f32)
+    blank = jnp.zeros((seqs, experts, rank, hidden), bf16)
+    b_gu = jnp.stack(
+        [gate_up_columns(ffn_low[:, :experts], blank), gate_up_columns(blank, ffn_low[:, experts : 2 * experts])],
+        axis=2,
+    ).reshape(seqs, 2 * experts * rank, 2 * hidden)
+    a_d = jnp.pad(ffn_low[:, 2 * experts :].reshape(seqs, experts * rank, hidden), ((0, 0), (64, 0), (0, 0)))
+    mixed, dx1b, dx1_own, n2, z_sum, g_gu, g_d = feed_forward(
+        x0, sum_out, dy, norm2_gain[None], wide_low,
+        jnp.pad(router_ffn, ((0, 0), (0, 128 - experts))),
+        widen_routes(route_f, experts), b_gu, a_d, z_o_gated, w_gate_up, w_down,
     )
-    ob = o.astype(bf16).reshape(rows, -1, width)
-    ob_e = jnp.einsum("rke,rkh->reh", hot_a.astype(bf16), ob, preferred_element_type=f32).astype(bf16)
-    z_o = low_back(ob_e, a_o)
-    b_o = jnp.transpose(wide[:, :, 14:18], (1, 2, 3, 0))
-    part_out = sum(ga_e[:, e, None] * dot(ob_e[:, e], w_out[e]) for e in range(experts))
-    part_out = part_out + low_sum(z_o * ga_e[..., None], b_o)
-    (sum_out,) = exchange([part_out.astype(bf16)], ["ar_cols"], 1)
-    sum_out = sum_out.astype(f32)
-    x1 = xf + sum_out
-    n2 = rms_scale(x1, norm2_gain).astype(bf16)
-    gf = gates_of(dot(n2, router_ffn), hot_f)
-    gf_e = jnp.sum(gf[..., None] * hot_f, axis=1)
-    z_gu = low_in(n2, experts + 2, 2 * experts)
-    b_gu, a_d = ffn_low[:, : 2 * experts], ffn_low[:, 2 * experts :]
-    b_d = jnp.transpose(wide[:, :, 18:22], (1, 2, 3, 0))
-    dz_d = low_in(dy, 18, experts)
-    low_gu = low_out(z_gu, b_gu)
-    low_dh = low_out(dz_d, a_d)
-    h_all, dh_gate, dgp_all, dup_all = [], [], [], []
-    for e in range(experts):
-        gp = dot(n2, w_gate_up[e, :, 0]) + low_gu[:, e]
-        up = dot(n2, w_gate_up[e, :, 1]) + low_gu[:, experts + e]
-        sg = jax.nn.sigmoid(gp)
-        silu = gp * sg
-        h = (silu * up).astype(bf16)
-        dh0 = dot(dy, w_down[e], 1, 1) + low_dh[:, e]
-        dh_gate.append(jnp.sum(dh0 * h.astype(f32), axis=1))
-        dh = dh0 * gf_e[:, e, None]
-        dgp_all.append((dh * up * sg * (1.0 + gp * (1.0 - sg))).astype(bf16))
-        dup_all.append((dh * silu).astype(bf16))
-        h_all.append(h)
-    h_all = jnp.stack(h_all, axis=1)
-    d_gu = jnp.stack(dgp_all + dup_all, axis=1)
-    z_d = low_back(h_all, a_d)
-    part_ffn = sum(gf_e[:, e, None] * dot(h_all[:, e], w_down[e]) for e in range(experts))
-    part_ffn = part_ffn + low_sum(z_d * gf_e[..., None], b_d)
-
-    def own(a):
-        return lax.dynamic_slice_in_dim(a, tp_rank * part, part, 1)
-
-    dgf = jnp.sum(jnp.stack(dh_gate, axis=1)[:, None, :] * hot_f, axis=-1)
-    dlf = gates_back(gf, dgf, hot_f)
-    dz_gu = low_back(d_gu, b_gu)
-    a_gu = jnp.transpose(wide[:, :, 6:14], (1, 2, 3, 0))
-    dn2 = sum(
-        dot(d_gu[:, e], w_gate_up[e, :, 0], 1, 1) + dot(d_gu[:, experts + e], w_gate_up[e, :, 1], 1, 1)
-        for e in range(experts)
+    g_gu = g_gu.reshape(seqs, experts, 2, rank, 2 * hidden)
+    grad_ffn = jnp.concatenate(
+        [
+            jnp.concatenate([g_gu[:, :, 0, :, :640], g_gu[:, :, 0, :, 1280:1344]], axis=-1),
+            jnp.concatenate([g_gu[:, :, 1, :, 640:1280], g_gu[:, :, 1, :, 1344:]], axis=-1),
+            g_d[:, 64:].reshape(seqs, experts, rank, hidden),
+        ],
+        axis=1,
     )
-    dn2 = dn2 + low_sum(dz_gu, a_gu) + dot(dlf.astype(bf16), router_ffn, 1, 1)
-    back2 = norm_back(x1, norm2_gain, dn2)
-    z_part = jnp.concatenate([z_o * ga_e[..., None], dz_gu, z_d * gf_e[..., None]], axis=1)
-    z_part = jnp.pad(z_part.reshape(rows, -1).astype(bf16), ((0, 0), (0, 128)))
-    sum_back, mixed_own, z_sum = exchange(
-        [back2.astype(bf16), part_ffn.astype(bf16), z_part], ["ar_cols", "rs_cols", "ar_rows"], 2
-    )
-    z_sum = z_sum[:, :256].reshape(rows, 16, rank)
-    dx1 = dy.astype(f32) + sum_back.astype(f32)
-    mixed = (mixed_own + own(x1)).astype(bf16)
-    dx1b = dx1.astype(bf16)
     dz_o = low_in(dx1b, 14, experts)
     g_e = jnp.stack([dot(dx1b, w_out[e], 1, 1) for e in range(experts)], axis=1) + low_out(dz_o, a_o)
     g_k = jnp.einsum("rke,reh->rkh", hot_a, g_e, precision=lax.Precision.HIGHEST)
@@ -742,12 +1441,9 @@
     dz_part = jnp.pad(dz_qkv.reshape(rows, -1).astype(bf16), ((0, 0), (0, 32)))
     back_own, dz_sum = exchange([back1.astype(bf16), dz_part], ["rs_cols", "ar_rows"], 3)
     dz_sum = dz_sum[:, :96].reshape(rows, 6, rank)
-    grad_tokens = (back_own + own(dx1)).astype(bf16)
+    grad_tokens = (back_own + dx1_own).astype(bf16)
     grad_heads = jnp.concatenate(
         [low_grad(z_q, dq_e), low_grad(z_kv, dkv_p), low_grad(dz_o * ga_e[..., None], ob_e)], axis=1
-    )
-    grad_ffn = jnp.concatenate(
-        [low_grad(z_gu, d_gu), low_grad(dz_d * gf_e[..., None], h_all)], axis=1
     )
     def strided(a):
         return lax.dynamic_slice_in_dim(
@@ -760,9 +1456,9 @@
     wide_terms = jnp.concatenate(
         [
             wide_grad(dz_sum, n1),
-            wide_grad(z_sum[:, 4:12], n2),
-            wide_grad(z_sum[:, :4], dx1b),
-            wide_grad(z_sum[:, 12:], dy),
+            wide_grad(z_sum[:, :128].reshape(rows, experts, 2, rank).swapaxes(1, 2).reshape(rows, 2 * experts, rank), n2),
+            wide_grad(z_sum[:, 128:192].reshape(rows, experts, rank), dx1b),
+            wide_grad(z_sum[:, 192:].reshape(rows, experts, rank), dy),
         ],
         axis=2,
     ).reshape(-1, seqs * wide_slots * rank)

time: 799 us -> 645 us (0.81)
  matrix products: 124 us -> 23.7 us
  other arithmetic: 60 us -> 21.8 us
    pallas_call x3 -> x1, Pallas kernels: 103 us -> 19.5 us  [exchange(): pl.pallas_call(functools.partial(exchange_kernel, kinds), out_shape=tuple...]
    pallas_call x2, Pallas kernels: 250 us -> 327 us  [the longest x1 247 us: attention(): pl.pallas_call(attention_kernel, out_shape=any_out + vmem_out, in_specs=[...]
    dot_general x46 -> x10, matrix products: 73.7 us -> 10.7 us  [dot(): lax.dot_general(a, b, (((ca,), (cb,)), ((), ())), preferred_element_type=...]
    another operation x16 -> x53, local copies, waits for them, and re-layouts: 23.6 us -> 71.7 us  [the longest x49 70.8 us: shards(): jnp.stack([wide[:, place[q, s]:place[q, s] + rank] for s in range(wide_sl...]
    pallas_call x3 -> x4, local copies, waits for them, and re-layouts: 35 us -> 5.13 us  [the longest x2 3.02 us: attention(): pl.pallas_call(attention_kernel, out_shape=any_out + vmem_out, in_specs=[...]
    convert_element_type x11 -> x3, other arithmetic: 19.1 us -> 1.55 us  [the longest x1 0.83 us: widen_routes(): return jnp.sum((routes[..., None] == lane).astype(f32), axis=1)]
    unnamed x308 -> x307, local copies, waits for them, and re-layouts: 32.7 us -> 22.9 us
  transfers between devices with their start and end apart: 1 -> 1, of which waited for: 0 -> 0; matrix products, arithmetic and copies ran while one was open for 16% -> 25% of each run, Pallas kernels for 18% -> 14%
where the time goes in v2:
time: 645 us; the launch traced here: 639 us
  Pallas kernels  419 us (65%)
  local copies, waits for them, and re-layouts  158 us (24%)
  matrix products  23.7 us (4%)
  other arithmetic  21.8 us (3%)
  between operations  16.8 us (3%)
    pallas_call x1, Pallas kernels, attention(): pl.pallas_call(attention_kernel, out_shape=any_out + vmem_out, in_specs=[...  247 us
    pallas_call x1, Pallas kernels, feed_forward(): pl.pallas_call(ffn_kernel, out_shape=(shape((rows, part), bf16), shape((r...  80.5 us
    another operation x49, local copies, waits for them, and re-layouts, shards(): jnp.stack([wide[:, place[q, s]:place[q, s] + rank] for s in range(wide_sl...  70.8 us
    pallas_call x1, Pallas kernels, reduce_ctx(): pl.pallas_call(functools.partial(reduce_kernel, spread_too), out_shape=tu...  43 us
    pallas_call x1, Pallas kernels, halo_back(): pl.pallas_call(halo_back_kernel, out_shape=jax.ShapeDtypeStruct((seqs, bl...  28.7 us
    unnamed x307, local copies, waits for them, and re-layouts  22.9 us
    pallas_call x1, Pallas kernels, exchange(): pl.pallas_call(functools.partial(exchange_kernel, kinds), out_shape=tuple...  19.5 us
  transfers between devices with their start and end apart: 1, of which 0 were waited for; matrix products, arithmetic and copies ran while one was open for 25% of the time, Pallas kernels for 14%

profile of v2, /device:TPU:1, one launch (start us, length us, event | category | flops | bytes accessed | tf_op | source)
XLA Modules:
  0.0 639.1 jit_solution(15847682502367380130)
XLA Ops:
  32.8 2.4 concatenate.64.s_gu
  36.5 247.0 %attention.1 = (bf16[4,2048,256]{2,1,0:T(8,128)(2,1)}, bf16[2048,512]{1,0:T(8,128)(2,1)}, bf16[4,256,2048]{2,1,0:T(8,128)(2,1)}, bf16[4,2048,1408]{2,1,0:T(8,128...) custom-call(bf16[4,128,256]{2,1,0:T(8,128)(2,1)} %s_q.1, ...), custom_call_target="tpu_custom_call" | custom-call | tf_op jit(solution)/shard_map/attention/pallas_call | solution.py:1211
  283.5 80.5 %feed_forward.1 = (bf16[256,256]{1,0:T(8,128)(2,1)}, bf16[256,2048]{1,0:T(8,128)(2,1)}, f32[256,256]{1,0:T(8,128)}, bf16[256,2048]{1,0:T(8,128)(2,1)}, bf16[256,...) custom-call(bf16[256,2048]{1,0:T(8,128)(2,1)} %get-tuple-element.34.x0, ...), custom_call_target="tpu_custom_call" | custom-call | tf_op jit(solution)/shard_map/feed_forward/pallas_call | solution.py:784
  367.7 2.3 slice_bitcast_fusion.38
  369.9 5.0 slice_bitcast_fusion.23
  375.0 5.2 slice_bitcast_fusion.22
  387.6 1.9 copy.474
  397.3 1.9 copy.482
  401.7 1.9 copy.486
  415.2 1.9 copy.497
  425.3 1.9 copy.503
  435.4 1.9 copy.509
  460.0 3.1 multiply_convert_fusion
  465.2 1.9 copy.467
  467.1 2.2 reshape.553
  469.3 3.9 fusion.82
  473.1 2.5 copy.469
  484.0 2.8 copy.581.src
  486.8 28.7 %halo_back.1 = f32[2,128,512]{2,1,0:T(8,128)S(1)} custom-call(bf16[2,1152,512]{2,1,0:T(8,128)(2,1)S(1)} %copy.581.src), custom_call_target="tpu_custom_call" | custom-call | tf_op jit(solution)/shard_map/halo_back/pallas_call | solution.py:379
  525.5 2.5 copy.551
  548.6 19.5 %exchange_3.1 = (f32[256,256]{1,0:T(8,128)S(1)}, bf16[256,128]{1,0:T(8,128)(2,1)S(1)}) custom-call(bf16[256,2048]{1,0:T(8,128)(2,1)S(1)} %fusion.12.refs_0_, bf16[256,128]{1,0:T(8,128)(2,1)S(1)} %pad.29.refs_1_), custom_call_target="tpu_custom_call" | custom-call | tf_op jit(solution)/shard_map/exchange_3/pallas_call | solution.py:285
  573.9 3.0 convert_element_type.216
  577.0 3.8 copy.563.refs_0_
  580.8 43.0 %reduce_ctx.1 = (f32[16,704]{1,0:T(8,128)S(1)}, bf16[16,32,256]{2,1,0:T(8,128)(2,1)S(1)}) custom-call(bf16[16,16,704]{2,1,0:T(8,128)(2,1)S(1)} %copy.563.refs_0_, bf16[16,32,256]{2,1,0:T(8,128)(2,1)S(1)} %pad.30.refs_1_), custom_call_target="tpu_custom_call" | custom-call | tf_op jit(solution)/shard_map/reduce_ctx/pallas_call | solution.py:457
  (535 shorter events, 151.5 us)
Async XLA Ops:
  7.2 620.8 %all-reduce.10.cloned.1.call-start = ((), (), s32[]{:S(2)}) async-start(), calls=%async_computation | async-start | bytes 1179648 | tf_op jit(solution)/shard_map/psum | solution.py:1475
  17.3 7.2 %copy-start.119 = (s32[2,128,2]{1,2,0:T(2,128)S(1)}, s32[2,128,2]{1,2,0:T(2,128)}, u32[]{:S(2)}) copy-start(s32[2,128,2]{1,2,0:T(2,128)} %param.33) | copy-start | bytes 6148
  17.3 7.2 %copy-start.109 = (bf16[2048,4]{0,1:T(4,128)(2,1)S(1)}, bf16[2048,4]{0,1:T(4,128)(2,1)}, u32[]{:S(2)}) copy-start(bf16[2048,4]{0,1:T(4,128)(2,1)} %param.22) | copy-start | bytes 49156
  415.2 9.2 %copy-start.22 = (bf16[2048,1,16]{2,0,1:T(8,128)(2,1)S(1)}, bf16[2048,1,16]{2,0,1:T(8,128)(2,1)}, u32[]{:S(2)}) copy-start(bf16[2048,1,16]{2,0,1:T(8,128)(2,1)} %get-tuple-element.80) | copy-start | bytes 196612
  425.3 9.3 %copy-start.21 = (bf16[2048,1,16]{2,0,1:T(8,128)(2,1)S(1)}, bf16[2048,1,16]{2,0,1:T(8,128)(2,1)}, u32[]{:S(2)}) copy-start(bf16[2048,1,16]{2,0,1:T(8,128)(2,1)} %get-tuple-element.74) | copy-start | bytes 196612
  435.4 8.6 %copy-start.20 = (bf16[2048,1,16]{2,0,1:T(8,128)(2,1)S(1)}, bf16[2048,1,16]{2,0,1:T(8,128)(2,1)}, u32[]{:S(2)}) copy-start(bf16[2048,1,16]{2,0,1:T(8,128)(2,1)} %get-tuple-element.68) | copy-start | bytes 196612
  444.2 9.9 %copy-start.100 = (bf16[2048,1,16]{0,2,1:T(8,128)(2,1)S(1)}, bf16[2048,1,16]{0,2,1:T(8,128)(2,1)}, u32[]{:S(2)}) copy-start(bf16[2048,1,16]{0,2,1:T(8,128)(2,1)} %copy.483) | copy-start | bytes 196612
  444.2 9.9 %copy-start.99 = (bf16[2048,1,16]{0,2,1:T(8,128)(2,1)S(1)}, bf16[2048,1,16]{0,2,1:T(8,128)(2,1)}, u32[]{:S(2)}) copy-start(bf16[2048,1,16]{0,2,1:T(8,128)(2,1)} %copy.484) | copy-start | bytes 196612
  444.2 9.9 %copy-start.98 = (bf16[2048,1,16]{0,2,1:T(8,128)(2,1)S(1)}, bf16[2048,1,16]{0,2,1:T(8,128)(2,1)}, u32[]{:S(2)}) copy-start(bf16[2048,1,16]{0,2,1:T(8,128)(2,1)} %copy.485) | copy-start | bytes 196612
  444.2 10.0 %copy-start.97 = (bf16[2048,1,16]{0,2,1:T(8,128)(2,1)S(1)}, bf16[2048,1,16]{0,2,1:T(8,128)(2,1)}, u32[]{:S(2)}) copy-start(bf16[2048,1,16]{0,2,1:T(8,128)(2,1)} %copy.486) | copy-start | bytes 196612
  444.2 10.0 %copy-start.96 = (bf16[2048,1,16]{0,2,1:T(8,128)(2,1)S(1)}, bf16[2048,1,16]{0,2,1:T(8,128)(2,1)}, u32[]{:S(2)}) copy-start(bf16[2048,1,16]{0,2,1:T(8,128)(2,1)} %copy.487) | copy-start | bytes 196612
  444.2 10.0 %copy-start.95 = (bf16[2048,1,16]{0,2,1:T(8,128)(2,1)S(1)}, bf16[2048,1,16]{0,2,1:T(8,128)(2,1)}, u32[]{:S(2)}) copy-start(bf16[2048,1,16]{0,2,1:T(8,128)(2,1)} %copy.488) | copy-start | bytes 196612
  444.2 10.0 %copy-start.94 = (bf16[2048,1,16]{0,2,1:T(8,128)(2,1)S(1)}, bf16[2048,1,16]{0,2,1:T(8,128)(2,1)}, u32[]{:S(2)}) copy-start(bf16[2048,1,16]{0,2,1:T(8,128)(2,1)} %copy.489) | copy-start | bytes 196612
  444.2 10.1 %copy-start.90 = (bf16[2048,1,16]{0,2,1:T(8,128)(2,1)S(1)}, bf16[2048,1,16]{0,2,1:T(8,128)(2,1)}, u32[]{:S(2)}) copy-start(bf16[2048,1,16]{0,2,1:T(8,128)(2,1)} %copy.490) | copy-start | bytes 196612
  444.2 10.1 %copy-start.88 = (bf16[2048,1,16]{0,2,1:T(8,128)(2,1)S(1)}, bf16[2048,1,16]{0,2,1:T(8,128)(2,1)}, u32[]{:S(2)}) copy-start(bf16[2048,1,16]{0,2,1:T(8,128)(2,1)} %copy.491) | copy-start | bytes 196612
  444.2 10.1 %copy-start.86 = (bf16[2048,1,16]{0,2,1:T(8,128)(2,1)S(1)}, bf16[2048,1,16]{0,2,1:T(8,128)(2,1)}, u32[]{:S(2)}) copy-start(bf16[2048,1,16]{0,2,1:T(8,128)(2,1)} %copy.492) | copy-start | bytes 196612
  444.2 10.1 %copy-start.91 = (bf16[2048,1,16]{0,2,1:T(8,128)(2,1)S(1)}, bf16[2048,1,16]{0,2,1:T(8,128)(2,1)}, u32[]{:S(2)}) copy-start(bf16[2048,1,16]{0,2,1:T(8,128)(2,1)} %copy.494) | copy-start | bytes 196612
  444.3 10.1 %copy-start.92 = (bf16[2048,1,16]{0,2,1:T(8,128)(2,1)S(1)}, bf16[2048,1,16]{0,2,1:T(8,128)(2,1)}, u32[]{:S(2)}) copy-start(bf16[2048,1,16]{0,2,1:T(8,128)(2,1)} %copy.495) | copy-start | bytes 196612
  445.3 9.2 %copy-start.93 = (bf16[2048,1,16]{0,2,1:T(8,128)(2,1)S(1)}, bf16[2048,1,16]{0,2,1:T(8,128)(2,1)}, u32[]{:S(2)}) copy-start(bf16[2048,1,16]{0,2,1:T(8,128)(2,1)} %copy.496) | copy-start | bytes 196612
  446.1 8.3 %copy-start.89 = (bf16[2048,1,16]{0,2,1:T(8,128)(2,1)S(1)}, bf16[2048,1,16]{0,2,1:T(8,128)(2,1)}, u32[]{:S(2)}) copy-start(bf16[2048,1,16]{0,2,1:T(8,128)(2,1)} %copy.497) | copy-start | bytes 196612
  447.0 7.4 %copy-start.87 = (bf16[2048,1,16]{0,2,1:T(8,128)(2,1)S(1)}, bf16[2048,1,16]{0,2,1:T(8,128)(2,1)}, u32[]{:S(2)}) copy-start(bf16[2048,1,16]{0,2,1:T(8,128)(2,1)} %copy.498) | copy-start | bytes 196612
  447.9 6.6 %copy-start.85 = (bf16[2048,1,16]{0,2,1:T(8,128)(2,1)S(1)}, bf16[2048,1,16]{0,2,1:T(8,128)(2,1)}, u32[]{:S(2)}) copy-start(bf16[2048,1,16]{0,2,1:T(8,128)(2,1)} %copy.499) | copy-start | bytes 196612
  520.9 7.1 %copy-start.10 = (bf16[2,1152,1,2,128]{4,3,2,1,0:T(2,128)(2,1)S(1)}, bf16[2,1152,1,2,128]{4,3,2,1,0:T(2,128)(2,1)}, u32[]{:S(2)}) copy-start(bf16[2,1152,1,2,128]{4,3,2,1,0:T(2,128)(2,1)} %get-tuple-element.111) | copy-start | bytes 3538948
  548.6 19.7 %copy-start.55 = (bf16[256,2048]{1,0:T(8,128)(2,1)S(1)}, bf16[256,2048]{1,0:T(8,128)(2,1)}, u32[]{:S(2)}) copy-start(bf16[256,2048]{1,0:T(8,128)(2,1)} %get-tuple-element.53) | copy-start | bytes 3145732
  (107 other events, 294.7 us)
Sparse Core Ops, SparseCore 0:
  367.8 116.2 all-reduce.9

commit v3 on v2

--- a/solution.py
+++ b/solution.py
@@ -42,442 +42,8 @@
     return ref.at[pl.ds(pl.multiple_of(rank * size, size), size), :]
 
 
-def gather_kernel(kinds, tp_kinds, *refs):
-    n, m = len(kinds), len(tp_kinds)
-    src, refs = list(refs[:n]), refs[n:]
-    tp_src, refs = refs[:m], refs[m:]
-    dst, refs = refs[:n], refs[n:]
-    tp_dst, refs = refs[:m], refs[m:]
-    send, recv, local, tp_send, tp_recv, tp_local = refs
-    src = [tp_dst[m - 1] if r is None else r for r in src]
-    me, tp = lax.axis_index("ctx"), lax.axis_index("tp")
-    core, side = me ^ 1, me ^ 2
-    up, down, far = lax.rem(me + 4, 16), lax.rem(me + 12, 16), lax.rem(me + 8, 16)
-    barrier = pltpu.get_barrier_semaphore()
-    for d in (core, side, up, down):
-        pl.semaphore_signal(barrier, inc=1, device_id=(d, tp), device_id_type=MESH)
-    for d in range(1, N_TP):
-        pl.semaphore_signal(barrier, inc=1, device_id=(me, tp ^ d), device_id_type=MESH)
-    pl.semaphore_wait(barrier, 4 + N_TP - 1)
-    started, staying = [], []
-    counter = [0] * n
-
-    def tp_copy(i, d, rank):
-        size = tp_src[i].shape[1 if tp_kinds[i] == "cols" else 0]
-        return pltpu.make_async_remote_copy(
-            src_ref=tp_src[i],
-            dst_ref=tp_part(tp_kinds[i], tp_dst[i], rank, size),
-            send_sem=tp_send.at[i, d],
-            recv_sem=tp_recv.at[i, d],
-            device_id=(me, tp ^ d),
-            device_id_type=MESH,
-        )
-
-    for i in range(m):
-        for d in range(1, N_TP):
-            c = tp_copy(i, d, tp)
-            c.start()
-            started.append(c)
-        size = tp_src[i].shape[1 if tp_kinds[i] == "cols" else 0]
-        c = pltpu.make_async_copy(
-            tp_src[i], tp_part(tp_kinds[i], tp_dst[i], tp, size), tp_local.at[i]
-        )
-        c.start()
-        staying.append(c)
-
-    def copy(t, item, owner, low, high, to, slot, own):
-        there = region(kinds[t], dst[t], owner, low, high)
-        return pltpu.make_async_remote_copy(
-            src_ref=own_part(kinds[t], src[t], low, high) if own else there,
-            dst_ref=there,
-            send_sem=send.at[t, slot],
-            recv_sem=recv.at[t, item],
-            device_id=(to, tp),
-            device_id_type=MESH,
-        )
-
-    def go(t, item, owner, low, high, to, own=False):
-        c = copy(t, item, owner, low, high, to, counter[t], own)
-        counter[t] += 1
-        c.start()
-        started.append(c)
-
-    arrive = {
-        0: (side, 0, 4),
-        1: (down, 0, 4),
-        2: (up, 0, 4),
-        3: (down ^ 2, 0, 2),
-        4: (up ^ 2, 0, 2),
-        5: (far, 1, 3),
-        6: (far, 0, 1),
-        7: (far, 3, 4),
-        8: (far ^ 2, 1, 2),
-        9: (far ^ 2, 0, 1),
-        10: (down ^ 2, 2, 4),
-        11: (up ^ 2, 2, 4),
-        12: (far ^ 2, 2, 4),
-    }
-
-    def got(t, item):
-        owner, low, high = arrive[item]
-        copy(t, item, owner, low, high, core, 0, False).wait_recv()
-        go(t, 13 + item, owner, low, high, core)
-
-    def first(t):
-        go(t, 0, me, 0, 4, side, True)
-        go(t, 2, me, 0, 4, down, True)
-        go(t, 1, me, 0, 4, up, True)
-        go(t, 26, me, 0, 4, core, True)
-        c = pltpu.make_async_copy(src[t], region(kinds[t], dst[t], me, 0, 4), local.at[t])
-        c.start()
-        staying.append(c)
-
-    for t in range(n - 1):
-        first(t)
-    for i in range(m):
-        for d in range(1, N_TP):
-            tp_copy(i, d, tp ^ d).wait_recv()
-    staying[m - 1].wait()
-    first(n - 1)
-    for t in range(n):
-        got(t, 0)
-        go(t, 3, side, 0, 2, up)
-        go(t, 4, side, 0, 2, down)
-        got(t, 1)
-        go(t, 5, down, 1, 3, up)
-        go(t, 10, down, 2, 4, side)
-        got(t, 2)
-        go(t, 6, up, 0, 1, down)
-        go(t, 7, up, 3, 4, down)
-        go(t, 11, up, 2, 4, side)
-    for t in range(n):
-        got(t, 3)
-        go(t, 8, down ^ 2, 1, 2, up)
-        got(t, 4)
-        go(t, 9, up ^ 2, 0, 1, down)
-        got(t, 5)
-        got(t, 6)
-        got(t, 7)
-        go(t, 12, far, 2, 4, side)
-    for t in range(n):
-        for item in range(8, 13):
-            got(t, item)
-    for t in range(n):
-        for item in range(13):
-            owner, low, high = arrive[item]
-            copy(t, 13 + item, owner ^ 1, low, high, core, 0, False).wait_recv()
-        copy(t, 26, core, 0, 4, core, 0, False).wait_recv()
-    for c in started:
-        c.wait_send()
-    for i, c in enumerate(staying):
-        if i != m - 1:
-            c.wait()
-
-
-def gather_all(shards, kinds, tp_shards, tp_kinds):
-    n, m = len(kinds), len(tp_kinds)
-    shapes, tp_shapes = [], []
-    for s, k in zip(tp_shards, tp_kinds):
-        shape = list(s.shape)
-        shape[1 if k == "cols" else 0] *= N_TP
-        tp_shapes.append(jax.ShapeDtypeStruct(tuple(shape), s.dtype))
-    for s, k in zip(list(shards) + [tp_shapes[-1]], kinds):
-        shape = list(s.shape)
-        shape[{"rows": 1, "flat": 0, "cols": 2}[k]] *= N_CTX
-        shapes.append(jax.ShapeDtypeStruct(tuple(shape), s.dtype))
-
-    def body(*refs):
-        gather_kernel(kinds, tp_kinds, *refs[: n - 1], None, *refs[n - 1 :])
-
-    out = pl.pallas_call(
-        body,
-        out_shape=tuple(shapes + tp_shapes),
-        in_specs=[ANY] * (n - 1 + m),
-        out_specs=tuple([ANY] * (n + m)),
-        scratch_shapes=[
-            pltpu.SemaphoreType.DMA((n, 32)),
-            pltpu.SemaphoreType.DMA((n, 27)),
-            pltpu.SemaphoreType.DMA((n,)),
-            pltpu.SemaphoreType.DMA((m, N_TP)),
-            pltpu.SemaphoreType.DMA((m, N_TP)),
-            pltpu.SemaphoreType.DMA((m,)),
-        ],
-        compiler_params=pltpu.CompilerParams(collective_id=0, has_side_effects=True),
-        name="gather_all",
-    )(*shards, *tp_shards)
-    return out[:n], out[n : n + m - 1]
-
-
-def exchange_kernel(kinds, *refs):
-    n = len(kinds)
-    src, refs = refs[:n], refs[n:]
-    dst, refs = refs[:n], refs[n:]
-    held, refs = refs[:n], refs[n:]
-    send, recv = refs
-    me, tp = lax.axis_index("ctx"), lax.axis_index("tp")
-    barrier = pltpu.get_barrier_semaphore()
-    for d in range(1, N_TP):
-        pl.semaphore_signal(barrier, inc=1, device_id=(me, tp ^ d), device_id_type=MESH)
-    pl.semaphore_wait(barrier, N_TP - 1)
-
-    def part(i, ref, rank):
-        if kinds[i].endswith("rows"):
-            size = src[i].shape[0] // N_TP
-            return ref.at[pl.ds(pl.multiple_of(rank * size, size), size), :]
-        size = src[i].shape[1] // N_TP
-        return ref.at[:, pl.ds(pl.multiple_of(rank * size, size), size)]
-
-    def scatter(i, d):
-        return pltpu.make_async_remote_copy(
-            src_ref=part(i, src[i], tp ^ d),
-            dst_ref=held[i].at[d],
-            send_sem=send.at[i, d],
-            recv_sem=recv.at[i, d],
-            device_id=(me, tp ^ d),
-            device_id_type=MESH,
-        )
-
-    def spread(i, d, rank):
-        return pltpu.make_async_remote_copy(
-            src_ref=part(i, dst[i], rank),
-            dst_ref=part(i, dst[i], rank),
-            send_sem=send.at[i, N_TP + d],
-            recv_sem=recv.at[i, N_TP + d],
-            device_id=(me, tp ^ d),
-            device_id_type=MESH,
-        )
-
-    for i in range(n):
-        for d in range(1, N_TP):
-            scatter(i, d).start()
-    for i in range(n):
-        for d in range(1, N_TP):
-            scatter(i, d).wait_recv()
-        total = part(i, src[i], tp)[...].astype(f32)
-        for d in range(1, N_TP):
-            total = total + held[i][d].astype(f32)
-        if kinds[i].startswith("ar"):
-            part(i, dst[i], tp)[...] = total.astype(dst[i].dtype)
-            for d in range(1, N_TP):
-                spread(i, d, tp).start()
-        else:
-            dst[i][...] = total
-    for i in range(n):
-        for d in range(1, N_TP):
-            scatter(i, d).wait_send()
-            if kinds[i].startswith("ar"):
-                spread(i, d, tp ^ d).wait_recv()
-                spread(i, d, tp).wait_send()
-
-
-def exchange(arrays, kinds, cid):
-    outs, held = [], []
-    for a, k in zip(arrays, kinds):
-        if k == "rs_cols":
-            outs.append(jax.ShapeDtypeStruct((a.shape[0], a.shape[1] // N_TP), f32))
-        else:
-            outs.append(jax.ShapeDtypeStruct(a.shape, a.dtype))
-        r, c = a.shape
-        held.append(
-            pltpu.VMEM((N_TP, r // N_TP, c) if k == "ar_rows" else (N_TP, r, c // N_TP), a.dtype)
-        )
-    n = len(kinds)
-    return pl.pallas_call(
-        functools.partial(exchange_kernel, kinds),
-        out_shape=tuple(outs),
-        in_specs=[VMEM] * n,
-        out_specs=tuple([VMEM] * n),
-        scratch_shapes=held
-        + [pltpu.SemaphoreType.DMA((n, 2 * N_TP)), pltpu.SemaphoreType.DMA((n, 2 * N_TP))],
-        compiler_params=pltpu.CompilerParams(
-            collective_id=cid, has_side_effects=True, vmem_limit_bytes=48 << 20
-        ),
-        name=f"exchange_{cid}",
-    )(*arrays)
-
-
-def halo_kernel(src, dst, send, recv, local):
-    me, tp = lax.axis_index("ctx"), lax.axis_index("tp")
-    block = src.shape[1]
-    barrier = pltpu.get_barrier_semaphore()
-    for d in range(1, N_CTX):
-        pl.semaphore_signal(
-            barrier, inc=1, device_id=(lax.rem(me + d, N_CTX), tp), device_id_type=MESH
-        )
-    pl.semaphore_wait(barrier, N_CTX - 1)
-
-    def copy(d):
-        return pltpu.make_async_remote_copy(
-            src_ref=src,
-            dst_ref=dst.at[:, pl.ds((PAST - d) * block, block), :],
-            send_sem=send.at[d],
-            recv_sem=recv.at[d],
-            device_id=(lax.rem(me + d, N_CTX), tp),
-            device_id_type=MESH,
-        )
-
-    own = pltpu.make_async_copy(src, dst.at[:, pl.ds(PAST * block, block), :], local)
-    own.start()
-    for d in range(1, PAST + 1):
-        copy(d).start()
-    own.wait()
-    for d in range(1, PAST + 1):
-        copy(d).wait()
-
-
-def halo(kv_own):
-    seqs, block, cols = kv_own.shape
-    return pl.pallas_call(
-        halo_kernel,
-        out_shape=jax.ShapeDtypeStruct((seqs, (PAST + 1) * block, cols), kv_own.dtype),
-        in_specs=[ANY],
-        out_specs=ANY,
-        scratch_shapes=[
-            pltpu.SemaphoreType.DMA((PAST + 1,)),
-            pltpu.SemaphoreType.DMA((PAST + 1,)),
-            pltpu.SemaphoreType.DMA,
-        ],
-        compiler_params=pltpu.CompilerParams(collective_id=8, has_side_effects=True),
-        name="halo",
-    )(kv_own)
-
-
-def halo_back_kernel(src, dst, held, send, recv):
-    me, tp = lax.axis_index("ctx"), lax.axis_index("tp")
-    block = dst.shape[1]
-    barrier = pltpu.get_barrier_semaphore()
-    for d in range(1, N_CTX):
-        pl.semaphore_signal(
-            barrier, inc=1, device_id=(lax.rem(me + d, N_CTX), tp), device_id_type=MESH
-        )
-    pl.semaphore_wait(barrier, N_CTX - 1)
-
-    def copy(d):
-        return pltpu.make_async_remote_copy(
-            src_ref=src.at[:, pl.ds((PAST - d) * block, block), :],
-            dst_ref=held.at[d],
-            send_sem=send.at[d],
-            recv_sem=recv.at[d],
-            device_id=(lax.rem(me + N_CTX - d, N_CTX), tp),
-            device_id_type=MESH,
-        )
-
-    for d in range(1, PAST + 1):
-        copy(d).start()
-    total = src[:, pl.ds(PAST * block, block), :].astype(f32)
-    for d in range(1, PAST + 1):
-        copy(d).wait_recv()
-        total = total + held[d].astype(f32)
-    dst[...] = total
-    for d in range(1, PAST + 1):
-        copy(d).wait_send()
-
-
-def halo_back(partial):
-    seqs, length, cols = partial.shape
-    block = length // (PAST + 1)
-    return pl.pallas_call(
-        halo_back_kernel,
-        out_shape=jax.ShapeDtypeStruct((seqs, block, cols), f32),
-        in_specs=[VMEM],
-        out_specs=VMEM,
-        scratch_shapes=[
-            pltpu.VMEM((PAST + 1, seqs, block, cols), partial.dtype),
-            pltpu.SemaphoreType.DMA((PAST + 1,)),
-            pltpu.SemaphoreType.DMA((PAST + 1,)),
-        ],
-        compiler_params=pltpu.CompilerParams(
-            collective_id=9, has_side_effects=True, vmem_limit_bytes=48 << 20
-        ),
-        name="halo_back",
-    )(partial)
-
-
-def reduce_kernel(spread_too, *refs):
-    n = len(spread_too)
-    src, refs = refs[:n], refs[n:]
-    dst, refs = refs[:n], refs[n:]
-    held, refs = refs[:n], refs[n:]
-    send, recv = refs
-    me, tp = lax.axis_index("ctx"), lax.axis_index("tp")
-    barrier = pltpu.get_barrier_semaphore()
-    for d in range(1, N_CTX):
-        pl.semaphore_signal(barrier, inc=1, device_id=(me ^ d, tp), device_id_type=MESH)
-    pl.semaphore_wait(barrier, N_CTX - 1)
-
-    def scatter(i, d):
-        return pltpu.make_async_remote_copy(
-            src_ref=src[i].at[me ^ d],
-            dst_ref=held[i].at[d],
-            send_sem=send.at[i, d],
-            recv_sem=recv.at[i, d],
-            device_id=(me ^ d, tp),
-            device_id_type=MESH,
-        )
-
-    def spread(i, d, rank):
-        return pltpu.make_async_remote_copy(
-            src_ref=dst[i].at[rank],
-            dst_ref=dst[i].at[rank],
-            send_sem=send.at[i, N_CTX + d],
-            recv_sem=recv.at[i, N_CTX + d],
-            device_id=(me ^ d, tp),
-            device_id_type=MESH,
-        )
-
-    for i in range(n):
-        for d in range(1, N_CTX):
-            scatter(i, d).start()
-    for i in range(n):
-        for d in range(1, N_CTX):
-            scatter(i, d).wait_recv()
-        total = src[i][me].astype(f32)
-        for d in range(1, N_CTX):
-            total = total + held[i][d].astype(f32)
-        if spread_too[i]:
-            dst[i][me] = total.astype(dst[i].dtype)
-            for d in range(1, N_CTX):
-                spread(i, d, me).start()
-        else:
-            dst[i][...] = total
-    for i in range(n):
-        for d in range(1, N_CTX):
-            scatter(i, d).wait_send()
-            if spread_too[i]:
-                spread(i, d, me ^ d).wait_recv()
-                spread(i, d, me).wait_send()
-
-
-def reduce_ctx(arrays, spread_too):
-    outs = [
-        jax.ShapeDtypeStruct(a.shape if s else a.shape[1:], a.dtype if s else f32)
-        for a, s in zip(arrays, spread_too)
-    ]
-    n = len(arrays)
-    return pl.pallas_call(
-        functools.partial(reduce_kernel, spread_too),
-        out_shape=tuple(outs),
-        in_specs=[VMEM] * n,
-        out_specs=tuple([VMEM] * n),
-        scratch_shapes=[pltpu.VMEM(a.shape, a.dtype) for a in arrays]
-        + [pltpu.SemaphoreType.DMA((n, 2 * N_CTX)), pltpu.SemaphoreType.DMA((n, 2 * N_CTX))],
-        compiler_params=pltpu.CompilerParams(
-            collective_id=10, has_side_effects=True, vmem_limit_bytes=48 << 20
-        ),
-        name="reduce_ctx",
-    )(*arrays)
-
-
 def rms_scale(values, gain):
     return values * lax.rsqrt(jnp.mean(values * values, axis=-1, keepdims=True) + eps) * gain
-
-
-def norm_back(values, gain, grad_normed):
-    inverse = lax.rsqrt(jnp.mean(values * values, axis=-1, keepdims=True) + eps)
-    scaled = grad_normed * gain
-    return inverse * scaled - values * inverse**3 * jnp.mean(
-        scaled * values, axis=-1, keepdims=True
-    )
 
 
 def doc_layout(doc_lengths, positions):
@@ -492,23 +58,6 @@
 
 def dot(a, b, ca=1, cb=0):
     return lax.dot_general(a, b, (((ca,), (cb,)), ((), ())), preferred_element_type=f32)
-
-
-def rope(x, cosine, sine, sign):
-    half = HEAD_DIM // 2
-    x1, x2 = x[..., :half], x[..., half:]
-    s = sine * sign
-    return jnp.concatenate([x1 * cosine - x2 * s, x2 * cosine + x1 * s], axis=-1)
-
-
-def gates_of(logits, onehot):
-    chosen = jnp.sum(logits[:, None, :] * onehot, axis=-1)
-    return jax.nn.softmax(chosen, axis=-1)
-
-
-def gates_back(gates, grad_gates, onehot):
-    inner = gates * (grad_gates - jnp.sum(gates * grad_gates, axis=-1, keepdims=True))
-    return jnp.sum(inner[..., None] * onehot, axis=1)
 
 
 def dot_nt(a, b):
@@ -1240,6 +789,429 @@
     )(*shards_in, *tp_shards, *small)
 
 
+def backward_kernel(
+    dx1, dx1_own, x0, n1, n2, dy, kv_all, q_all, probs, ob, gates, z_q, z_kv, z_sum,
+    hot0, hot1, cosine, sine, gain, router, b_q, b_kv, a_o, f_gu, f_d,
+    h_q, h_kv, h_o, h_wide,
+    grad_tokens, wide_a, wide_b, heads_out, gu_out, d_out,
+    w_q, w_kv, w_o, wide, dob, dkv, dkv_held, dq, dkv_own, dn, parts, own, held, z_part, z_held, z_done,
+    dots, tails, gu_src, d_src, a_src, b_src, heads_src, gu_held, d_held, a_held, b_held, heads_held,
+    load, tp_send, tp_recv, core_send, core_recv, kv_send, kv_recv, ctx_send, ctx_recv,
+):
+    me, tp = lax.axis_index("ctx"), lax.axis_index("tp")
+    core = me ^ 1
+    on_core = lax.rem(me, 2)
+    rows, model = x0.shape
+    part = model // N_TP
+    half = rows // 2
+    experts = w_q.shape[0]
+    width = w_q.shape[2]
+    heads = width // HEAD_DIM
+    span = (PAST + 1) * half
+    greet([(me ^ d, tp) for d in range(1, N_CTX)] + [(me, tp ^ d) for d in range(1, N_TP)])
+    loads = []
+    for i, (h, w) in enumerate(((h_wide, wide), (h_o, w_o), (h_q, w_q), (h_kv, w_kv))):
+        c = pltpu.make_async_copy(h, w, load.at[i])
+        c.start()
+        loads.append(c)
+
+    ctx_src = [gu_src, d_src, a_src, b_src, heads_src]
+    ctx_held = [gu_held, d_held, a_held, b_held, heads_held]
+    ctx_dst = [gu_out, d_out, None, None, heads_out]
+
+    def ctx_scatter(i, d):
+        return pltpu.make_async_remote_copy(
+            src_ref=ctx_src[i].at[me ^ d],
+            dst_ref=ctx_held[i].at[d],
+            send_sem=ctx_send.at[i, d],
+            recv_sem=ctx_recv.at[i, d],
+            device_id=(me ^ d, tp),
+            device_id_type=MESH,
+        )
+
+    def ctx_spread(i, d, rank):
+        return pltpu.make_async_remote_copy(
+            src_ref=ctx_dst[i].at[rank],
+            dst_ref=ctx_dst[i].at[rank],
+            send_sem=ctx_send.at[i, N_CTX + d],
+            recv_sem=ctx_recv.at[i, N_CTX + d],
+            device_id=(me ^ d, tp),
+            device_id_type=MESH,
+        )
+
+    def ctx_start(i):
+        for d in range(1, N_CTX):
+            ctx_scatter(i, d).start()
+
+    def ctx_total(i):
+        total = ctx_src[i][me].astype(f32)
+        for d in range(1, N_CTX):
+            ctx_scatter(i, d).wait_recv()
+            total = total + ctx_held[i][d].astype(f32)
+        return total
+
+    def ctx_again(i):
+        ctx_dst[i][me] = ctx_total(i).astype(ctx_dst[i].dtype)
+        for d in range(1, N_CTX):
+            ctx_spread(i, d, me).start()
+
+    def ctx_end(i):
+        for d in range(1, N_CTX):
+            ctx_scatter(i, d).wait_send()
+            if ctx_dst[i] is not None:
+                ctx_spread(i, d, me ^ d).wait_recv()
+                ctx_spread(i, d, me).wait_send()
+
+    for i in range(N_CTX):
+        s, slot = i // 8, i % 8
+        at = slice(16 * slot, 16 * slot + 16)
+        first = 640 * (slot % 2)
+        gu_src[i, :, :640] = f_gu[s, at, first : first + 640].astype(bf16)
+        gu_src[i, :, 640:] = f_gu[s, at, 1280:].astype(bf16)
+        d_src[i] = f_d[s, 64 + 8 * slot : 72 + 8 * slot, :]
+    ctx_start(0)
+    ctx_start(1)
+
+    lane = lax.broadcasted_iota(jnp.int32, (rows, 128), 1)
+    seq = lax.broadcasted_iota(jnp.int32, (rows, 128), 0) // half
+    hots = (hot0, hot1)
+
+    loads[0].wait()
+    dz_o = by_seq(dx1[...], lambda s, v: dot(v, wide[:, 256 + 128 * s : 384 + 128 * s]))
+    loads[1].wait()
+    g = [jnp.zeros((rows, width), f32), jnp.zeros((rows, width), f32)]
+    g_ao = [jnp.zeros((128, width), f32), jnp.zeros((128, width), f32)]
+    for e in range(experts):
+        dz_e = jnp.where(lane // 16 == e, dz_o, 0.0)
+        g_e = dot_nt(dx1[...], w_o[e]) + by_seq(dz_e.astype(bf16), lambda s, v: dot(v, a_o[s]))
+        o_e = jnp.where(hot0[:, e : e + 1] > 0, ob[0].astype(f32), 0.0)
+        o_e = o_e + jnp.where(hot1[:, e : e + 1] > 0, ob[1].astype(f32), 0.0)
+        o_e = o_e.astype(bf16)
+        dz_e = (dz_e * gates[:, e : e + 1]).astype(bf16)
+        for s in range(2):
+            at = slice(half * s, half * s + half)
+            g_ao[s] = g_ao[s] + dot_tn(dz_e[at], o_e[at])
+        for k in range(2):
+            g[k] = g[k] + jnp.where(hots[k][:, e : e + 1] > 0, g_e, 0.0)
+    d_gates = jnp.zeros((rows, 128), f32)
+    for k in range(2):
+        d_gate = jnp.sum(g[k] * ob[k].astype(f32), axis=1, keepdims=True)
+        d_gates = d_gates + jnp.where(hots[k][...] > 0, d_gate, 0.0)
+        gate = jnp.sum(hots[k][...] * gates[...], axis=1, keepdims=True)
+        d_out = (g[k] * gate).astype(bf16)
+        for s in range(2):
+            for h in range(heads):
+                dob[s * heads + h, k * half : k * half + half, :] = d_out[
+                    half * s : half * s + half, HEAD_DIM * h : HEAD_DIM * h + HEAD_DIM
+                ]
+    d_logits = gates[...] * (d_gates - jnp.sum(gates[...] * d_gates, axis=1, keepdims=True))
+    d_logits = d_logits.astype(bf16)
+
+    def attend_back(i, carry):
+        s = i // heads
+        h = lax.rem(i, heads)
+        at = pl.ds(pl.multiple_of(h * HEAD_DIM, HEAD_DIM), HEAD_DIM)
+        v_at = pl.ds(pl.multiple_of(width + h * HEAD_DIM, HEAD_DIM), HEAD_DIM)
+        keys = kv_all[:, s, :, at].reshape(span, HEAD_DIM)
+        values = kv_all[:, s, :, v_at].reshape(span, HEAD_DIM)
+        seq_rows = pl.ds(pl.multiple_of(s * half, half), half)
+        d_keys = jnp.zeros((span, HEAD_DIM), f32)
+        d_values = jnp.zeros((span, HEAD_DIM), f32)
+        for k in range(2):
+            k_rows = slice(k * half, k * half + half)
+            d_o = dob[i, k_rows, :]
+            p = probs[i, k_rows, :]
+            delta = jnp.sum(d_o.astype(f32) * ob[k, seq_rows, at].astype(f32), axis=1, keepdims=True)
+            d_s = (p.astype(f32) * (dot_nt(d_o, values) - delta)).astype(bf16)
+            d_q = dot(d_s, keys) * HEAD_DIM**-0.5
+            turned = d_q * cosine[seq_rows, :] - pltpu.roll(d_q, HEAD_DIM // 2, 1) * sine[seq_rows, :]
+            dq[k, seq_rows, at] = turned.astype(bf16)
+            d_keys = d_keys + dot_tn(d_s, q_all[i, k_rows, :])
+            d_values = d_values + dot_tn(p, d_o)
+        d_keys = (d_keys * HEAD_DIM**-0.5).astype(bf16)
+        dkv[:, s, :, at] = d_keys.reshape(PAST + 1, half, HEAD_DIM)
+        dkv[:, s, :, v_at] = d_values.astype(bf16).reshape(PAST + 1, half, HEAD_DIM)
+        return carry
+
+    lax.fori_loop(0, 2 * heads, attend_back, 0)
+
+    def to_core(back):
+        return pltpu.make_async_remote_copy(
+            src_ref=dkv.at[PAST - back],
+            dst_ref=dkv_held.at[back // 2],
+            send_sem=core_send.at[back // 2],
+            recv_sem=core_recv.at[back // 2],
+            device_id=(core, tp),
+            device_id_type=MESH,
+        )
+
+    def to_owner(back):
+        return pltpu.make_async_remote_copy(
+            src_ref=dkv.at[PAST - back],
+            dst_ref=dkv_held.at[3 + back // 2],
+            send_sem=kv_send.at[back // 2],
+            recv_sem=kv_recv.at[back // 2],
+            device_id=(lax.rem(me + N_CTX - back, N_CTX), tp),
+            device_id_type=MESH,
+        )
+
+    for back in (1, 3, 5, 7):
+        to_core(back).start()
+    for back in (1, 3, 5, 7):
+        to_core(back).wait_recv()
+        mine = PAST - (back - 1) - 2 * on_core
+        dkv[mine] = (dkv[mine].astype(f32) + dkv_held[back // 2].astype(f32)).astype(bf16)
+    for back in (2, 4, 6, 8):
+        to_owner(back).start()
+
+    loads[2].wait()
+    dz_q = jnp.zeros((rows, 128), f32)
+    g_bq = jnp.zeros((128, width), f32)
+    chosen = []
+    for e in range(experts):
+        dq_e = jnp.where(hot0[:, e : e + 1] > 0, dq[0].astype(f32), 0.0)
+        dq_e = dq_e + jnp.where(hot1[:, e : e + 1] > 0, dq[1].astype(f32), 0.0)
+        dq_e = dq_e.astype(bf16)
+        chosen.append(dq_e)
+        mine = (lane // 64 == seq) & ((lane % 64) // 16 == e)
+        dz_q = dz_q + jnp.where(mine, dot_nt(dq_e, b_q[...]), 0.0)
+        z_e = jnp.where(mine, z_q[...].astype(f32), 0.0).astype(bf16)
+        g_bq = g_bq + dot_tn(z_e, dq_e)
+    dz_q = dz_q.astype(bf16)
+    z_part[:, :128] = dz_q
+    for j in range(N_TP):
+        at = slice(part * j, part * j + part)
+        total = dot_nt(dz_q, wide[at, 512:640]) + dot_nt(d_logits, router[at, :])
+        for e in range(experts):
+            total = total + dot_nt(chosen[e], w_q[e, at, :])
+        dn[j] = total
+    own_columns = lax.broadcasted_iota(jnp.int32, (model, part), 1)
+    own_columns = (own_columns // 16) * 128 + tp * 16 + own_columns % 16
+    pick = (lax.broadcasted_iota(jnp.int32, (model, part), 0) == own_columns).astype(bf16)
+    n2_own = dot(n2[...], pick).astype(bf16)
+    dx1_cols = dot(dx1[...], pick).astype(bf16)
+    dy_own = dot(dy[...], pick).astype(bf16)
+    n1_own = dot(n1[...], pick).astype(bf16)
+    lane_m = lax.broadcasted_iota(jnp.int32, (part, 128), 1)
+    for s in range(2):
+        at = slice(half * s, half * s + half)
+        a_src[:, :, 128 * s : 128 * s + 128] = (
+            dot_tn(n2_own[at], z_sum[at, :128]).astype(bf16).reshape(N_CTX, 16, 128)
+        )
+        low = jnp.where(
+            lane_m < 64, dot_tn(dx1_cols[at], z_sum[at, 128:]), dot_tn(dy_own[at], z_sum[at, 128:])
+        )
+        a_src[:, :, 256 + 128 * s : 384 + 128 * s] = low.astype(bf16).reshape(N_CTX, 16, 128)
+
+    total = dkv[PAST].astype(f32)
+    for back in (2, 4, 6, 8):
+        to_owner(back).wait_recv()
+        total = total + dkv_held[3 + back // 2].astype(f32)
+    ctx_start(2)
+    ctx_again(0)
+    ctx_again(1)
+    for h in range(heads):
+        at = slice(HEAD_DIM * h, HEAD_DIM * h + HEAD_DIM)
+        d_k = jnp.concatenate([total[0, :, at], total[1, :, at]], axis=0)
+        turned = d_k * cosine[...] - pltpu.roll(d_k, HEAD_DIM // 2, 1) * sine[...]
+        dkv_own[:, at] = turned.astype(bf16)
+    dkv_own[:, width:] = jnp.concatenate([total[0, :, width:], total[1, :, width:]], axis=0).astype(bf16)
+    loads[3].wait()
+    dz_kv = dot_nt(dkv_own[...], b_kv[...])
+    keep = (lane[:, :64] // 16) % 2 == seq[:, :64]
+    dz_kv = jnp.where(keep, dz_kv, 0.0).astype(bf16)
+    z_part[:, 128:] = jnp.pad(dz_kv.astype(f32), ((0, 0), (0, 64))).astype(bf16)
+
+    def scatter(d):
+        return pltpu.make_async_remote_copy(
+            src_ref=parts.at[d],
+            dst_ref=held.at[d],
+            send_sem=tp_send.at[0, d],
+            recv_sem=tp_recv.at[0, d],
+            device_id=(me, tp ^ d),
+            device_id_type=MESH,
+        )
+
+    z_rows = rows // N_TP
+
+    def z_region(ref, rank):
+        return ref.at[pl.ds(pl.multiple_of(rank * z_rows, z_rows), z_rows), :]
+
+    def z_scatter(d):
+        return pltpu.make_async_remote_copy(
+            src_ref=z_region(z_part, tp ^ d),
+            dst_ref=z_held.at[d],
+            send_sem=tp_send.at[1, d],
+            recv_sem=tp_recv.at[1, d],
+            device_id=(me, tp ^ d),
+            device_id_type=MESH,
+        )
+
+    def z_spread(d, rank):
+        return pltpu.make_async_remote_copy(
+            src_ref=z_region(z_done, rank),
+            dst_ref=z_region(z_done, rank),
+            send_sem=tp_send.at[2, d],
+            recv_sem=tp_recv.at[2, d],
+            device_id=(me, tp ^ d),
+            device_id_type=MESH,
+        )
+
+    def tail(d, rank):
+        return pltpu.make_async_remote_copy(
+            src_ref=tails.at[rank],
+            dst_ref=tails.at[rank],
+            send_sem=tp_send.at[3, d],
+            recv_sem=tp_recv.at[3, d],
+            device_id=(me, tp ^ d),
+            device_id_type=MESH,
+        )
+
+    for d in range(1, N_TP):
+        z_scatter(d).start()
+    along = jnp.zeros((rows, 1), f32)
+    for j in range(1, N_TP + 1):
+        d = j % N_TP
+        peer = tp ^ d
+        at = pl.ds(pl.multiple_of(peer * part, part), part)
+        total = dn[peer] + dot_nt(dz_kv, wide[at, 640:704]) + dot_nt(dkv_own[...], w_kv[at, :])
+        scaled = total * gain[:, at]
+        along = along + jnp.sum(scaled * x0[:, at].astype(f32), axis=1, keepdims=True)
+        if d:
+            parts[d] = total.astype(bf16)
+            scatter(d).start()
+        else:
+            own[...] = total
+    dots[...] = jnp.broadcast_to(along, dots.shape)
+    tails[tp] = jnp.transpose(dots[...])[:8, :]
+    for d in range(1, N_TP):
+        tail(d, tp).start()
+    total = z_region(z_part, tp)[...].astype(f32)
+    for d in range(1, N_TP):
+        z_scatter(d).wait_recv()
+        total = total + z_held[d].astype(f32)
+    z_region(z_done, tp)[...] = total.astype(bf16)
+    for d in range(1, N_TP):
+        z_spread(d, tp).start()
+    g_bkv = dot_tn(z_kv[...], dkv_own[...])
+    heads_src[:4] = g_bq.astype(bf16).reshape(4, 32, width)
+    heads_src[4] = g_bkv[:32, :width].astype(bf16)
+    heads_src[5] = g_bkv[32:64, width:].astype(bf16)
+    for s in range(2):
+        heads_src[6 + 2 * s : 8 + 2 * s] = g_ao[s][:64].astype(bf16).reshape(2, 32, width)
+    heads_src[10:] = jnp.zeros((6, 32, width), bf16)
+    ctx_start(4)
+    for d in range(1, N_TP):
+        z_spread(d, tp ^ d).wait_recv()
+    b_src[...] = dot_tn(n1_own, z_done[...]).astype(bf16).reshape(N_CTX, 16, part)
+    ctx_start(3)
+    total = own[...]
+    for d in range(1, N_TP):
+        scatter(d).wait_recv()
+        total = total + held[d].astype(f32)
+    for d in range(1, N_TP):
+        tail(d, tp ^ d).wait_recv()
+    whole = tails[0]
+    for d in range(1, N_TP):
+        whole = whole + tails[d]
+    dots[...] = jnp.transpose(jnp.broadcast_to(whole[:1], (128, rows)))
+    own_at = pl.ds(pl.multiple_of(tp * part, part), part)
+    own[...] = total * gain[:, own_at]
+    step = 32
+
+    def finish(i, carry):
+        at = pl.ds(pl.multiple_of(i * step, step), step)
+        x = x0[at, :].astype(f32)
+        inverse = lax.rsqrt(jnp.mean(x * x, axis=1, keepdims=True) + eps)
+        mean = dots[at, :1] * (1.0 / model)
+        back = inverse * own[at, :] - x0[at, own_at].astype(f32) * inverse**3 * mean
+        grad_tokens[at, :] = (dx1_own[at, :] + back).astype(bf16)
+        return carry
+
+    lax.fori_loop(0, rows // step, finish, 0)
+    ctx_again(4)
+    wide_a[...] = ctx_total(2)
+    wide_b[...] = ctx_total(3)
+    for i in range(5):
+        ctx_end(i)
+    for back in (1, 3, 5, 7):
+        to_core(back).wait_send()
+        to_owner(back + 1).wait_send()
+    for d in range(1, N_TP):
+        scatter(d).wait_send()
+        z_scatter(d).wait_send()
+        z_spread(d, tp).wait_send()
+        tail(d, tp).wait_send()
+
+
+def backward(vmem, hbm):
+    dx1, dx1_own, kv_all, f_gu = vmem[0], vmem[1], vmem[6], vmem[23]
+    w_q, w_kv, w_o, wide = hbm
+    rows, model = dx1.shape
+    part = model // N_TP
+    width = w_q.shape[2]
+    heads = width // HEAD_DIM
+    half = rows // 2
+    hidden = vmem[24].shape[2]
+    shape = jax.ShapeDtypeStruct
+    reduced = [
+        ((N_CTX, 16, 768), bf16),
+        ((N_CTX, 8, hidden), f32),
+        ((N_CTX, 16, 512), bf16),
+        ((N_CTX, 16, part), bf16),
+        ((N_CTX, 32, width), bf16),
+    ]
+    return pl.pallas_call(
+        backward_kernel,
+        out_shape=(
+            shape((rows, part), bf16),
+            shape((16, 512), f32),
+            shape((16, part), f32),
+            shape(*reduced[4]),
+            shape(*reduced[0]),
+            shape(*reduced[1]),
+        ),
+        in_specs=[VMEM] * len(vmem) + [ANY] * 4,
+        out_specs=tuple([VMEM] * 6),
+        scratch_shapes=[
+            pltpu.VMEM(w_q.shape, bf16),
+            pltpu.VMEM(w_kv.shape, bf16),
+            pltpu.VMEM(w_o.shape, bf16),
+            pltpu.VMEM(wide.shape, bf16),
+            pltpu.VMEM((2 * heads, rows, HEAD_DIM), bf16),
+            pltpu.VMEM(kv_all.shape, bf16),
+            pltpu.VMEM((8,) + kv_all.shape[1:], bf16),
+            pltpu.VMEM((2, rows, width), bf16),
+            pltpu.VMEM((rows, 2 * width), bf16),
+            pltpu.VMEM((N_TP, rows, part), f32),
+            pltpu.VMEM((N_TP, rows, part), bf16),
+            pltpu.VMEM((rows, part), f32),
+            pltpu.VMEM((N_TP, rows, part), bf16),
+            pltpu.VMEM((rows, 256), bf16),
+            pltpu.VMEM((N_TP, rows // N_TP, 256), bf16),
+            pltpu.VMEM((rows, 256), bf16),
+            pltpu.VMEM((rows, 128), f32),
+            pltpu.VMEM((N_TP, 8, rows), f32),
+        ]
+        + [pltpu.VMEM(*a) for a in reduced + reduced]
+        + [
+            pltpu.SemaphoreType.DMA((4,)),
+            pltpu.SemaphoreType.DMA((4, N_TP)),
+            pltpu.SemaphoreType.DMA((4, N_TP)),
+            pltpu.SemaphoreType.DMA((4,)),
+            pltpu.SemaphoreType.DMA((4,)),
+            pltpu.SemaphoreType.DMA((5,)),
+            pltpu.SemaphoreType.DMA((5,)),
+            pltpu.SemaphoreType.DMA((5, 2 * N_CTX)),
+            pltpu.SemaphoreType.DMA((5, 2 * N_CTX)),
+        ],
+        compiler_params=pltpu.CompilerParams(
+            collective_id=3, has_side_effects=True, vmem_limit_bytes=60 << 20
+        ),
+        name="backward",
+    )(*vmem, *hbm)
+
+
 def shards(
     tokens,
     norm1_gain,
@@ -1262,7 +1234,6 @@
 ):
     seqs, block, part = tokens.shape
     rows = seqs * block
-    n_ctx = lax.axis_size("ctx")
     n_tp = lax.axis_size("tp")
     model = part * n_tp
     experts = w_query.shape[0]
@@ -1272,13 +1243,6 @@
     rank = adapt_heads.shape[2]
     wide_slots = adapt_wide.shape[1]
     ctx_rank = lax.axis_index("ctx")
-    tp_rank = lax.axis_index("tp")
-
-    def split(a):
-        return a.reshape((seqs, block) + a.shape[1:])
-
-    def merge(a):
-        return a.reshape((rows,) + a.shape[2:])
 
     wide_own = adapt_wide.astype(bf16)[adapter_index]
     groups = [[6, 10, 7, 11, 8, 12, 9, 13], list(range(14, 22)), [0, 1, 2, 3], [4, 5]]
@@ -1291,8 +1255,6 @@
     ffn_low = adapt_ffn.astype(bf16)[adapter_index]
     route_a = attention_routes.reshape(rows, -1)
     route_f = feedforward_routes.reshape(rows, -1)
-    hot_a = jax.nn.one_hot(route_a, experts, dtype=f32)
-    hot_f = jax.nn.one_hot(route_f, experts, dtype=f32)
 
     positions = ctx_rank * block + jnp.arange(block, dtype=jnp.int32)
     doc_ids, offsets = doc_layout(doc_lengths, positions)
@@ -1300,34 +1262,8 @@
     frequency = 10000.0 ** (-2.0 * jnp.arange(half, dtype=f32) / HEAD_DIM)
     angles = offsets.astype(f32).reshape(rows)[:, None] * frequency
     cosine, sine = jnp.cos(angles), jnp.sin(angles)
-
-    def low_in(v, first, count):
-        return merge(
-            jnp.einsum(
-                "sbd,dscr->sbcr", split(v), wide[:, :, first : first + count],
-                preferred_element_type=f32,
-            )
-        )
-
-    def low_out(z, factor):
-        return merge(
-            jnp.einsum("sbcr,scrh->sbch", split(z).astype(bf16), factor, preferred_element_type=f32)
-        )
-
-    def low_sum(z, factor):
-        return merge(
-            jnp.einsum("sbcr,scrh->sbh", split(z).astype(bf16), factor, preferred_element_type=f32)
-        )
-
-    def low_back(dp, factor):
-        return merge(
-            jnp.einsum("sbch,scrh->sbcr", split(dp), factor, preferred_element_type=f32)
-        )
-
-    def low_grad(z, dp):
-        return jnp.einsum(
-            "sbcr,sbch->scrh", split(z).astype(bf16), split(dp), preferred_element_type=f32
-        )
+    cosine = jnp.concatenate([cosine, cosine], axis=1)
+    sine = jnp.concatenate([-sine, sine], axis=1)
 
     b_q, b_kv, a_o = heads_low[:, :experts], heads_low[:, experts : experts + 2], heads_low[:, experts + 2 :]
     key_pos = (ctx_rank - PAST) * block + jnp.arange((PAST + 1) * block, dtype=jnp.int32)
@@ -1342,6 +1278,8 @@
         axis=0,
     )
     a_o_wide = jnp.pad(a_o.reshape(seqs, experts * rank, width), ((0, 0), (0, 64), (0, 0)))
+    b_q = b_q.reshape(seqs * experts * rank, width)
+    hot0, hot1 = widen_routes(route_a[:, :1], experts), widen_routes(route_a[:, 1:], experts)
     router_wide = jnp.pad(router_attn, ((0, 0), (0, 128 - experts)))
     (
         w_query, w_key_value, w_out, w_gate_up, w_down, wide, _, dy,
@@ -1358,34 +1296,17 @@
         [
             norm1_gain[None],
             router_wide,
-            widen_routes(route_a[:, :1], experts),
-            widen_routes(route_a[:, 1:], experts),
-            jnp.concatenate([cosine, cosine], axis=1),
-            jnp.concatenate([-sine, sine], axis=1),
+            hot0,
+            hot1,
+            cosine,
+            sine,
             jnp.broadcast_to(doc_ids.reshape(rows, 1), (rows, 128)),
             jnp.broadcast_to(key_doc[:, None, :], (seqs, 8, key_doc.shape[1])),
-            b_q.reshape(seqs * experts * rank, width),
+            b_q,
             b_kv_wide,
             a_o_wide,
         ],
     )
-    wide_low = wide
-    place = {qs: rank * i for i, qs in enumerate(order)}
-    wide = jnp.stack([jnp.stack([wide[:, place[q, s] : place[q, s] + rank] for s in range(wide_slots)], axis=1) for q in range(seqs)], axis=1)
-    ga_e = gates[:, :experts]
-    ga = jnp.sum(ga_e[:, None, :] * hot_a, axis=-1)
-    scale = HEAD_DIM ** (-0.5)
-    length = (PAST + 1) * block
-    kv_all = jnp.swapaxes(kv_all, 0, 1).reshape(seqs, length, 2, heads, HEAD_DIM)
-    probs = jnp.swapaxes(probs.reshape(seqs, heads, 2, block, length), 1, 2).astype(f32)
-    q_s = jnp.transpose(q_all.reshape(seqs, heads, 2, block, HEAD_DIM), (0, 3, 2, 1, 4))
-    ob = jnp.swapaxes(ob, 0, 1)
-    o = ob.reshape(seqs, block, 2, heads, HEAD_DIM).astype(f32)
-    ob_e = jnp.einsum("rke,rkh->reh", hot_a.astype(bf16), ob, preferred_element_type=f32).astype(bf16)
-    xf = x0.astype(f32)
-    z_q = jnp.where(jnp.arange(rows)[:, None] < block, z_q[:, :64], z_q[:, 64:]).reshape(rows, experts, rank).astype(f32)
-    z_kv = z_kv[:, :64].reshape(rows, 2, 2, rank)
-    z_kv = jnp.where(jnp.arange(rows)[:, None, None] < block, z_kv[:, :, 0], z_kv[:, :, 1]).astype(f32)
     blank = jnp.zeros((seqs, experts, rank, hidden), bf16)
     b_gu = jnp.stack(
         [gate_up_columns(ffn_low[:, :experts], blank), gate_up_columns(blank, ffn_low[:, experts : 2 * experts])],
@@ -1393,86 +1314,39 @@
     ).reshape(seqs, 2 * experts * rank, 2 * hidden)
     a_d = jnp.pad(ffn_low[:, 2 * experts :].reshape(seqs, experts * rank, hidden), ((0, 0), (64, 0), (0, 0)))
     mixed, dx1b, dx1_own, n2, z_sum, g_gu, g_d = feed_forward(
-        x0, sum_out, dy, norm2_gain[None], wide_low,
+        x0, sum_out, dy, norm2_gain[None], wide,
         jnp.pad(router_ffn, ((0, 0), (0, 128 - experts))),
         widen_routes(route_f, experts), b_gu, a_d, z_o_gated, w_gate_up, w_down,
     )
-    g_gu = g_gu.reshape(seqs, experts, 2, rank, 2 * hidden)
+    grad_tokens, wide_a, wide_b, head_sum, gu_sum, d_sum = backward(
+        [
+            dx1b, dx1_own, x0, n1, n2, dy, kv_all, q_all, probs, ob, gates, z_q, z_kv, z_sum,
+            hot0, hot1, cosine, sine, norm1_gain[None], router_wide, b_q, b_kv_wide, a_o_wide, g_gu, g_d,
+        ],
+        [w_query, w_key_value, w_out, wide],
+    )
+    grad_wide = jnp.concatenate([wide_a, wide_b[:, : 704 - 512]], axis=1).T
+    back_order = np.argsort(np.array([q * wide_slots + s for q, s in order]))
+    grad_wide = grad_wide.reshape(seqs * wide_slots, rank, -1)[back_order]
+    grad_wide = grad_wide.reshape(seqs, wide_slots, rank, -1)[adapter_index]
+    head_sum = head_sum.reshape(-1, rank, width).astype(f32)
+    grad_heads = jnp.concatenate(
+        [
+            head_sum[: seqs * experts].reshape(seqs, experts, rank, width),
+            jnp.swapaxes(head_sum[8:12].reshape(2, seqs, rank, width), 0, 1),
+            head_sum[12:20].reshape(seqs, experts, rank, width),
+        ],
+        axis=1,
+    )[adapter_index]
+    gu_sum = gu_sum.reshape(seqs, experts, 2, rank, 768).astype(f32)
     grad_ffn = jnp.concatenate(
         [
-            jnp.concatenate([g_gu[:, :, 0, :, :640], g_gu[:, :, 0, :, 1280:1344]], axis=-1),
-            jnp.concatenate([g_gu[:, :, 1, :, 640:1280], g_gu[:, :, 1, :, 1344:]], axis=-1),
-            g_d[:, 64:].reshape(seqs, experts, rank, hidden),
+            gu_sum[:, :, 0, :, :704],
+            jnp.concatenate([gu_sum[:, :, 1, :, :640], gu_sum[:, :, 1, :, 704:]], axis=-1),
+            d_sum.reshape(seqs, experts, rank, hidden),
         ],
         axis=1,
-    )
-    dz_o = low_in(dx1b, 14, experts)
-    g_e = jnp.stack([dot(dx1b, w_out[e], 1, 1) for e in range(experts)], axis=1) + low_out(dz_o, a_o)
-    g_k = jnp.einsum("rke,reh->rkh", hot_a, g_e, precision=lax.Precision.HIGHEST)
-    dga = jnp.sum(g_k * ob.astype(f32), axis=-1)
-    dob = (g_k * ga[..., None]).astype(bf16)
-    dob_s = dob.reshape(seqs, block, -1, heads, HEAD_DIM)
-    delta = jnp.sum(dob_s.astype(f32) * o, axis=-1)
-    delta = jnp.transpose(delta, (0, 2, 3, 1))[..., None]
-    d_p = jnp.einsum("sqthd,skhd->sthqk", dob_s, kv_all[:, :, 1], preferred_element_type=f32)
-    d_s = (probs * (d_p - delta)).astype(bf16)
-    dqr = jnp.einsum("sthqk,skhd->sqthd", d_s, kv_all[:, :, 0], preferred_element_type=f32) * scale
-    dkr = jnp.einsum("sthqk,sqthd->skhd", d_s, q_s, preferred_element_type=f32) * scale
-    dvv = jnp.einsum("sthqk,sqthd->skhd", probs.astype(bf16), dob_s, preferred_element_type=f32)
-    dkv = jnp.concatenate([dkr, dvv], axis=2).reshape(seqs, length, 2 * width).astype(bf16)
-    dkv = halo_back(dkv)
-    dkv = dkv.reshape(rows, 2, heads, HEAD_DIM)
-    dkp = rope(dkv[:, 0], cosine[:, None], sine[:, None], -1.0).astype(bf16).reshape(rows, width)
-    dvp = dkv[:, 1].astype(bf16).reshape(rows, width)
-    dqp = rope(
-        dqr.reshape(rows, -1, heads, HEAD_DIM), cosine[:, None, None], sine[:, None, None], -1.0
-    ).astype(bf16).reshape(rows, -1, width)
-    dq_e = jnp.einsum("rke,rkh->reh", hot_a.astype(bf16), dqp, preferred_element_type=f32).astype(bf16)
-    dkv_p = jnp.stack([dkp, dvp], axis=1)
-    dz_q = low_back(dq_e, b_q)
-    dz_kv = low_back(dkv_p, b_kv)
-    a_qkv = jnp.transpose(wide[:, :, :6], (1, 2, 3, 0))
-    dz_qkv = jnp.concatenate([dz_q, dz_kv], axis=1)
-    dla = gates_back(ga, dga, hot_a)
-    dn1 = sum(dot(dq_e[:, e], w_query[e], 1, 1) for e in range(experts))
-    dn1 = dn1 + dot(dkv_p.reshape(rows, 2 * width), w_key_value.reshape(model, 2 * width), 1, 1)
-    dn1 = dn1 + low_sum(dz_qkv, a_qkv) + dot(dla.astype(bf16), router_attn, 1, 1)
-    back1 = norm_back(xf, norm1_gain, dn1)
-    dz_part = jnp.pad(dz_qkv.reshape(rows, -1).astype(bf16), ((0, 0), (0, 32)))
-    back_own, dz_sum = exchange([back1.astype(bf16), dz_part], ["rs_cols", "ar_rows"], 3)
-    dz_sum = dz_sum[:, :96].reshape(rows, 6, rank)
-    grad_tokens = (back_own + dx1_own).astype(bf16)
-    grad_heads = jnp.concatenate(
-        [low_grad(z_q, dq_e), low_grad(z_kv, dkv_p), low_grad(dz_o * ga_e[..., None], ob_e)], axis=1
-    )
-    def strided(a):
-        return lax.dynamic_slice_in_dim(
-            a.reshape(rows, n_ctx, n_tp, model // (n_ctx * n_tp)), tp_rank, 1, 2
-        ).reshape(seqs, block, -1)
-
-    def wide_grad(z, v):
-        return jnp.einsum("sbcr,sbm->mscr", split(z).astype(bf16), strided(v), preferred_element_type=f32)
-
-    wide_terms = jnp.concatenate(
-        [
-            wide_grad(dz_sum, n1),
-            wide_grad(z_sum[:, :128].reshape(rows, experts, 2, rank).swapaxes(1, 2).reshape(rows, 2 * experts, rank), n2),
-            wide_grad(z_sum[:, 128:192].reshape(rows, experts, rank), dx1b),
-            wide_grad(z_sum[:, 192:].reshape(rows, experts, rank), dy),
-        ],
-        axis=2,
-    ).reshape(-1, seqs * wide_slots * rank)
-    head_rows = seqs * grad_heads.shape[1] * rank // N_CTX
-    head_terms = jnp.pad(
-        grad_heads.reshape(N_CTX, head_rows, width).astype(bf16), ((0, 0), (0, 32 - head_rows), (0, 0))
-    )
-    grad_wide, head_sum = reduce_ctx(
-        [wide_terms.reshape(N_CTX, -1, seqs * wide_slots * rank).astype(bf16), head_terms],
-        [False, True],
-    )
-    grad_wide = grad_wide.T.reshape(seqs, wide_slots, rank, -1)[adapter_index]
-    grad_heads = head_sum[:, :head_rows].astype(f32).reshape(grad_heads.shape)[adapter_index]
-    grad_ffn = lax.psum(grad_ffn.astype(bf16), "ctx").astype(f32)[adapter_index]
+    )[adapter_index]
     mixed = mixed.reshape(seqs, block, part)
     grad_tokens = grad_tokens.reshape(seqs, block, part)
     return (mixed, grad_tokens, grad_wide, grad_heads, grad_ffn)

time: 645 us -> 454 us (0.70)
  local copies, waits for them, and re-layouts: 158 us -> 21.2 us
  matrix products: 23.7 us -> 0 us
  between operations: 16.8 us -> 1.1 us
  other arithmetic: 21.8 us -> 7.73 us
    another operation x60 -> x2, local copies, waits for them, and re-layouts: 70.9 us -> 0.02 us  [the longest x49 70.8 us: shards(): jnp.stack([wide[:, place[q, s]:place[q, s] + rank] for s in range(wide_sl...]
    dot_general x24 -> x0, matrix products: 22.6 us -> none  [the longest x10 10.7 us: dot(): lax.dot_general(a, b, (((ca,), (cb,)), ((), ())), preferred_element_type=...]
    unnamed x307 -> x43, local copies, waits for them, and re-layouts: 22.9 us -> 3.25 us
    convert_element_type x11 -> x0, local copies, waits for them, and re-layouts: 13.3 us -> none  [the longest x2 6.87 us: shards(): wide_terms.reshape(N_CTX, -1, seqs * wide_slots * rank).astype(bf16)]
    slice x12 -> x2, local copies, waits for them, and re-layouts: 9.44 us -> 0.03 us  [the longest x1 0.02 us: shards(): head_sum[:seqs * experts].reshape(seqs, experts, rank, width)]
    reshape x17 -> x3, local copies, waits for them, and re-layouts: 9.26 us -> 0.43 us  [the longest x1 0.27 us: shards(): grad_wide = grad_wide.reshape(seqs, wide_slots, rank, -1)[adapter_index]]
    pallas_call x3 -> x1, Pallas kernels: 91.2 us -> 95.6 us  [backward(): pl.pallas_call(backward_kernel, out_shape=(shape((rows, part), bf16), sha...]
  transfers between devices with their start and end apart: 1 -> 0, of which waited for: 0 -> 0; matrix products, arithmetic and copies ran while one was open for 25% -> 0% of each run, Pallas kernels for 14% -> 0%
where the time goes in v3:
time: 454 us; the launch traced here: 453 us
  Pallas kernels  423 us (93%)
  local copies, waits for them, and re-layouts  21.2 us (5%)
  other arithmetic  7.73 us (2%)
    pallas_call x1, Pallas kernels, attention(): pl.pallas_call(attention_kernel, out_shape=any_out + vmem_out, in_specs=[...  247 us
    pallas_call x1, Pallas kernels, backward(): pl.pallas_call(backward_kernel, out_shape=(shape((rows, part), bf16), sha...  95.6 us
    pallas_call x1, Pallas kernels, feed_forward(): pl.pallas_call(ffn_kernel, out_shape=(shape((rows, part), bf16), shape((r...  80.5 us

profile of v3, /device:TPU:1, one launch (start us, length us, event | category | flops | bytes accessed | tf_op | source)
XLA Modules:
  0.0 453.4 jit_solution(8832212671517682506)
XLA Ops:
  0.7 0.9 reduce_window_sum.12
  1.6 0.8 fusion.5
  3.1 0.8 pad_maximum_fusion.4.sine
  3.9 0.8 pad_maximum_fusion.3.cosine
  4.7 0.8 broadcast_in_dim.60.q_doc
  8.5 2.3 concatenate.36.s_gu
  11.3 0.7 pad.18.a_o
  13.6 0.7 copy.68
  14.3 0.8 fusion
  15.5 0.9 pad.17.router
  16.4 0.7 copy.78
  17.1 247.2 %attention.1 = (bf16[4,2048,256]{2,1,0:T(8,128)(2,1)}, bf16[2048,512]{1,0:T(8,128)(2,1)}, bf16[4,256,2048]{2,1,0:T(8,128)(2,1)}, bf16[4,2048,1408]{2,1,0:T(8,128...) custom-call(bf16[4,128,256]{2,1,0:T(8,128)(2,1)} %s_q.1, ...), custom_call_target="tpu_custom_call" | custom-call | tf_op jit(solution)/shard_map/attention/pallas_call | solution.py:760
  265.4 0.9 copy.59
  266.3 0.8 pad.20.a_d
  267.4 0.9 pad.19.router
  268.3 0.8 convert_reduce_fusion.hot
  269.1 80.5 %feed_forward.1 = (bf16[256,256]{1,0:T(8,128)(2,1)}, bf16[256,2048]{1,0:T(8,128)(2,1)}, f32[256,256]{1,0:T(8,128)}, bf16[256,2048]{1,0:T(8,128)(2,1)}, bf16[256,...) custom-call(bf16[256,2048]{1,0:T(8,128)(2,1)} %get-tuple-element.36.x0, ...), custom_call_target="tpu_custom_call" | custom-call | tf_op jit(solution)/shard_map/feed_forward/pallas_call | solution.py:333
  349.6 95.6 %backward.1 = (bf16[256,256]{1,0:T(8,128)(2,1)}, f32[16,512]{1,0:T(8,128)}, f32[16,256]{1,0:T(8,128)}, bf16[16,32,256]{2,1,0:T(8,128)(2,1)}, bf16[16,16,768]{2,1,0:T(8,128)(2,1)}, /*index=5*/f32[16,8,704]{2,1,0:T(8,128)}) custom-call(bf16[256,2048]{1,0:T(8,128)(2,1)} %get-tuple-element.44.dx1, f32[256,256]{1,0:T(8,128)} %get-tuple-element.45.dx1_own, ...), custom_call_target="tpu_custom_call" | custom-call | tf_op jit(solution)/shard_map/backward/pallas_call | solution.py:1164
  445.3 1.1 convert.1
  446.7 1.6 gather_fusion.7
  448.5 1.3 gather_fusion.6
  450.9 1.3 gather_fusion.5
  452.1 0.7 copy.83
  452.8 0.7 copy.84
  (93 shorter events, 8.9 us)
Async XLA Ops:
  0.6 5.6 %copy-start.17 = (s32[2]{0:T(128)S(1)}, s32[2]{0:T(128)}, u32[]{:S(2)}) copy-start(s32[2]{0:T(128)} %param.38) | copy-start | bytes 28
  0.6 5.7 %copy-start.4 = (f32[2,10,16,256]{3,2,1,0:T(8,128)S(1)}, f32[2,10,16,256]{3,2,1,0:T(8,128)}, u32[]{:S(2)}) copy-start(f32[2,10,16,256]{3,2,1,0:T(8,128)} %param.33) | copy-start | bytes 983044
  2.6 5.0 %copy-start = (bf16[4,128,2,704]{1,3,2,0:T(8,128)(2,1)S(1)}, bf16[4,128,2,704]{1,3,2,0:T(8,128)(2,1)}, u32[]{:S(2)}) copy-start(bf16[4,128,2,704]{1,3,2,0:T(8,128)(2,1)} %param.30) | copy-start | bytes 4325380
  8.4 3.6 copy-start.5
  10.7 2.2 copy-start.16
  10.7 3.6 copy-start.14
  10.7 4.4 copy-start.10
  13.0 3.4 copy-start.6
  17.1 247.2 %copy-start.1 = (f32[2,12,16,704]{3,2,1,0:T(8,128)S(1)}, f32[2,12,16,704]{3,2,1,0:T(8,128)}, u32[]{:S(2)}) copy-start(f32[2,12,16,704]{3,2,1,0:T(8,128)} %param.34) | copy-start | bytes 3244036
  265.4 1.7 copy-start.11
  266.3 2.0 copy-start.13
  445.3 1.3 copy-start.3
  446.7 1.7 copy-start.2
  448.4 1.4 copy-start.9
  448.4 1.4 copy-start.12
  448.4 1.6 copy-start.15
  449.8 2.4 copy-start.7
  449.9 2.8 copy-start.8

commit v4 on v3

v4 whole, which is shorter than its diff:
```python
import functools

import jax
import numpy as np
import jax.numpy as jnp
from jax import lax
from jax.experimental import pallas as pl
from jax.experimental.pallas import tpu as pltpu
from jax.sharding import PartitionSpec as P

HEAD_DIM = 128
WINDOW = 1024
eps = 1e-06
big_negative = -1e30
bf16 = jnp.bfloat16
f32 = jnp.float32

MESH = pl.DeviceIdType.MESH
ANY = pl.BlockSpec(memory_space=pl.ANY)
VMEM = pl.BlockSpec(memory_space=pltpu.VMEM)
N_CTX, N_TP = 16, 8
FAR = 4
PAST = 8


def region(kind, ref, owner, low, high):
    rows = pl.ds(pl.multiple_of(owner * 128 + 32 * low, 32), 32 * (high - low))
    cols = pl.ds(pl.multiple_of(owner * 128, 128), 128)
    if kind == "rows":
        return ref.at[pl.ds(low, high - low), cols, :]
    if kind == "flat":
        return ref.at[rows, :]
    if kind == "cols":
        return ref.at[pl.ds(low, high - low), :, cols]
    if high - low == 1:
        half = ref.shape[1] // 2
        return ref.at[low // 2, pl.ds(half * (low % 2), half), cols]
    return ref.at[pl.ds(low // 2, (high - low) // 2), :, cols]


def own_part(kind, ref, low, high):
    if kind == "flat":
        return ref.at[pl.ds(32 * low, 32 * (high - low)), :]
    if kind == "pair":
        return ref
    return ref.at[pl.ds(low, high - low)]


def tp_part(kind, ref, rank, size):
    if kind == "cols":
        return ref.at[:, pl.ds(pl.multiple_of(rank * size, size), size)]
    return ref.at[pl.ds(pl.multiple_of(rank * size, size), size), :]


def rms_scale(values, gain):
    return values * lax.rsqrt(jnp.mean(values * values, axis=-1, keepdims=True) + eps) * gain


def doc_layout(doc_lengths, positions):
    docs = doc_lengths.shape[1]
    upto = np.tril(np.ones((docs, docs), np.int32))
    ends = jnp.sum(doc_lengths[:, None, :] * upto[None], axis=2)
    passed = positions[None, :, None] >= ends[:, None, :]
    doc_ids = jnp.sum(passed.astype(jnp.int32), axis=2)
    starting = jnp.sum(jnp.where(passed, doc_lengths[:, None, :], 0), axis=2)
    inside = positions[None, :] < ends[:, -1:]
    doc_ids = jnp.where(inside, doc_ids, -1 - positions[None, :])
    return (doc_ids, positions[None, :] - starting)


def dot(a, b, ca=1, cb=0):
    return lax.dot_general(a, b, (((ca,), (cb,)), ((), ())), preferred_element_type=f32)


class Scatter:
    def __init__(self, parts, held, relay, send, recv, row):
        self.me, self.tp = lax.axis_index("ctx"), lax.axis_index("tp")
        self.parts, self.held, self.relay_buffer = parts, held, relay
        self.send, self.recv, self.row = send, recv, row

    def copy_to(self, d, to):
        return pltpu.make_async_remote_copy(
            src_ref=self.parts.at[d],
            dst_ref=self.held.at[d],
            send_sem=self.send.at[self.row, d],
            recv_sem=self.recv.at[self.row, d],
            device_id=(self.me, self.tp ^ to),
            device_id_type=MESH,
        )

    def copy(self, d):
        if d != FAR:
            return self.copy_to(d, d % FAR)
        return pltpu.make_async_remote_copy(
            src_ref=self.relay_buffer,
            dst_ref=self.held.at[FAR],
            send_sem=self.send.at[self.row, FAR],
            recv_sem=self.recv.at[self.row, FAR],
            device_id=(self.me, self.tp ^ FAR),
            device_id_type=MESH,
        )

    def relay(self):
        total = self.parts[FAR].astype(f32)
        for d in range(FAR + 1, N_TP):
            self.copy(d).wait_recv()
            total = total + self.held[d].astype(f32)
        self.relay_buffer[...] = total.astype(bf16)
        self.copy(FAR).start()

    def total(self, own):
        for d in range(1, FAR + 1):
            self.copy(d).wait_recv()
            own = own + self.held[d].astype(f32)
        return own

    def sent(self):
        for d in range(1, N_TP):
            self.copy(d).wait_send()


class Spread:
    def __init__(self, source, place, send, recv, row):
        self.me, self.tp = lax.axis_index("ctx"), lax.axis_index("tp")
        self.source, self.place = source, place
        self.send, self.recv, self.row = send, recv, row

    def copy(self, d, owner, to, source=None):
        return pltpu.make_async_remote_copy(
            src_ref=self.place(owner) if source is None else source,
            dst_ref=self.place(owner),
            send_sem=self.send.at[self.row, d],
            recv_sem=self.recv.at[self.row, d],
            device_id=(self.me, self.tp ^ to),
            device_id_type=MESH,
        )

    def start(self):
        for d in (FAR, 1, 2, 3):
            self.copy(d, self.tp, d, self.source).start()

    def relay(self):
        self.copy(FAR, self.tp ^ FAR, FAR).wait_recv()
        for d in (1, 2, 3):
            self.copy(FAR + d, self.tp ^ FAR, d).start()

    def wait(self):
        for d in (1, 2, 3):
            self.copy(d, self.tp ^ d, d).wait_recv()
            self.copy(FAR + d, self.tp ^ (FAR + d), d).wait_recv()

    def sent(self):
        for d in (FAR, 1, 2, 3):
            self.copy(d, self.tp, d, self.source).wait_send()
        for d in (1, 2, 3):
            self.copy(FAR + d, self.tp ^ FAR, d).wait_send()


class CtxSum:
    def __init__(self, source, core_held, held, out, send, recv, row):
        self.me, self.tp = lax.axis_index("ctx"), lax.axis_index("tp")
        self.core, self.chip = lax.rem(self.me, 2), self.me // 2
        self.source, self.core_held, self.held, self.out = source, core_held, held, out
        self.send, self.recv, self.row = send, recv, row

    def copy(self, item, src, dst, to):
        return pltpu.make_async_remote_copy(
            src_ref=src,
            dst_ref=dst,
            send_sem=self.send.at[self.row, item],
            recv_sem=self.recv.at[self.row, item],
            device_id=(to, self.tp),
            device_id_type=MESH,
        )

    def to_core(self):
        return self.copy(0, self.source.at[1 - self.core], self.core_held, self.me ^ 1)

    def to_chip(self, d):
        return self.copy(
            d, self.source.at[self.core, self.chip ^ d], self.held.at[d], self.me ^ (2 * d)
        )

    def spread(self, d, chip):
        there = self.out.at[self.core, chip]
        return self.copy(7 + d, there, there, self.me ^ (2 * d))

    def back_to_core(self, core):
        return self.copy(15, self.out.at[core], self.out.at[core], self.me ^ 1)

    def start(self):
        self.to_core().start()

    def chips(self):
        self.to_core().wait()
        self.source[self.core] = (
            self.source[self.core].astype(f32) + self.core_held[...].astype(f32)
        ).astype(self.source.dtype)
        for d in range(1, 8):
            self.to_chip(d).start()

    def total(self):
        total = self.source[self.core, self.chip].astype(f32)
        for d in range(1, 8):
            self.to_chip(d).wait_recv()
            total = total + self.held[d].astype(f32)
        for d in range(1, 8):
            self.to_chip(d).wait_send()
        return total

    def again(self):
        self.out[self.core, self.chip] = self.total().astype(self.out.dtype)
        for d in range(1, 8):
            self.spread(d, self.chip).start()

    def other_core(self):
        for d in range(1, 8):
            self.spread(d, self.chip ^ d).wait_recv()
            self.spread(d, self.chip).wait_send()
        self.back_to_core(self.core).start()

    def finish(self):
        self.back_to_core(1 - self.core).wait_recv()
        self.back_to_core(self.core).wait_send()


def dot_nt(a, b):
    return dot(a, b, 1, 1)


def dot_tn(a, b):
    return dot(a, b, 0, 0)


def by_seq(rows, f):
    half = rows.shape[0] // 2
    return jnp.concatenate([f(0, rows[:half]), f(1, rows[half:])], axis=0)


def column_of(values, lane, e):
    return jnp.sum(jnp.where(lane == e, values, 0.0), axis=1, keepdims=True)


def greet(targets):
    barrier = pltpu.get_barrier_semaphore()
    for device in targets:
        pl.semaphore_signal(barrier, inc=1, device_id=device, device_id_type=MESH)
    pl.semaphore_wait(barrier, len(targets))


def masked_gates(logits, hot):
    largest = jnp.max(jnp.where(hot > 0, logits, big_negative), axis=1, keepdims=True)
    powers = jnp.where(hot > 0, jnp.exp(logits - largest), 0.0)
    return powers / jnp.sum(powers, axis=1, keepdims=True)


def ffn_kernel(
    x0, attn, dy, gain, wide, router, table, b_gu, a_d, z_o, w_gu_hbm, w_d_hbm,
    ff_parts, ff_own, dx1, dx1_own, n2, z_sum, gu_out, d_out,
    w_gu, w_d, hg, dgu, dh_tmp, z_gu, dz_d, z_part, parts, relay, own, held, z_held, dots, tails, inverse,
    g_gu, g_d, gu_src, gu_core, gu_held, d_src, d_core, d_held,
    load, send, recv, ctx_send, ctx_recv,
):
    me, tp = lax.axis_index("ctx"), lax.axis_index("tp")
    hot = table.at[:, 512:640]
    rows, model = x0.shape
    experts = w_gu.shape[0]
    part = model // N_TP
    greet([(me ^ d, tp) for d in range(1, N_CTX)] + [(me, tp ^ d) for d in range(1, N_TP)])

    def fetch(e):
        return (
            pltpu.make_async_copy(w_gu_hbm.at[e], w_gu.at[e], load.at[0, e]),
            pltpu.make_async_copy(w_d_hbm.at[e], w_d.at[e], load.at[1, e]),
        )

    for e in range(experts):
        for c in fetch(e):
            c.start()

    step = 32

    def normalize(i, carry):
        at = pl.ds(pl.multiple_of(i * step, step), step)
        x = x0[at, :].astype(f32) + attn[at, :].astype(f32)
        r = lax.rsqrt(jnp.mean(x * x, axis=1, keepdims=True) + eps)
        inverse[at, :] = jnp.broadcast_to(r, (step, 128))
        n2[at, :] = (x * r * gain[...]).astype(bf16)
        return carry

    lax.fori_loop(0, rows // step, normalize, 0)
    lane = lax.broadcasted_iota(jnp.int32, (rows, 128), 1)
    gates = masked_gates(dot(n2[...], router[...]), hot[...])
    pair_lane = lax.broadcasted_iota(jnp.int32, (rows, 256), 1)
    mine = pair_lane // 128 == lax.broadcasted_iota(jnp.int32, (rows, 256), 0) // (rows // 2)
    pair_lane = pair_lane % 128
    z_gu[...] = jnp.where(mine, dot(n2[...], wide[:, :256]), 0.0).astype(bf16)
    dz_d[...] = jnp.where(mine, dot(dy[...], wide[:, 256:512]), 0.0).astype(bf16)
    g_gu[...] = jnp.zeros_like(g_gu)
    g_d[...] = jnp.zeros_like(g_d)
    zero = jnp.zeros((rows, 256), f32)

    def expert(e, carry):
        d_gates, dz_gu, z_d = carry
        for c in fetch(e):
            c.wait()
        gate = column_of(gates, lane, e)
        z_in = jnp.where(pair_lane // 32 == e, z_gu[...].astype(f32), 0.0).astype(bf16)
        dz_in = jnp.where(pair_lane // 16 == 4 + e, dz_d[...].astype(f32), 0.0).astype(bf16)
        dh_tmp[:, :704] = dot_nt(dy[...], w_d[e]) + dot(dz_in, a_d[...])
        pre = dot(n2[...], w_gu[e]) + dot(z_in, b_gu[...])

        def tile(g, u, d):
            sg = jax.nn.sigmoid(g)
            silu = g * sg
            h = silu * u
            dg = d * gate
            return h, (dg * u * sg * (1.0 + g * (1.0 - sg))), dg * silu, h * d

        h, dgp, dup, hd = tile(pre[:, :640], pre[:, 640:1280], dh_tmp[:, :640])
        hg[e, :, :640] = (h * gate).astype(bf16)
        dgu[e, :, :640] = dgp.astype(bf16)
        dgu[e, :, 640:1280] = dup.astype(bf16)
        dgf = jnp.sum(hd, axis=1, keepdims=True)
        last = pre[:, 1280:]
        h, dgp, dup, hd = tile(last, pltpu.roll(last, 64, 1), dh_tmp[:, 640:])
        hg[e, :, 640:] = (h * gate).astype(bf16)[:, :64]
        dgu[e, :, 1280:] = jnp.where(lane < 64, dgp, pltpu.roll(dup, 64, 1)).astype(bf16)
        dgf = dgf + jnp.sum(jnp.where(lane < 64, hd, 0.0), axis=1, keepdims=True)
        d_gates = d_gates + jnp.where(lane == e, dgf, 0.0)
        keep = mine & (pair_lane // 32 == e)
        dz_gu = dz_gu + jnp.where(keep, dot_nt(dgu[e], b_gu[...]), 0.0)
        keep = mine & (pair_lane // 16 == 4 + e)
        z_d = z_d + jnp.where(keep, dot_nt(hg[e], a_d[...]), 0.0)
        g_gu[...] += dot_tn(z_in, dgu[e])
        g_d[...] += dot_tn(dz_in, hg[e])
        return d_gates, dz_gu, z_d

    d_gates, dz_gu, z_d = lax.fori_loop(
        0, experts, expert, (jnp.zeros((rows, 128), f32), zero, zero)
    )
    d_logits = gates * (d_gates - jnp.sum(gates * d_gates, axis=1, keepdims=True))
    d_logits = d_logits.astype(bf16)
    dz_gu, z_d = dz_gu.astype(bf16), z_d.astype(bf16)
    z_part[:, :128] = dz_gu[:, :128] + dz_gu[:, 128:]
    z_part[:, 128:] = z_o[...] + z_d[:, :128] + z_d[:, 128:]

    for i in range(N_CTX):
        s, slot = i // 8, i % 8
        at = slice(128 * s + 16 * slot, 128 * s + 16 * slot + 16)
        cols = 640 * (slot % 2)
        gu_src[i % 2, i // 2, :, :640] = g_gu[at, cols : cols + 640].astype(bf16)
        gu_src[i % 2, i // 2, :, 640:] = g_gu[at, 1280:].astype(bf16)
        first = 128 * s + 64 + 8 * slot
        d_src[i % 2, i // 2] = g_d[first : first + 8, :]
    gu_sum = CtxSum(gu_src, gu_core, gu_held, gu_out, ctx_send, ctx_recv, 0)
    d_sum = CtxSum(d_src, d_core, d_held, d_out, ctx_send, ctx_recv, 1)
    gu_sum.start()
    d_sum.start()
    scatter = Scatter(parts, held, relay, send, recv, 0)

    def x_at(at):
        return x0[:, at].astype(f32) + attn[:, at].astype(f32)

    def piece(j, along):
        d = lax.rem(j + FAR + 1, N_TP)
        peer = tp ^ d
        at = pl.ds(pl.multiple_of(peer * part, part), part)
        w_rows = wide[at, :256]
        dn = dot_nt(d_logits, router[at, :])
        dn = dn + dot_nt(dz_gu, w_rows)
        for e in range(experts):
            dn = dn + dot_nt(dgu[e], w_gu[e, at, :])
        parts[d] = dn.astype(bf16)

        @pl.when((d != 0) & (d != FAR))
        def _():
            scatter.copy_to(d, lax.rem(d, FAR)).start()

        @pl.when(d == 0)
        def _():
            own[...] = dn

        return along + jnp.sum(dn * gain[:, at] * x_at(at), axis=1, keepdims=True)

    def out_piece(d, carry):
        peer = tp ^ d
        at = pl.ds(pl.multiple_of(peer * part, part), part)
        w_rows = wide[at, 256:512]
        ff = dot_nt(z_d, w_rows)
        for e in range(experts):
            ff = ff + dot(hg[e], w_d[e, :, at])
        ff_parts[d] = ff.astype(bf16)

        @pl.when(d == 0)
        def _():
            ff_own[...] = ff + x_at(at)

        return carry

    z_rows = rows // N_TP

    def z_region(ref, rank):
        return ref.at[pl.ds(pl.multiple_of(rank * z_rows, z_rows), z_rows), :]

    def z_scatter(d):
        return pltpu.make_async_remote_copy(
            src_ref=z_region(z_part, tp ^ d),
            dst_ref=z_held.at[d],
            send_sem=send.at[2, d],
            recv_sem=recv.at[2, d],
            device_id=(me, tp ^ d),
            device_id_type=MESH,
        )

    def z_spread(d, rank):
        return pltpu.make_async_remote_copy(
            src_ref=z_region(z_sum, rank),
            dst_ref=z_region(z_sum, rank),
            send_sem=send.at[3, d],
            recv_sem=recv.at[3, d],
            device_id=(me, tp ^ d),
            device_id_type=MESH,
        )

    def columns(ref, rank):
        return ref.at[:, pl.ds(pl.multiple_of(rank * part, part), part)]

    def tail(d, rank):
        return pltpu.make_async_remote_copy(
            src_ref=tails.at[rank],
            dst_ref=tails.at[rank],
            send_sem=send.at[5, d],
            recv_sem=recv.at[5, d],
            device_id=(me, tp ^ d),
            device_id_type=MESH,
        )

    along = lax.fori_loop(0, N_TP, piece, jnp.zeros((rows, 1), f32))
    dots[...] = jnp.broadcast_to(along, dots.shape)
    tails[tp] = jnp.transpose(dots[...])[:8, :]
    for d in range(1, N_TP):
        tail(d, tp).start()
        z_scatter(d).start()
    scatter.relay()
    gu_sum.chips()
    d_sum.chips()
    lax.fori_loop(0, N_TP, out_piece, 0)
    at = pl.ds(pl.multiple_of(tp * part, part), part)
    total = scatter.total(own[...]) * gain[:, at]
    for d in range(1, N_TP):
        tail(d, tp ^ d).wait_recv()
    whole = tails[0]
    for d in range(1, N_TP):
        whole = whole + tails[d]
    dots[...] = jnp.transpose(jnp.broadcast_to(whole[:1], (128, rows)))
    r = inverse[:, :1]
    total = dy[:, at].astype(f32) + r * total - x_at(at) * r**3 * (dots[:, :1] * (1.0 / model))
    dx1_own[...] = total
    columns(dx1, tp)[...] = total.astype(bf16)
    spread = Spread(None, lambda rank: columns(dx1, rank), send, recv, 4)
    spread.start()
    gu_sum.again()
    d_sum.again()
    total = z_region(z_part, tp)[...].astype(f32)
    for d in range(1, N_TP):
        z_scatter(d).wait_recv()
        total = total + z_held[d].astype(f32)
    z_region(z_sum, tp)[...] = total.astype(bf16)
    for d in range(1, N_TP):
        z_spread(d, tp).start()
    spread.relay()
    gu_sum.other_core()
    d_sum.other_core()
    spread.wait()
    gu_sum.finish()
    d_sum.finish()
    scatter.sent()
    spread.sent()
    for d in range(1, N_TP):
        z_scatter(d).wait_send()
        z_spread(d, tp ^ d).wait_recv()
        z_spread(d, tp).wait_send()
        tail(d, tp).wait_send()


def feed_forward(x0, attn, dy, gain, wide, router, table, b_gu, a_d, z_o, w_gu, w_d):
    rows, model = x0.shape
    part = model // N_TP
    experts, _, cols = w_gu.shape
    hidden = w_d.shape[1]
    shape = jax.ShapeDtypeStruct
    return pl.pallas_call(
        ffn_kernel,
        out_shape=(
            shape((N_TP, rows, part), bf16),
            shape((rows, part), f32),
            shape((rows, model), bf16),
            shape((rows, part), f32),
            shape((rows, model), bf16),
            shape((rows, 256), bf16),
            shape((2, 8, 16, 768), bf16),
            shape((2, 8, 8, hidden), f32),
        ),
        in_specs=[VMEM] * 10 + [ANY] * 2,
        out_specs=tuple([VMEM] * 8),
        scratch_shapes=[
            pltpu.VMEM(w_gu.shape, bf16),
            pltpu.VMEM(w_d.shape, bf16),
            pltpu.VMEM((experts, rows, hidden), bf16),
            pltpu.VMEM((experts, rows, cols), bf16),
            pltpu.VMEM((rows, 768), f32),
            pltpu.VMEM((rows, 256), bf16),
            pltpu.VMEM((rows, 256), bf16),
            pltpu.VMEM((rows, 256), bf16),
            pltpu.VMEM((N_TP, rows, part), bf16),
            pltpu.VMEM((rows, part), bf16),
            pltpu.VMEM((rows, part), f32),
            pltpu.VMEM((N_TP, rows, part), bf16),
            pltpu.VMEM((N_TP, rows // N_TP, 256), bf16),
            pltpu.VMEM((rows, 128), f32),
            pltpu.VMEM((N_TP, 8, rows), f32),
            pltpu.VMEM((rows, 128), f32),
            pltpu.VMEM(b_gu.shape, f32),
            pltpu.VMEM(a_d.shape, f32),
            pltpu.VMEM((2, 8, 16, 768), bf16),
            pltpu.VMEM((8, 16, 768), bf16),
            pltpu.VMEM((8, 16, 768), bf16),
            pltpu.VMEM((2, 8, 8, hidden), f32),
            pltpu.VMEM((8, 8, hidden), f32),
            pltpu.VMEM((8, 8, hidden), f32),
            pltpu.SemaphoreType.DMA((2, experts)),
            pltpu.SemaphoreType.DMA((6, N_TP)),
            pltpu.SemaphoreType.DMA((6, N_TP)),
            pltpu.SemaphoreType.DMA((2, 16)),
            pltpu.SemaphoreType.DMA((2, 16)),
        ],
        compiler_params=pltpu.CompilerParams(
            collective_id=2, has_side_effects=True, vmem_limit_bytes=63 << 20
        ),
        name="feed_forward",
    )(x0, attn, dy, gain, wide, router, table, b_gu, a_d, z_o, w_gu, w_d)


def widen_routes(routes, experts):
    lane = jnp.arange(128, dtype=jnp.int32)
    return jnp.sum((routes[..., None] == lane).astype(f32), axis=1)


def gate_up_columns(gate, up):
    return jnp.concatenate([gate[..., :640], up[..., :640], gate[..., 640:], up[..., 640:]], axis=-1)


def attention_kernel(
    s_q, s_kv, s_o, s_gu, s_d, tokens, cotangent, s_wide,
    gain, router, table, k_doc, b_q, b_kv, a_o,
    g_q, g_kv, g_o, g_gu, g_d, g_wide, wide_mid, dy,
    x0, attn, n1, kv_all, q_all, probs, ob, z_o, z_q, z_kv, gates,
    w_q, w_kv, w_o, wide, parts, relay, own, held,
    send, recv, local, tp_send, tp_recv, tp_local, kv_send, kv_recv, load, sum_send, sum_recv,
):
    me, tp = lax.axis_index("ctx"), lax.axis_index("tp")
    core, side = me ^ 1, me ^ 2
    up, down, far = lax.rem(me + 4, 16), lax.rem(me + 12, 16), lax.rem(me + 8, 16)
    on_core, on_side = lax.rem(me, 2), lax.rem(me // 2, 2)
    cosine, sine, hot0, hot1 = (table.at[:, 128 * i : 128 * i + 128] for i in range(4))
    q_doc = table.at[:, 640:768]
    rows, model = x0.shape
    part = model // N_TP
    half = rows // 2
    experts = w_q.shape[0]
    width = w_q.shape[2]
    heads = width // HEAD_DIM
    span = (PAST + 1) * half
    greet([(d, tp) for d in (core, side, up, down, far)] + [(me, tp ^ d) for d in range(1, N_TP)])

    kinds = ["flat", "flat", "rows", "cols"] + ["flat"] * experts + ["pair"] * (experts // 2)
    src = [s_kv, wide_mid, s_q, s_o] + [s_gu.at[e] for e in range(experts)]
    dst = [g_kv, g_wide, g_q, g_o] + [g_gu.at[e] for e in range(experts)]
    src += [s_d.at[pl.ds(e, 2)] for e in range(0, experts, 2)]
    dst += [g_d.at[pl.ds(e, 2)] for e in range(0, experts, 2)]
    tp_src, tp_dst, tp_kinds = [tokens, s_wide, cotangent], [x0, wide_mid, dy], ["cols", "rows", "cols"]
    started, staying = [], [None] * len(kinds)
    counter = [0] * len(kinds)

    def place_of(i):
        size = tp_src[i].shape[1 if tp_kinds[i] == "cols" else 0]
        return lambda rank: tp_part(tp_kinds[i], tp_dst[i], rank, size)

    tp_all = [Spread(tp_src[i], place_of(i), tp_send, tp_recv, i) for i in range(3)]

    def tp_own(i):
        return pltpu.make_async_copy(tp_src[i], place_of(i)(tp), tp_local.at[i])

    def tp_start(i):
        tp_all[i].start()
        tp_own(i).start()

    def tp_wait(i):
        tp_all[i].wait()
        tp_own(i).wait()

    def copy(t, item, owner, low, high, to, slot, own_shard):
        there = region(kinds[t], dst[t], owner, low, high)
        return pltpu.make_async_remote_copy(
            src_ref=own_part(kinds[t], src[t], low, high) if own_shard else there,
            dst_ref=there,
            send_sem=send.at[t, slot],
            recv_sem=recv.at[t, item],
            device_id=(to, tp),
            device_id_type=MESH,
        )

    def go(t, item, owner, low, high, to, own_shard=False):
        c = copy(t, item, owner, low, high, to, counter[t], own_shard)
        counter[t] += 1
        c.start()
        started.append(c)

    cuts = [2, 2, 3, 3] + [2] * 6

    def arrive(t, item):
        cut = cuts[t]
        mid = cut // 2 if t % 2 else (cut + 1) // 2
        return {
            0: (side, 0, 4),
            1: (down, 0, 4),
            2: (up, 0, 4),
            3: (down ^ 2, 0, cut),
            4: (up ^ 2, 0, cut),
            5: (far, 2, 4),
            6: (far, 0, 2),
            7: (far ^ 2, mid, cut),
            8: (far ^ 2, 0, mid),
            9: (down ^ 2, cut, 4),
            10: (up ^ 2, cut, 4),
            11: (far ^ 2, cut, 4),
        }[item]

    def got(t, item):
        owner, low, high = arrive(t, item)
        copy(t, item, owner, low, high, core, 0, False).wait_recv()
        go(t, 12 + item, owner, low, high, core)

    def first(t):
        go(t, 0, me, 0, 4, side, True)
        go(t, 2, me, 0, 4, down, True)
        go(t, 1, me, 0, 4, up, True)
        go(t, 24, me, 0, 4, core, True)
        c = pltpu.make_async_copy(src[t], region(kinds[t], dst[t], me, 0, 4), local.at[t])
        c.start()
        staying[t] = c

    def second(t):
        got(t, 0)
        go(t, 3, side, 0, cuts[t], up)
        go(t, 4, side, 0, cuts[t], down)
        got(t, 1)
        go(t, 5, down, 2, 4, up)
        go(t, 9, down, cuts[t], 4, side)
        got(t, 2)
        go(t, 6, up, 0, 2, down)
        go(t, 10, up, cuts[t], 4, side)

    def third(t):
        got(t, 3)
        _, low, high = arrive(t, 7)
        go(t, 7, down ^ 2, low, high, up)
        got(t, 4)
        _, low, high = arrive(t, 8)
        go(t, 8, up ^ 2, low, high, down)
        got(t, 5)
        got(t, 6)
        go(t, 11, far, cuts[t], 4, side)

    def fourth(t):
        for item in range(7, 12):
            got(t, item)

    def finish(t):
        for item in range(12):
            owner, low, high = arrive(t, item)
            copy(t, 12 + item, owner ^ 1, low, high, core, 0, False).wait_recv()
        copy(t, 24, core, 0, 4, core, 0, False).wait_recv()

    tp_start(0)
    tp_start(1)
    for t in (0, 2):
        first(t)
    tp_all[0].relay()
    tp_all[1].relay()
    tp_wait(1)
    first(1)
    tp_wait(0)
    step = 32

    def normalize(i, carry):
        at = pl.ds(pl.multiple_of(i * step, step), step)
        n1[at, :] = rms_scale(x0[at, :].astype(f32), gain[...]).astype(bf16)
        return carry

    lax.fori_loop(0, rows // step, normalize, 0)
    gates[...] = masked_gates(dot(n1[...], router[...]), hot0[...] + hot1[...])

    second(0)
    second(2)
    second(1)
    first(3)
    third(0)
    third(2)
    third(1)
    first(4)
    first(5)
    fourth(0)
    fourth(2)
    fourth(1)

    def fetch(t, ref):
        finish(t)
        staying[t].wait()
        c = pltpu.make_async_copy(dst[t], ref, load.at[t])
        c.start()
        return c

    fetches = [fetch(0, w_kv), fetch(1, wide), fetch(2, w_q)]

    lane = lax.broadcasted_iota(jnp.int32, (rows, 128), 1)
    seq = lax.broadcasted_iota(jnp.int32, (rows, 128), 0) // half

    def rotary(x):
        return x * cosine[...] + pltpu.roll(x, HEAD_DIM // 2, 1) * sine[...]

    fetches[0].wait()
    fetches[1].wait()
    z = dot(n1[...], wide[:, 512:640])
    z_q[...] = jnp.where(lane // 64 == seq, z, 0.0).astype(bf16)
    z = dot(n1[...], wide[:, 640:704])
    z_kv[...] = jnp.where((lane // 16) % 2 == seq, jnp.pad(z, ((0, 0), (0, 64))), 0.0).astype(bf16)
    kv = dot(n1[...], w_kv[...]) + dot(z_kv[:, :64], b_kv[...])
    for h in range(heads):
        at = slice(HEAD_DIM * h, HEAD_DIM * h + HEAD_DIM)
        turned = rotary(kv[:, at]).astype(bf16)
        kv_all[PAST, 0, :, at] = turned[:half]
        kv_all[PAST, 1, :, at] = turned[half:]
    for s in range(2):
        kv_all[PAST, s, :, width:] = kv[half * s : half * s + half, width:].astype(bf16)

    def kv_copy(slot, back, to, to_back):
        return pltpu.make_async_remote_copy(
            src_ref=kv_all.at[PAST - back],
            dst_ref=kv_all.at[PAST - to_back],
            send_sem=kv_send.at[slot],
            recv_sem=kv_recv.at[to_back],
            device_id=(to, tp),
            device_id_type=MESH,
        )

    def kv_arrived(back):
        kv_copy(0, back, core, back).wait_recv()

    def when(condition, c):
        if condition is None:
            c.start()
        else:
            pl.when(condition)(c.start)
        kv_started.append((condition, c))

    kv_started = []
    when(None, kv_copy(0, 0, up, 4))
    when(None, kv_copy(1, 0, far, 8))
    when(on_side == 0, kv_copy(2, 0, side, 2))
    when(on_core == 0, kv_copy(3, 0, core, 1))
    second(3)
    first(6)
    first(7)

    fetches[2].wait()
    queries = [jnp.zeros((rows, width), f32), jnp.zeros((rows, width), f32)]
    for e in range(experts):
        z_e = jnp.where((lane % 64) // 16 == e, z_q[...].astype(f32), 0.0).astype(bf16)
        q_e = dot(n1[...], w_q[e]) + dot(z_e, b_q[...])
        for k, hot in enumerate((hot0, hot1)):
            queries[k] = queries[k] + jnp.where(hot[:, e : e + 1] > 0, q_e, 0.0)
    for k in range(2):
        for h in range(heads):
            turned = rotary(queries[k][:, HEAD_DIM * h : HEAD_DIM * h + HEAD_DIM]).astype(bf16)
            for s in range(2):
                q_all[s * heads + h, k * half : k * half + half, :] = turned[half * s : half * s + half]

    tp_start(2)
    second(4)
    kv_arrived(4)
    when(on_side == 0, kv_copy(4, 4, side, 6))
    when(on_side == 1, kv_copy(5, 4, side, 2))
    when(on_core == 0, kv_copy(6, 4, core, 5))
    when(on_core == 1, kv_copy(7, 4, core, 3))
    kv_arrived(8)
    when(on_side == 1, kv_copy(8, 8, side, 6))
    when(on_core == 1, kv_copy(9, 8, core, 7))
    first(8)
    second(5)
    kv_arrived(2)
    when(on_core == 0, kv_copy(10, 2, core, 3))
    when(on_core == 1, kv_copy(11, 2, core, 1))
    kv_arrived(6)
    when(on_core == 0, kv_copy(12, 6, core, 7))
    when(on_core == 1, kv_copy(13, 6, core, 5))
    third(3)
    first(9)
    for back in (1, 3, 5, 7):
        kv_arrived(back)
    tp_all[2].relay()
    second(6)

    row = lax.broadcasted_iota(jnp.int32, (half, span), 0)
    key = lax.broadcasted_iota(jnp.int32, (half, span), 1)
    near = (key > row) & (key <= row + PAST * half)

    def attend(i, carry):
        s = i // heads
        h = lax.rem(i, heads)
        at = pl.ds(pl.multiple_of(h * HEAD_DIM, HEAD_DIM), HEAD_DIM)
        v_at = pl.ds(pl.multiple_of(width + h * HEAD_DIM, HEAD_DIM), HEAD_DIM)
        keys = kv_all[:, s, :, at].reshape(span, HEAD_DIM)
        values = kv_all[:, s, :, v_at].reshape(span, HEAD_DIM)
        seq_rows = pl.ds(pl.multiple_of(s * half, half), half)
        allowed = near & (q_doc[seq_rows, :1] == k_doc[s, :1, :])
        for k in range(2):
            q = q_all[i, k * half : k * half + half, :]
            scores = dot_nt(q, keys) * HEAD_DIM**-0.5
            scores = jnp.where(allowed, scores, big_negative)
            peak = jnp.max(scores, axis=1, keepdims=True)
            powers = jnp.exp(scores - peak)
            p = (powers * (1.0 / jnp.sum(powers, axis=1, keepdims=True))).astype(bf16)
            probs[i, k * half : k * half + half, :] = p
            ob[k, seq_rows, at] = dot(p, values).astype(bf16)
        return carry

    lax.fori_loop(0, 2 * heads, attend, 0)
    fourth(3)
    third(4)
    fetches.append(fetch(3, w_o))

    fetches[3].wait()
    z_acc = jnp.zeros((rows, 256), f32)
    pair_lane = lax.broadcasted_iota(jnp.int32, (rows, 256), 1)
    mine = pair_lane // 128 == lax.broadcasted_iota(jnp.int32, (rows, 256), 0) // half
    chosen = []
    for e in range(experts):
        o_e = jnp.where(hot0[:, e : e + 1] > 0, ob[0].astype(f32), 0.0)
        o_e = o_e + jnp.where(hot1[:, e : e + 1] > 0, ob[1].astype(f32), 0.0)
        o_e = o_e.astype(bf16)
        chosen.append(o_e)
        low = dot_nt(o_e, a_o[...]) * gates[:, e : e + 1]
        z_acc = z_acc + jnp.where(mine & ((pair_lane % 128) // 16 == e), low, 0.0)
    z_acc = z_acc.astype(bf16)
    z_o[...] = z_acc[:, :128] + z_acc[:, 128:]

    def columns(ref, rank):
        return ref.at[:, pl.ds(pl.multiple_of(rank * part, part), part)]

    scatter = Scatter(parts, held, relay, sum_send, sum_recv, 0)
    spread = Spread(None, lambda rank: columns(attn, rank), sum_send, sum_recv, 1)
    for d in (5, 6, 7, 4, 1, 2, 3, 0):
        at = pl.ds(pl.multiple_of((tp ^ d) * part, part), part)
        total = dot_nt(z_acc, wide[at, 256:512])
        for e in range(experts):
            total = total + dot(chosen[e], w_o[e, :, at]) * gates[:, e : e + 1]
        if d:
            parts[d] = total.astype(bf16)
            if d != FAR:
                scatter.copy(d).start()
        else:
            own[...] = total
    second(7)
    scatter.relay()
    second(8)
    third(5)
    columns(attn, tp)[...] = scatter.total(own[...]).astype(bf16)
    spread.start()
    second(9)
    third(6)
    spread.relay()
    third(7)
    third(8)
    spread.wait()
    fourth(4)
    fourth(5)
    third(9)
    fourth(6)
    fourth(7)
    fourth(8)
    fourth(9)
    tp_wait(2)
    for t in range(4, len(kinds)):
        finish(t)
    for c in started:
        c.wait_send()
    for t, c in enumerate(staying):
        if t > 3:
            c.wait()
    for condition, c in kv_started:
        if condition is None:
            c.wait_send()
        else:
            pl.when(condition)(c.wait_send)
    scatter.sent()
    spread.sent()
    for c in tp_all:
        c.sent()


def attention(shards_in, tp_shards, small):
    s_q, s_kv, s_o, s_gu, s_d = shards_in
    tokens, cotangent, s_wide = tp_shards
    rows, part = tokens.shape
    model = part * N_TP
    experts, _, width = s_q.shape
    half = rows // 2
    heads = width // HEAD_DIM
    shape = jax.ShapeDtypeStruct

    def grown(a, d):
        return shape(tuple(n * (N_CTX if i == d else 1) for i, n in enumerate(a.shape)), a.dtype)

    gathered = (grown(s_q, 1), grown(s_kv, 0), grown(s_o, 2), grown(s_gu, 1), grown(s_d, 2))
    wide_mid = shape((s_wide.shape[0] * N_TP, s_wide.shape[1]), bf16)
    wide = grown(wide_mid, 0)
    vmem_out = (
        shape((rows, model), bf16),
        shape((rows, model), bf16),
        shape((rows, model), bf16),
        shape((PAST + 1, 2, half, 2 * width), bf16),
        shape((2 * heads, rows, HEAD_DIM), bf16),
        shape((2 * heads, rows, (PAST + 1) * half), bf16),
        shape((2, rows, width), bf16),
        shape((rows, 128), bf16),
        shape((rows, 128), bf16),
        shape((rows, 128), bf16),
        shape((rows, 128), f32),
    )
    any_out = gathered + (wide, wide_mid, shape((rows, model), bf16))
    return pl.pallas_call(
        attention_kernel,
        out_shape=any_out + vmem_out,
        in_specs=[ANY] * 8 + [VMEM] * len(small),
        out_specs=tuple([ANY] * len(any_out) + [VMEM] * len(vmem_out)),
        scratch_shapes=[
            pltpu.VMEM(gathered[0].shape, bf16),
            pltpu.VMEM(gathered[1].shape, bf16),
            pltpu.VMEM(gathered[2].shape, bf16),
            pltpu.VMEM(wide.shape, bf16),
            pltpu.VMEM((N_TP, rows, part), bf16),
            pltpu.VMEM((rows, part), bf16),
            pltpu.VMEM((rows, part), f32),
            pltpu.VMEM((N_TP, rows, part), bf16),
            pltpu.SemaphoreType.DMA((10, 25)),
            pltpu.SemaphoreType.DMA((10, 25)),
            pltpu.SemaphoreType.DMA((10,)),
            pltpu.SemaphoreType.DMA((3, N_TP)),
            pltpu.SemaphoreType.DMA((3, N_TP)),
            pltpu.SemaphoreType.DMA((3,)),
            pltpu.SemaphoreType.DMA((14,)),
            pltpu.SemaphoreType.DMA((PAST + 1,)),
            pltpu.SemaphoreType.DMA((4,)),
            pltpu.SemaphoreType.DMA((2, N_TP)),
            pltpu.SemaphoreType.DMA((2, N_TP)),
        ],
        compiler_params=pltpu.CompilerParams(
            collective_id=0, has_side_effects=True, vmem_limit_bytes=60 << 20
        ),
        name="attention",
    )(*shards_in, *tp_shards, *small)


def backward_kernel(
    dx1, dx1_own, ob, gates, z_q, z_kv, z_sum, table, gain, router, b_q, b_kv, a_o, ff_parts, ff_own,
    h_q, h_kv, h_o, h_wide, h_x0, h_n1, h_n2, h_dy, h_kv_all, h_q_all, h_probs,
    mixed, grad_tokens, wide_a, wide_b, heads_out,
    w_q, w_kv, w_o, wide, x0, n1, n2, dy, kv_all, q_all, probs, dob, dkv, dkv_held, dq, dkv_own, dn, parts, relay, own, held, ff_held, ff_relay,
    z_part, z_held, z_done, dots, tails, a_src, b_src, heads_src, a_core, b_core, heads_core, a_held, b_held, heads_held,
    load, tp_send, tp_recv, core_send, core_recv, kv_send, kv_recv, ctx_send, ctx_recv,
):
    me, tp = lax.axis_index("ctx"), lax.axis_index("tp")
    core = me ^ 1
    on_core = lax.rem(me, 2)
    rows, model = x0.shape
    cosine, sine, hot0, hot1 = (table.at[:, 128 * i : 128 * i + 128] for i in range(4))
    part = model // N_TP
    half = rows // 2
    experts = w_q.shape[0]
    width = w_q.shape[2]
    heads = width // HEAD_DIM
    span = (PAST + 1) * half
    loads = []
    for i, (h, w) in enumerate(
        (
            (h_wide, wide),
            (h_o, w_o),
            (h_kv_all, kv_all),
            (h_probs, probs),
            (h_q_all, q_all),
            (h_q, w_q),
            (h_n2, n2),
            (h_dy, dy),
            (h_n1, n1),
            (h_kv, w_kv),
            (h_x0, x0),
        )
    ):
        c = pltpu.make_async_copy(h, w, load.at[i])
        c.start()
        loads.append(c)
    greet([(me ^ d, tp) for d in range(1, N_CTX)] + [(me, tp ^ d) for d in range(1, N_TP)])
    a_sum = CtxSum(a_src, a_core, a_held, None, ctx_send, ctx_recv, 0)
    b_sum = CtxSum(b_src, b_core, b_held, None, ctx_send, ctx_recv, 1)
    heads_sum = CtxSum(heads_src, heads_core, heads_held, heads_out, ctx_send, ctx_recv, 2)
    ff = Scatter(ff_parts, ff_held, ff_relay, tp_send, tp_recv, 4)
    for d in (5, 6, 7, 1, 2, 3):
        ff.copy(d).start()

    lane = lax.broadcasted_iota(jnp.int32, (rows, 128), 1)
    seq = lax.broadcasted_iota(jnp.int32, (rows, 128), 0) // half
    hots = (hot0, hot1)

    loads[0].wait()
    pair_lane = lax.broadcasted_iota(jnp.int32, (rows, 256), 1)
    mine = pair_lane // 128 == lax.broadcasted_iota(jnp.int32, (rows, 256), 0) // half
    dz_o = dot(dx1[...], wide[:, 256:512])
    loads[1].wait()
    g = [jnp.zeros((rows, width), f32), jnp.zeros((rows, width), f32)]
    g_ao = jnp.zeros((256, width), f32)
    for e in range(experts):
        dz_e = jnp.where(mine & ((pair_lane % 128) // 16 == e), dz_o, 0.0)
        g_e = dot_nt(dx1[...], w_o[e]) + dot(dz_e.astype(bf16), a_o[...])
        o_e = jnp.where(hot0[:, e : e + 1] > 0, ob[0].astype(f32), 0.0)
        o_e = o_e + jnp.where(hot1[:, e : e + 1] > 0, ob[1].astype(f32), 0.0)
        o_e = o_e.astype(bf16)
        dz_e = (dz_e * gates[:, e : e + 1]).astype(bf16)
        g_ao = g_ao + dot_tn(dz_e, o_e)
        for k in range(2):
            g[k] = g[k] + jnp.where(hots[k][:, e : e + 1] > 0, g_e, 0.0)
    d_gates = jnp.zeros((rows, 128), f32)
    for k in range(2):
        d_gate = jnp.sum(g[k] * ob[k].astype(f32), axis=1, keepdims=True)
        d_gates = d_gates + jnp.where(hots[k][...] > 0, d_gate, 0.0)
        gate = jnp.sum(hots[k][...] * gates[...], axis=1, keepdims=True)
        d_out = (g[k] * gate).astype(bf16)
        for s in range(2):
            for h in range(heads):
                dob[s * heads + h, k * half : k * half + half, :] = d_out[
                    half * s : half * s + half, HEAD_DIM * h : HEAD_DIM * h + HEAD_DIM
                ]
    d_logits = gates[...] * (d_gates - jnp.sum(gates[...] * d_gates, axis=1, keepdims=True))
    d_logits = d_logits.astype(bf16)

    def attend_back(i, carry):
        s = i // heads
        h = lax.rem(i, heads)
        at = pl.ds(pl.multiple_of(h * HEAD_DIM, HEAD_DIM), HEAD_DIM)
        v_at = pl.ds(pl.multiple_of(width + h * HEAD_DIM, HEAD_DIM), HEAD_DIM)
        keys = kv_all[:, s, :, at].reshape(span, HEAD_DIM)
        values = kv_all[:, s, :, v_at].reshape(span, HEAD_DIM)
        seq_rows = pl.ds(pl.multiple_of(s * half, half), half)
        d_keys = jnp.zeros((span, HEAD_DIM), f32)
        d_values = jnp.zeros((span, HEAD_DIM), f32)
        for k in range(2):
            k_rows = slice(k * half, k * half + half)
            d_o = dob[i, k_rows, :]
            p = probs[i, k_rows, :]
            delta = jnp.sum(d_o.astype(f32) * ob[k, seq_rows, at].astype(f32), axis=1, keepdims=True)
            d_s = (p.astype(f32) * (dot_nt(d_o, values) - delta)).astype(bf16)
            d_q = dot(d_s, keys) * HEAD_DIM**-0.5
            turned = d_q * cosine[seq_rows, :] - pltpu.roll(d_q, HEAD_DIM // 2, 1) * sine[seq_rows, :]
            dq[k, seq_rows, at] = turned.astype(bf16)
            d_keys = d_keys + dot_tn(d_s, q_all[i, k_rows, :])
            d_values = d_values + dot_tn(p, d_o)
        d_keys = (d_keys * HEAD_DIM**-0.5).astype(bf16)
        dkv[:, s, :, at] = d_keys.reshape(PAST + 1, half, HEAD_DIM)
        dkv[:, s, :, v_at] = d_values.astype(bf16).reshape(PAST + 1, half, HEAD_DIM)
        return carry

    ff.relay()
    for i in (2, 3, 4):
        loads[i].wait()
    lax.fori_loop(0, 2 * heads, attend_back, 0)

    def to_core(back):
        return pltpu.make_async_remote_copy(
            src_ref=dkv.at[PAST - back],
            dst_ref=dkv_held.at[back // 2],
            send_sem=core_send.at[back // 2],
            recv_sem=core_recv.at[back // 2],
            device_id=(core, tp),
            device_id_type=MESH,
        )

    def to_owner(back):
        return pltpu.make_async_remote_copy(
            src_ref=dkv.at[PAST - back],
            dst_ref=dkv_held.at[3 + back // 2],
            send_sem=kv_send.at[back // 2],
            recv_sem=kv_recv.at[back // 2],
            device_id=(lax.rem(me + N_CTX - back, N_CTX), tp),
            device_id_type=MESH,
        )

    for back in (1, 3, 5, 7):
        to_core(back).start()
    for back in (1, 3, 5, 7):
        to_core(back).wait_recv()
        slot = PAST - (back - 1) - 2 * on_core
        dkv[slot] = (dkv[slot].astype(f32) + dkv_held[back // 2].astype(f32)).astype(bf16)
    for back in (2, 4, 6, 8):
        to_owner(back).start()

    mixed[...] = ff.total(ff_own[...]).astype(bf16)
    loads[5].wait()
    dz_q = jnp.zeros((rows, 128), f32)
    g_bq = jnp.zeros((128, width), f32)
    chosen = []
    for e in range(experts):
        dq_e = jnp.where(hot0[:, e : e + 1] > 0, dq[0].astype(f32), 0.0)
        dq_e = dq_e + jnp.where(hot1[:, e : e + 1] > 0, dq[1].astype(f32), 0.0)
        dq_e = dq_e.astype(bf16)
        chosen.append(dq_e)
        keep = (lane // 64 == seq) & ((lane % 64) // 16 == e)
        dz_q = dz_q + jnp.where(keep, dot_nt(dq_e, b_q[...]), 0.0)
        z_e = jnp.where(keep, z_q[...].astype(f32), 0.0).astype(bf16)
        g_bq = g_bq + dot_tn(z_e, dq_e)
    dz_q = dz_q.astype(bf16)
    z_part[:, :128] = dz_q
    for j in range(N_TP):
        at = slice(part * j, part * j + part)
        total = dot_nt(dz_q, wide[at, 512:640]) + dot_nt(d_logits, router[at, :])
        for e in range(experts):
            total = total + dot_nt(chosen[e], w_q[e, at, :])
        dn[j] = total
    for i in (6, 7, 8):
        loads[i].wait()
    own_columns = lax.broadcasted_iota(jnp.int32, (model, part), 1)
    own_columns = (own_columns // 16) * 128 + tp * 16 + own_columns % 16
    pick = (lax.broadcasted_iota(jnp.int32, (model, part), 0) == own_columns).astype(bf16)

    def to_pairs(ref, at, values):
        values = values.astype(bf16).reshape(8, 2, 16, values.shape[1])
        for c in range(2):
            ref[c, :, :, at] = values[:, c]

    n2_own = dot(n2[...], pick).astype(bf16)
    dx1_cols = dot(dx1[...], pick).astype(bf16)
    dy_own = dot(dy[...], pick).astype(bf16)
    n1_own = dot(n1[...], pick).astype(bf16)
    lane_m = lax.broadcasted_iota(jnp.int32, (part, 128), 1)
    for s in range(2):
        at = slice(half * s, half * s + half)
        to_pairs(a_src, slice(128 * s, 128 * s + 128), dot_tn(n2_own[at], z_sum[at, :128]))
        low = jnp.where(
            lane_m < 64, dot_tn(dx1_cols[at], z_sum[at, 128:]), dot_tn(dy_own[at], z_sum[at, 128:])
        )
        to_pairs(a_src, slice(256 + 128 * s, 384 + 128 * s), low)
    a_sum.start()

    total = dkv[PAST].astype(f32)
    for back in (2, 4, 6, 8):
        to_owner(back).wait_recv()
        total = total + dkv_held[3 + back // 2].astype(f32)
    a_sum.chips()
    for h in range(heads):
        at = slice(HEAD_DIM * h, HEAD_DIM * h + HEAD_DIM)
        d_k = jnp.concatenate([total[0, :, at], total[1, :, at]], axis=0)
        turned = d_k * cosine[...] - pltpu.roll(d_k, HEAD_DIM // 2, 1) * sine[...]
        dkv_own[:, at] = turned.astype(bf16)
    dkv_own[:, width:] = jnp.concatenate([total[0, :, width:], total[1, :, width:]], axis=0).astype(bf16)
    loads[9].wait()
    loads[10].wait()
    dz_kv = dot_nt(dkv_own[...], b_kv[...])
    keep = (lane[:, :64] // 16) % 2 == seq[:, :64]
    dz_kv = jnp.where(keep, dz_kv, 0.0).astype(bf16)
    z_part[:, 128:] = jnp.pad(dz_kv.astype(f32), ((0, 0), (0, 64))).astype(bf16)

    scatter = Scatter(parts, held, relay, tp_send, tp_recv, 0)
    z_rows = rows // N_TP

    def z_region(ref, rank):
        return ref.at[pl.ds(pl.multiple_of(rank * z_rows, z_rows), z_rows), :]

    def z_scatter(d):
        return pltpu.make_async_remote_copy(
            src_ref=z_region(z_part, tp ^ d),
            dst_ref=z_held.at[d],
            send_sem=tp_send.at[1, d],
            recv_sem=tp_recv.at[1, d],
            device_id=(me, tp ^ d),
            device_id_type=MESH,
        )

    def z_spread(d, rank):
        return pltpu.make_async_remote_copy(
            src_ref=z_region(z_done, rank),
            dst_ref=z_region(z_done, rank),
            send_sem=tp_send.at[2, d],
            recv_sem=tp_recv.at[2, d],
            device_id=(me, tp ^ d),
            device_id_type=MESH,
        )

    def tail(d, rank):
        return pltpu.make_async_remote_copy(
            src_ref=tails.at[rank],
            dst_ref=tails.at[rank],
            send_sem=tp_send.at[3, d],
            recv_sem=tp_recv.at[3, d],
            device_id=(me, tp ^ d),
            device_id_type=MESH,
        )

    for d in range(1, N_TP):
        z_scatter(d).start()
    g_bkv = dot_tn(z_kv[...], dkv_own[...])
    blocks = [g_bq[32 * i : 32 * i + 32] for i in range(4)] + [g_bkv[:32, :width], g_bkv[32:64, width:]]
    blocks += [g_ao[128 * s + 32 * i : 128 * s + 32 * i + 32] for s in range(2) for i in range(2)]
    blocks += [jnp.zeros((32, width), f32)] * 6
    for i in range(N_CTX):
        heads_src[i % 2, i // 2] = blocks[i].astype(bf16)
    heads_sum.start()
    along = jnp.zeros((rows, 1), f32)
    for d in (5, 6, 7, 4, 1, 2, 3, 0):
        peer = tp ^ d
        at = pl.ds(pl.multiple_of(peer * part, part), part)
        total = dn[peer] + dot_nt(dz_kv, wide[at, 640:704]) + dot_nt(dkv_own[...], w_kv[at, :])
        scaled = total * gain[:, at]
        along = along + jnp.sum(scaled * x0[:, at].astype(f32), axis=1, keepdims=True)
        if d:
            parts[d] = total.astype(bf16)
            if d != FAR:
                scatter.copy(d).start()
        else:
            own[...] = total
    dots[...] = jnp.broadcast_to(along, dots.shape)
    tails[tp] = jnp.transpose(dots[...])[:8, :]
    for d in range(1, N_TP):
        tail(d, tp).start()
    total = z_region(z_part, tp)[...].astype(f32)
    for d in range(1, N_TP):
        z_scatter(d).wait_recv()
        total = total + z_held[d].astype(f32)
    z_region(z_done, tp)[...] = total.astype(bf16)
    for d in range(1, N_TP):
        z_spread(d, tp).start()
    heads_sum.chips()
    scatter.relay()
    for d in range(1, N_TP):
        z_spread(d, tp ^ d).wait_recv()
    to_pairs(b_src, slice(0, part), dot_tn(n1_own, z_done[...]))
    b_sum.start()
    heads_sum.again()
    total = scatter.total(own[...])
    b_sum.chips()
    for d in range(1, N_TP):
        tail(d, tp ^ d).wait_recv()
    whole = tails[0]
    for d in range(1, N_TP):
        whole = whole + tails[d]
    dots[...] = jnp.transpose(jnp.broadcast_to(whole[:1], (128, rows)))
    own_at = pl.ds(pl.multiple_of(tp * part, part), part)
    own[...] = total * gain[:, own_at]
    step = 32

    def finish(i, carry):
        at = pl.ds(pl.multiple_of(i * step, step), step)
        x = x0[at, :].astype(f32)
        inverse = lax.rsqrt(jnp.mean(x * x, axis=1, keepdims=True) + eps)
        mean = dots[at, :1] * (1.0 / model)
        back = inverse * own[at, :] - x0[at, own_at].astype(f32) * inverse**3 * mean
        grad_tokens[at, :] = (dx1_own[at, :] + back).astype(bf16)
        return carry

    lax.fori_loop(0, rows // step, finish, 0)
    wide_a[...] = a_sum.total()
    heads_sum.other_core()
    wide_b[...] = b_sum.total()
    heads_sum.finish()
    for back in (1, 3, 5, 7):
        to_core(back).wait_send()
        to_owner(back + 1).wait_send()
    scatter.sent()
    ff.sent()
    for d in range(1, N_TP):
        z_scatter(d).wait_send()
        z_spread(d, tp).wait_send()
        tail(d, tp).wait_send()


def backward(vmem, hbm):
    dx1 = vmem[0]
    w_q, w_kv, w_o, wide, x0, n1, n2, dy, kv_all, q_all, probs = hbm
    rows, model = dx1.shape
    part = model // N_TP
    width = w_q.shape[2]
    heads = width // HEAD_DIM
    half = rows // 2
    shape = jax.ShapeDtypeStruct
    reduced = [(2, 8, 16, 512), (2, 8, 16, part), (2, 8, 32, width)]
    return pl.pallas_call(
        backward_kernel,
        out_shape=(
            shape((rows, part), bf16),
            shape((rows, part), bf16),
            shape((16, 512), f32),
            shape((16, part), f32),
            shape(reduced[2], bf16),
        ),
        in_specs=[VMEM] * len(vmem) + [ANY] * len(hbm),
        out_specs=tuple([VMEM] * 5),
        scratch_shapes=[
            pltpu.VMEM(a.shape, bf16) for a in hbm
        ]
        + [
            pltpu.VMEM((2 * heads, rows, HEAD_DIM), bf16),
            pltpu.VMEM(kv_all.shape, bf16),
            pltpu.VMEM((8,) + kv_all.shape[1:], bf16),
            pltpu.VMEM((2, rows, width), bf16),
            pltpu.VMEM((rows, 2 * width), bf16),
            pltpu.VMEM((N_TP, rows, part), f32),
            pltpu.VMEM((N_TP, rows, part), bf16),
            pltpu.VMEM((rows, part), bf16),
            pltpu.VMEM((rows, part), f32),
            pltpu.VMEM((N_TP, rows, part), bf16),
            pltpu.VMEM((N_TP, rows, part), bf16),
            pltpu.VMEM((rows, part), bf16),
            pltpu.VMEM((rows, 256), bf16),
            pltpu.VMEM((N_TP, rows // N_TP, 256), bf16),
            pltpu.VMEM((rows, 256), bf16),
            pltpu.VMEM((rows, 128), f32),
            pltpu.VMEM((N_TP, 8, rows), f32),
        ]
        + [pltpu.VMEM(a, bf16) for a in reduced]
        + [pltpu.VMEM(a[1:], bf16) for a in reduced + reduced]
        + [
            pltpu.SemaphoreType.DMA((len(hbm),)),
            pltpu.SemaphoreType.DMA((5, N_TP)),
            pltpu.SemaphoreType.DMA((5, N_TP)),
            pltpu.SemaphoreType.DMA((4,)),
            pltpu.SemaphoreType.DMA((4,)),
            pltpu.SemaphoreType.DMA((5,)),
            pltpu.SemaphoreType.DMA((5,)),
            pltpu.SemaphoreType.DMA((3, 16)),
            pltpu.SemaphoreType.DMA((3, 16)),
        ],
        compiler_params=pltpu.CompilerParams(
            collective_id=3, has_side_effects=True, vmem_limit_bytes=60 << 20
        ),
        name="backward",
    )(*vmem, *hbm)


def shards(
    tokens,
    norm1_gain,
    router_attn,
    w_query,
    w_key_value,
    w_out,
    norm2_gain,
    router_ffn,
    w_gate_up,
    w_down,
    adapt_wide,
    adapt_heads,
    adapt_ffn,
    attention_routes,
    feedforward_routes,
    doc_lengths,
    adapter_index,
    cotangent,
):
    seqs, block, part = tokens.shape
    rows = seqs * block
    n_tp = lax.axis_size("tp")
    model = part * n_tp
    experts = w_query.shape[0]
    width = w_query.shape[2]
    heads = width // HEAD_DIM
    hidden = w_down.shape[1]
    rank = adapt_heads.shape[2]
    wide_slots = adapt_wide.shape[1]
    ctx_rank = lax.axis_index("ctx")


    def by_sequence(a):
        return jnp.where(adapter_index[0] == 0, a, a[::-1])

    wide_own = by_sequence(adapt_wide.astype(bf16))
    groups = [[6, 10, 7, 11, 8, 12, 9, 13], list(range(14, 22)), [0, 1, 2, 3], [4, 5]]
    order = [(q, s) for g in groups[:3] for q in range(seqs) for s in g]
    order += [(q, s) for s in groups[3] for q in range(seqs)]
    wide_cols = wide_own.reshape(seqs * wide_slots, rank, -1)[
        np.array([q * wide_slots + s for q, s in order])
    ].reshape(seqs * wide_slots * rank, -1).T
    heads_low = by_sequence(adapt_heads.astype(bf16))
    ffn_low = by_sequence(adapt_ffn.astype(bf16))
    route_a = attention_routes.reshape(rows, -1)
    route_f = feedforward_routes.reshape(rows, -1)

    positions = ctx_rank * block + jnp.arange(block, dtype=jnp.int32)
    doc_ids, offsets = doc_layout(doc_lengths, positions)
    half = HEAD_DIM // 2
    frequency = 10000.0 ** (-2.0 * jnp.arange(half, dtype=f32) / HEAD_DIM)
    angles = offsets.astype(f32).reshape(rows)[:, None] * frequency
    cosine, sine = jnp.cos(angles), jnp.sin(angles)
    cosine = jnp.concatenate([cosine, cosine], axis=1)
    sine = jnp.concatenate([-sine, sine], axis=1)

    b_q, b_kv, a_o = heads_low[:, :experts], heads_low[:, experts : experts + 2], heads_low[:, experts + 2 :]
    key_pos = (ctx_rank - PAST) * block + jnp.arange((PAST + 1) * block, dtype=jnp.int32)
    key_doc = doc_layout(doc_lengths, jnp.maximum(key_pos, 0))[0]
    key_doc = jnp.where(key_pos[None, :] >= 0, key_doc, -(1 << 20))
    blank = jnp.zeros((seqs, rank, width), bf16)
    b_kv_wide = jnp.concatenate(
        [
            jnp.concatenate([b_kv[:, 0], blank], axis=-1).reshape(seqs * rank, 2 * width),
            jnp.concatenate([blank, b_kv[:, 1]], axis=-1).reshape(seqs * rank, 2 * width),
        ],
        axis=0,
    )
    a_o_wide = jnp.pad(a_o.reshape(seqs, experts * rank, width), ((0, 0), (0, 64), (0, 0))).reshape(256, width)
    b_q = b_q.reshape(seqs * experts * rank, width)
    table = jnp.concatenate(
        [
            cosine,
            sine,
            widen_routes(route_a[:, :1], experts),
            widen_routes(route_a[:, 1:], experts),
            widen_routes(route_f, experts),
            jnp.broadcast_to(doc_ids.reshape(rows, 1).astype(f32), (rows, 128)),
        ],
        axis=1,
    )
    router_wide = jnp.pad(router_attn, ((0, 0), (0, 128 - experts)))
    (
        w_query, w_key_value, w_out, w_gate_up, w_down, wide, _, dy,
        x0, sum_out, n1, kv_all, q_all, probs, ob, z_o_gated, z_q, z_kv, gates,
    ) = attention(
        [
            w_query,
            w_key_value.reshape(-1, 2 * width),
            w_out,
            gate_up_columns(w_gate_up[:, :, 0], w_gate_up[:, :, 1]),
            w_down,
        ],
        [tokens.reshape(rows, part), cotangent.reshape(rows, part), wide_cols],
        [
            norm1_gain[None],
            router_wide,
            table,
            jnp.broadcast_to(key_doc[:, None, :], (seqs, 8, key_doc.shape[1])).astype(f32),
            b_q,
            b_kv_wide,
            a_o_wide,
        ],
    )
    blank = jnp.zeros((seqs, experts, rank, hidden), bf16)
    b_gu = jnp.stack(
        [gate_up_columns(ffn_low[:, :experts], blank), gate_up_columns(blank, ffn_low[:, experts : 2 * experts])],
        axis=2,
    ).reshape(seqs, 2 * experts * rank, 2 * hidden)
    a_d = jnp.pad(ffn_low[:, 2 * experts :].reshape(seqs, experts * rank, hidden), ((0, 0), (64, 0), (0, 0)))
    ff_parts, ff_own, dx1b, dx1_own, n2, z_sum, gu_sum, d_sum = feed_forward(
        x0, sum_out, dy, norm2_gain[None], wide,
        jnp.pad(router_ffn, ((0, 0), (0, 128 - experts))),
        table, b_gu.reshape(256, 2 * hidden), a_d.reshape(256, hidden), z_o_gated, w_gate_up, w_down,
    )
    mixed, grad_tokens, wide_a, wide_b, head_sum = backward(
        [
            dx1b, dx1_own, ob, gates, z_q, z_kv, z_sum, table, norm1_gain[None], router_wide, b_q, b_kv_wide, a_o_wide, ff_parts, ff_own,
        ],
        [w_query, w_key_value, w_out, wide, x0, n1, n2, dy, kv_all, q_all, probs],
    )
    grad_wide = jnp.concatenate([wide_a, wide_b[:, : 704 - 512]], axis=1).T
    back_order = np.argsort(np.array([q * wide_slots + s for q, s in order]))
    grad_wide = grad_wide.reshape(seqs * wide_slots, rank, -1)[back_order]
    grad_wide = by_sequence(grad_wide.reshape(seqs, wide_slots, rank, -1))
    head_sum = jnp.swapaxes(head_sum, 0, 1).reshape(-1, rank, width).astype(f32)
    grad_heads = by_sequence(jnp.concatenate(
        [
            head_sum[: seqs * experts].reshape(seqs, experts, rank, width),
            jnp.swapaxes(head_sum[8:12].reshape(2, seqs, rank, width), 0, 1),
            head_sum[12:20].reshape(seqs, experts, rank, width),
        ],
        axis=1,
    ))
    gu_sum = jnp.swapaxes(gu_sum, 0, 1).reshape(seqs, experts, 2, rank, 768).astype(f32)
    grad_ffn = by_sequence(jnp.concatenate(
        [
            gu_sum[:, :, 0, :, :704],
            jnp.concatenate([gu_sum[:, :, 1, :, :640], gu_sum[:, :, 1, :, 704:]], axis=-1),
            jnp.swapaxes(d_sum, 0, 1).reshape(seqs, experts, rank, hidden),
        ],
        axis=1,
    ))
    mixed = mixed.reshape(seqs, block, part)
    grad_tokens = grad_tokens.reshape(seqs, block, part)
    return (mixed, grad_tokens, grad_wide, grad_heads, grad_ffn)


def solution(mesh):
    placed = (
        P(None, "ctx", "tp"),
        P(),
        P(),
        P(None, "ctx", "tp"),
        P("ctx", None, "tp"),
        P(None, "tp", "ctx"),
        P(),
        P(),
        P(None, "ctx", None, "tp"),
        P(None, "tp", "ctx"),
        P(None, None, None, ("ctx", "tp")),
        P(None, None, None, "tp"),
        P(None, None, None, "tp"),
        P(None, "ctx", None),
        P(None, "ctx", None),
        P(),
        P(),
        P(None, "ctx", "tp"),
    )
    return jax.shard_map(
        shards,
        mesh=mesh,
        in_specs=placed,
        out_specs=(
            P(None, "ctx", "tp"),
            P(None, "ctx", "tp"),
            P(None, None, None, ("ctx", "tp")),
            P(None, None, None, "tp"),
            P(None, None, None, "tp"),
        ),
        check_vma=False,
    )
```

time: 454 us -> 379 us (0.83); the launches traced: 453 us -> 372 us
  Pallas kernels: 423 us -> 343 us
    pallas_call x1, Pallas kernels: 247 us -> 201 us  [attention(): pl.pallas_call(attention_kernel, out_shape=any_out + vmem_out, in_specs=[...]
    pallas_call x1, Pallas kernels: 95.6 us -> 76.3 us  [backward(): pl.pallas_call(backward_kernel, out_shape=(shape((rows, part), bf16), sha...]
    pallas_call x1, Pallas kernels: 80.5 us -> 66.3 us  [feed_forward(): pl.pallas_call(ffn_kernel, out_shape=(shape((N_TP, rows, part), bf16), sh...]
    gather x6 -> x0, local copies, waits for them, and re-layouts: 5.91 us -> none  [the longest x1 1.64 us: shards(): jnp.concatenate([gu_sum[:, :, 0, :, :704], jnp.concatenate([gu_sum[:, :,...]
where the time goes in v4:
time: 379 us; the launch traced here: 372 us
  Pallas kernels  343 us (91%)
  local copies, waits for them, and re-layouts  18.7 us (5%)
  other arithmetic  8.71 us (2%)
    pallas_call x1, Pallas kernels, attention(): pl.pallas_call(attention_kernel, out_shape=any_out + vmem_out, in_specs=[...  201 us
    pallas_call x1, Pallas kernels, backward(): pl.pallas_call(backward_kernel, out_shape=(shape((rows, part), bf16), sha...  76.3 us
    pallas_call x1, Pallas kernels, feed_forward(): pl.pallas_call(ffn_kernel, out_shape=(shape((N_TP, rows, part), bf16), sh...  66.3 us

profile of v4, /device:TPU:1, one launch (start us, length us, event | category | flops | bytes accessed | tf_op | source)
XLA Modules:
  0.0 372.3 jit_solution(18079627230456862151)
XLA Ops:
  0.6 0.8 multiply_reduce_fusion
  1.5 0.8 fusion.6
  3.2 0.8 fusion.16
  4.1 0.8 convert_reduce_fusion
  4.9 1.0 concatenate.34.table
  8.5 2.2 concatenate.33.s_gu
  11.3 0.7 pad.18
  14.1 0.7 copy.102
  15.1 0.9 pad.17.router
  16.0 0.7 copy.107
  16.7 200.7 %attention.1 = (bf16[4,2048,256]{2,1,0:T(8,128)(2,1)}, bf16[2048,512]{1,0:T(8,128)(2,1)}, bf16[4,256,2048]{2,1,0:T(8,128)(2,1)}, bf16[4,2048,1408]{2,1,0:T(8,128...) custom-call(bf16[4,128,256]{2,1,0:T(8,128)(2,1)} %s_q.1, ...), custom_call_target="tpu_custom_call" | custom-call | tf_op jit(solution)/shard_map/attention/pallas_call | solution.py:943
  218.1 0.9 copy.93
  219.0 0.8 pad.20
  220.1 0.9 pad.19.router
  221.0 66.3 %feed_forward.1 = (bf16[8,256,256]{2,1,0:T(8,128)(2,1)}, f32[256,256]{1,0:T(8,128)}, bf16[256,2048]{1,0:T(8,128)(2,1)}, f32[256,256]{1,0:T(8,128)}, bf16[256,204...) custom-call(bf16[256,2048]{1,0:T(8,128)(2,1)} %get-tuple-element.36.x0.h_x, ...), custom_call_target="tpu_custom_call" | custom-call | tf_op jit(solution)/shard_map/feed_forward/pallas_call | solution.py:493
  287.3 1.1 convert_element_type.97
  288.8 1.1 reverse_select_fusion
  289.9 76.3 %backward.1 = (bf16[256,256]{1,0:T(8,128)(2,1)}, bf16[256,256]{1,0:T(8,128)(2,1)}, f32[16,512]{1,0:T(8,128)}, f32[16,256]{1,0:T(8,128)}, bf16[2,8,32,256]{3,2,1,0:T(8,128)(2,1)}) custom-call(bf16[256,2048]{1,0:T(8,128)(2,1)} %get-tuple-element.43.dx1, f32[256,256]{1,0:T(8,128)} %get-tuple-element.44.dx1_own, bf16[2,256,256]{2,1,0:T(8,128)(2,1)} %get-tuple-element.45.ob, ...), custom_call_target="tpu_custom_call" | custom-call | tf_op jit(solution)/shard_map/backward/pallas_call | solution.py:1305
  366.1 1.0 convert_bitcast_fusion
  367.3 0.8 reverse_select_fusion.2
  369.1 0.6 rev.21
  369.8 0.7 copy.100
  370.6 0.7 copy.115
  371.2 0.7 copy.116
  (91 shorter events, 8.7 us)
Async XLA Ops:
  3.9 2.9 copy-start.14
  3.9 2.9 copy-start.4
  4.9 2.7 copy-start
  8.5 3.6 copy-start.2
  10.7 2.8 copy-start.13
  11.3 3.5 copy-start.9
  13.1 2.9 copy-start.5
  16.7 200.7 %copy-start.1 = (f32[2,12,16,704]{3,2,1,0:T(8,128)S(1)}, f32[2,12,16,704]{3,2,1,0:T(8,128)}, u32[]{:S(2)}) copy-start(f32[2,12,16,704]{3,2,1,0:T(8,128)} %param.36) | copy-start | bytes 3244036
  218.0 1.7 copy-start.10
  287.3 1.3 copy-start.3
  367.1 0.9 copy-start.8
  367.1 0.9 copy-start.11
  367.2 1.0 copy-start.12
  368.8 1.7 copy-start.7
  369.1 2.1 copy-start.6

commit v5 on v4

--- a/solution.py
+++ b/solution.py
@@ -548,7 +548,13 @@
 
 
 def gate_up_columns(gate, up):
-    return jnp.concatenate([gate[..., :640], up[..., :640], gate[..., 640:], up[..., 640:]], axis=-1)
+    def put(part, before, after):
+        sides = [(0, 0, 0)] * (part.ndim - 1) + [(before, after, 0)]
+        return lax.pad(part, jnp.zeros((), part.dtype), sides)
+
+    return (
+        put(gate[..., :640], 0, 768) + put(up[..., :640], 640, 128)
+    ) + (put(gate[..., 640:], 1280, 64) + put(up[..., 640:], 1344, 0))
 
 
 def attention_kernel(
@@ -617,7 +623,7 @@
         c.start()
         started.append(c)
 
-    cuts = [2, 2, 3, 3] + [2] * 6
+    cuts = [2, 2, 3, 3, 3, 3, 3, 2, 2, 2]
 
     def arrive(t, item):
         cut = cuts[t]
@@ -683,14 +689,18 @@
             copy(t, 12 + item, owner ^ 1, low, high, core, 0, False).wait_recv()
         copy(t, 24, core, 0, 4, core, 0, False).wait_recv()
 
+    tp_start(1)
     tp_start(0)
-    tp_start(1)
     for t in (0, 2):
         first(t)
+    tp_all[1].relay()
     tp_all[0].relay()
-    tp_all[1].relay()
     tp_wait(1)
     first(1)
+    second(0)
+    second(2)
+    first(3)
+    second(1)
     tp_wait(0)
     step = 32
 
@@ -702,10 +712,6 @@
     lax.fori_loop(0, rows // step, normalize, 0)
     gates[...] = masked_gates(dot(n1[...], router[...]), hot0[...] + hot1[...])
 
-    second(0)
-    second(2)
-    second(1)
-    first(3)
     third(0)
     third(2)
     third(1)
@@ -1080,7 +1086,6 @@
         dkv[:, s, :, v_at] = d_values.astype(bf16).reshape(PAST + 1, half, HEAD_DIM)
         return carry
 
-    ff.relay()
     for i in (2, 3, 4):
         loads[i].wait()
     lax.fori_loop(0, 2 * heads, attend_back, 0)
@@ -1114,7 +1119,7 @@
     for back in (2, 4, 6, 8):
         to_owner(back).start()
 
-    mixed[...] = ff.total(ff_own[...]).astype(bf16)
+    ff.relay()
     loads[5].wait()
     dz_q = jnp.zeros((rows, 128), f32)
     g_bq = jnp.zeros((128, width), f32)
@@ -1224,8 +1229,19 @@
     for i in range(N_CTX):
         heads_src[i % 2, i // 2] = blocks[i].astype(bf16)
     heads_sum.start()
+    def finish_z():
+        total = z_region(z_part, tp)[...].astype(f32)
+        for d in range(1, N_TP):
+            z_scatter(d).wait_recv()
+            total = total + z_held[d].astype(f32)
+        z_region(z_done, tp)[...] = total.astype(bf16)
+        for d in range(1, N_TP):
+            z_spread(d, tp).start()
+
     along = jnp.zeros((rows, 1), f32)
     for d in (5, 6, 7, 4, 1, 2, 3, 0):
+        if d == FAR:
+            finish_z()
         peer = tp ^ d
         at = pl.ds(pl.multiple_of(peer * part, part), part)
         total = dn[peer] + dot_nt(dz_kv, wide[at, 640:704]) + dot_nt(dkv_own[...], w_kv[at, :])
@@ -1241,20 +1257,14 @@
     tails[tp] = jnp.transpose(dots[...])[:8, :]
     for d in range(1, N_TP):
         tail(d, tp).start()
-    total = z_region(z_part, tp)[...].astype(f32)
-    for d in range(1, N_TP):
-        z_scatter(d).wait_recv()
-        total = total + z_held[d].astype(f32)
-    z_region(z_done, tp)[...] = total.astype(bf16)
-    for d in range(1, N_TP):
-        z_spread(d, tp).start()
     heads_sum.chips()
+    mixed[...] = ff.total(ff_own[...]).astype(bf16)
     scatter.relay()
+    heads_sum.again()
     for d in range(1, N_TP):
         z_spread(d, tp ^ d).wait_recv()
     to_pairs(b_src, slice(0, part), dot_tn(n1_own, z_done[...]))
     b_sum.start()
-    heads_sum.again()
     total = scatter.total(own[...])
     b_sum.chips()
     for d in range(1, N_TP):
@@ -1389,7 +1399,8 @@
 
 
     def by_sequence(a):
-        return jnp.where(adapter_index[0] == 0, a, a[::-1])
+        first = adapter_index[0] == 0
+        return jnp.stack([jnp.where(first, a[0], a[1]), jnp.where(first, a[1], a[0])])
 
     wide_own = by_sequence(adapt_wide.astype(bf16))
     groups = [[6, 10, 7, 11, 8, 12, 9, 13], list(range(14, 22)), [0, 1, 2, 3], [4, 5]]

time: 379 us -> 353 us (0.931); the launches traced: 372 us -> 353 us
  Pallas kernels: 343 us -> 327 us
  local copies, waits for them, and re-layouts: 18.7 us -> 14 us
    pallas_call x1, Pallas kernels: 76.3 us -> 65.2 us  [backward(): pl.pallas_call(backward_kernel, out_shape=(shape((rows, part), bf16), sha...]
    pallas_call x1, Pallas kernels: 201 us -> 194 us  [attention(): pl.pallas_call(attention_kernel, out_shape=any_out + vmem_out, in_specs=[...]
where the time goes in v5:
time: 353 us
  Pallas kernels  327 us (93%)
  local copies, waits for them, and re-layouts  14 us (4%)
  other arithmetic  10.8 us (3%)
    pallas_call x1, Pallas kernels, attention(): pl.pallas_call(attention_kernel, out_shape=any_out + vmem_out, in_specs=[...  194 us
    pallas_call x1, Pallas kernels, feed_forward(): pl.pallas_call(ffn_kernel, out_shape=(shape((N_TP, rows, part), bf16), sh...  67 us
    pallas_call x1, Pallas kernels, backward(): pl.pallas_call(backward_kernel, out_shape=(shape((rows, part), bf16), sha...  65.2 us

profile of v5, /device:TPU:1, one launch (start us, length us, event | category | flops | bytes accessed | tf_op | source)
XLA Modules:
  0.0 352.6 jit_solution(15734806878821307257)
XLA Ops:
  0.7 0.9 multiply_reduce_fusion
  1.6 0.8 fusion.15
  3.2 0.8 fusion.22
  4.1 0.8 convert_reduce_fusion
  5.0 1.0 concatenate.24.table
  7.7 0.6 pad_maximum_fusion.8
  8.3 0.7 pad.58
  10.0 0.7 copy.98
  11.6 1.3 add_add_fusion.s_gu
  13.3 0.9 pad.57.router
  14.2 0.7 copy.103
  14.9 194.4 %attention.1 = (bf16[4,2048,256]{2,1,0:T(8,128)(2,1)}, bf16[2048,512]{1,0:T(8,128)(2,1)}, bf16[4,256,2048]{2,1,0:T(8,128)(2,1)}, bf16[4,2048,1408]{2,1,0:T(8,128...) custom-call(bf16[4,128,256]{2,1,0:T(8,128)(2,1)} %s_q.1, ...), custom_call_target="tpu_custom_call" | custom-call | tf_op jit(solution)/shard_map/attention/pallas_call | solution.py:949
  209.7 0.9 copy.90
  210.6 0.8 pad.68
  211.7 0.9 pad.59.router
  212.6 67.0 %feed_forward.1 = (bf16[8,256,256]{2,1,0:T(8,128)(2,1)}, f32[256,256]{1,0:T(8,128)}, bf16[256,2048]{1,0:T(8,128)(2,1)}, f32[256,256]{1,0:T(8,128)}, bf16[256,204...) custom-call(bf16[256,2048]{1,0:T(8,128)(2,1)} %get-tuple-element.36.x0.h_x, ...), custom_call_target="tpu_custom_call" | custom-call | tf_op jit(solution)/shard_map/feed_forward/pallas_call | solution.py:493
  279.6 1.1 convert_element_type.97
  281.1 1.1 pad_maximum_fusion.1
  282.2 65.2 %backward.1 = (bf16[256,256]{1,0:T(8,128)(2,1)}, bf16[256,256]{1,0:T(8,128)(2,1)}, f32[16,512]{1,0:T(8,128)}, f32[16,256]{1,0:T(8,128)}, bf16[2,8,32,256]{3,2,1,0:T(8,128)(2,1)}) custom-call(bf16[256,2048]{1,0:T(8,128)(2,1)} %get-tuple-element.43.dx1, f32[256,256]{1,0:T(8,128)} %get-tuple-element.44.dx1_own, bf16[2,256,256]{2,1,0:T(8,128)(2,1)} %get-tuple-element.45.ob, ...), custom_call_target="tpu_custom_call" | custom-call | tf_op jit(solution)/shard_map/backward/pallas_call | solution.py:1315
  347.4 1.0 convert_bitcast_fusion
  348.6 0.7 pad_maximum_fusion.5
  350.3 1.0 copy.96
  351.3 0.7 copy.108
  351.9 0.7 copy.109
  (91 shorter events, 6.8 us)
Async XLA Ops:
  0.6 5.4 %copy-start.14 = (s32[2]{0:T(128)S(1)}, s32[2]{0:T(128)}, u32[]{:S(2)}) copy-start(s32[2]{0:T(128)} %param.40) | copy-start | bytes 28
  0.6 5.4 %copy-start.3 = (f32[2,10,16,256]{3,2,1,0:T(8,128)S(1)}, f32[2,10,16,256]{3,2,1,0:T(8,128)}, u32[]{:S(2)}) copy-start(f32[2,10,16,256]{3,2,1,0:T(8,128)} %param.35) | copy-start | bytes 983044
  5.0 4.0 %copy-start.4 = (f32[2,22,16,16]{1,3,2,0:T(8,128)S(1)}, f32[2,22,16,16]{1,3,2,0:T(8,128)}, u32[]{:S(2)}) copy-start(f32[2,22,16,16]{1,3,2,0:T(8,128)} %param.34) | copy-start | bytes 135172
  6.1 3.3 copy-start.13
  6.1 4.6 %copy-start = (bf16[4,128,2,704]{1,3,2,0:T(8,128)(2,1)S(1)}, bf16[4,128,2,704]{1,3,2,0:T(8,128)(2,1)}, u32[]{:S(2)}) copy-start(bf16[4,128,2,704]{1,3,2,0:T(8,128)(2,1)} %param.32) | copy-start | bytes 4325380
  11.6 1.4 copy-start.9
  13.0 1.2 copy-start.5
  14.9 194.4 %copy-start.1 = (f32[2,12,16,704]{3,2,1,0:T(8,128)S(1)}, f32[2,12,16,704]{3,2,1,0:T(8,128)}, u32[]{:S(2)}) copy-start(f32[2,12,16,704]{3,2,1,0:T(8,128)} %param.36) | copy-start | bytes 3244036
  209.7 1.7 copy-start.10
  279.6 1.3 copy-start.2
  348.5 0.9 copy-start.8
  348.5 0.9 copy-start.11
  348.5 1.0 copy-start.12
  349.6 1.7 copy-start.7
  349.6 2.3 copy-start.6

commit v6 on v5

--- a/solution.py
+++ b/solution.py
@@ -255,18 +255,22 @@
 
 
 def ffn_kernel(
-    x0, attn, dy, gain, wide, router, table, b_gu, a_d, z_o, w_gu_hbm, w_d_hbm,
+    gain, router, table, b_gu, a_d, z_o, h_x0, h_attn, h_wide, h_dy, w_gu_hbm, w_d_hbm,
     ff_parts, ff_own, dx1, dx1_own, n2, z_sum, gu_out, d_out,
-    w_gu, w_d, hg, dgu, dh_tmp, z_gu, dz_d, z_part, parts, relay, own, held, z_held, dots, tails, inverse,
+    x0, attn, wide, dy, w_gu, w_d, hg, dgu, dh_tmp, z_gu, dz_d, z_part, parts, relay, own, held, z_held, dots, tails, inverse,
     g_gu, g_d, gu_src, gu_core, gu_held, d_src, d_core, d_held,
-    load, send, recv, ctx_send, ctx_recv,
+    load, small_load, send, recv, ctx_send, ctx_recv,
 ):
     me, tp = lax.axis_index("ctx"), lax.axis_index("tp")
     hot = table.at[:, 512:640]
     rows, model = x0.shape
     experts = w_gu.shape[0]
     part = model // N_TP
-    greet([(me ^ d, tp) for d in range(1, N_CTX)] + [(me, tp ^ d) for d in range(1, N_TP)])
+    smalls = []
+    for i, (h, v) in enumerate(((h_x0, x0), (h_attn, attn), (h_wide, wide), (h_dy, dy))):
+        c = pltpu.make_async_copy(h, v, small_load.at[i])
+        c.start()
+        smalls.append(c)
 
     def fetch(e):
         return (
@@ -274,10 +278,13 @@
             pltpu.make_async_copy(w_d_hbm.at[e], w_d.at[e], load.at[1, e]),
         )
 
+
+    greet([(me ^ d, tp) for d in range(1, N_CTX)] + [(me, tp ^ d) for d in range(1, N_TP)])
     for e in range(experts):
         for c in fetch(e):
             c.start()
-
+    for c in smalls:
+        c.wait()
     step = 32
 
     def normalize(i, carry):
@@ -484,8 +491,10 @@
         tail(d, tp).wait_send()
 
 
-def feed_forward(x0, attn, dy, gain, wide, router, table, b_gu, a_d, z_o, w_gu, w_d):
+def feed_forward(small, large):
+    x0, attn, wide, dy, w_gu, w_d = large
     rows, model = x0.shape
+    b_gu, a_d = small[3], small[4]
     part = model // N_TP
     experts, _, cols = w_gu.shape
     hidden = w_d.shape[1]
@@ -502,11 +511,12 @@
             shape((2, 8, 16, 768), bf16),
             shape((2, 8, 8, hidden), f32),
         ),
-        in_specs=[VMEM] * 10 + [ANY] * 2,
+        in_specs=[VMEM] * len(small) + [ANY] * len(large),
         out_specs=tuple([VMEM] * 8),
         scratch_shapes=[
-            pltpu.VMEM(w_gu.shape, bf16),
-            pltpu.VMEM(w_d.shape, bf16),
+            pltpu.VMEM(a.shape, bf16) for a in large
+        ]
+        + [
             pltpu.VMEM((experts, rows, hidden), bf16),
             pltpu.VMEM((experts, rows, cols), bf16),
             pltpu.VMEM((rows, 768), f32),
@@ -530,6 +540,7 @@
             pltpu.VMEM((8, 8, hidden), f32),
             pltpu.VMEM((8, 8, hidden), f32),
             pltpu.SemaphoreType.DMA((2, experts)),
+            pltpu.SemaphoreType.DMA((4,)),
             pltpu.SemaphoreType.DMA((6, N_TP)),
             pltpu.SemaphoreType.DMA((6, N_TP)),
             pltpu.SemaphoreType.DMA((2, 16)),
@@ -539,7 +550,7 @@
             collective_id=2, has_side_effects=True, vmem_limit_bytes=63 << 20
         ),
         name="feed_forward",
-    )(x0, attn, dy, gain, wide, router, table, b_gu, a_d, z_o, w_gu, w_d)
+    )(*small, *large)
 
 
 def widen_routes(routes, experts):
@@ -558,12 +569,12 @@
 
 
 def attention_kernel(
-    s_q, s_kv, s_o, s_gu, s_d, tokens, cotangent, s_wide,
+    s_q, s_kv, s_o, s_gu, s_d, tokens, cotangent, s_wide, s_rest,
     gain, router, table, k_doc, b_q, b_kv, a_o,
-    g_q, g_kv, g_o, g_gu, g_d, g_wide, wide_mid, dy,
-    x0, attn, n1, kv_all, q_all, probs, ob, z_o, z_q, z_kv, gates,
-    w_q, w_kv, w_o, wide, parts, relay, own, held,
-    send, recv, local, tp_send, tp_recv, tp_local, kv_send, kv_recv, load, sum_send, sum_recv,
+    g_q, g_kv, g_o, g_gu, g_d, g_wide, wide_mid, dy, g_rest,
+    h_n1, h_kv_all, h_q_all, h_probs, x0, attn, ob, z_o, z_q, z_kv, gates,
+    n1, kv_all, q_all, probs, w_q, w_kv, w_o, wide, rest, parts, relay, own, held,
+    send, recv, local, tp_send, tp_recv, tp_local, kv_send, kv_recv, load, store, rest_send, rest_recv, sum_send, sum_recv,
 ):
     me, tp = lax.axis_index("ctx"), lax.axis_index("tp")
     core, side = me ^ 1, me ^ 2
@@ -578,7 +589,7 @@
     width = w_q.shape[2]
     heads = width // HEAD_DIM
     span = (PAST + 1) * half
-    greet([(d, tp) for d in (core, side, up, down, far)] + [(me, tp ^ d) for d in range(1, N_TP)])
+    greet([(core, tp)] + [(me ^ (2 * d), tp) for d in range(1, 8)] + [(me, tp ^ d) for d in range(1, N_TP)])
 
     kinds = ["flat", "flat", "rows", "cols"] + ["flat"] * experts + ["pair"] * (experts // 2)
     src = [s_kv, wide_mid, s_q, s_o] + [s_gu.at[e] for e in range(experts)]
@@ -689,6 +700,37 @@
             copy(t, 12 + item, owner ^ 1, low, high, core, 0, False).wait_recv()
         copy(t, 24, core, 0, 4, core, 0, False).wait_recv()
 
+    def rest_copy(item, owner, to, source=None):
+        there = g_rest.at[owner, tp]
+        return pltpu.make_async_remote_copy(
+            src_ref=there if source is None else source,
+            dst_ref=there,
+            send_sem=rest_send.at[item],
+            recv_sem=rest_recv.at[item],
+            device_id=(to, tp),
+            device_id_type=MESH,
+        )
+
+    rest_all = Spread(None, lambda rank: g_rest.at[:, rank], tp_send, tp_recv, 3)
+    rest_own = pltpu.make_async_copy(s_rest, g_rest.at[me, tp], tp_local.at[3])
+
+    def rest_start():
+        rest_own.start()
+        for d in range(1, 8):
+            rest_copy(d, me, me ^ (2 * d), s_rest).start()
+        rest_copy(8, me, core, s_rest).start()
+
+    def rest_core():
+        for d in range(1, 8):
+            rest_copy(d, me ^ (2 * d), core).wait_recv()
+            rest_copy(8 + d, me ^ (2 * d), core).start()
+
+    def rest_spread():
+        for d in range(8):
+            rest_copy(8 + d, core ^ (2 * d), core).wait_recv()
+        rest_own.wait()
+        rest_all.start()
+
     tp_start(1)
     tp_start(0)
     for t in (0, 2):
@@ -697,6 +739,7 @@
     tp_all[0].relay()
     tp_wait(1)
     first(1)
+    rest_start()
     second(0)
     second(2)
     first(3)
@@ -736,11 +779,12 @@
     def rotary(x):
         return x * cosine[...] + pltpu.roll(x, HEAD_DIM // 2, 1) * sine[...]
 
+    rest_core()
     fetches[0].wait()
     fetches[1].wait()
-    z = dot(n1[...], wide[:, 512:640])
+    z = dot(n1[...], wide[:, :128])
     z_q[...] = jnp.where(lane // 64 == seq, z, 0.0).astype(bf16)
-    z = dot(n1[...], wide[:, 640:704])
+    z = dot(n1[...], wide[:, 128:192])
     z_kv[...] = jnp.where((lane // 16) % 2 == seq, jnp.pad(z, ((0, 0), (0, 64))), 0.0).astype(bf16)
     kv = dot(n1[...], w_kv[...]) + dot(z_kv[:, :64], b_kv[...])
     for h in range(heads):
@@ -793,6 +837,7 @@
             for s in range(2):
                 q_all[s * heads + h, k * half : k * half + half, :] = turned[half * s : half * s + half]
 
+    rest_spread()
     tp_start(2)
     second(4)
     kv_arrived(4)
@@ -815,6 +860,7 @@
     first(9)
     for back in (1, 3, 5, 7):
         kv_arrived(back)
+    rest_all.relay()
     tp_all[2].relay()
     second(6)
 
@@ -843,11 +889,20 @@
         return carry
 
     lax.fori_loop(0, 2 * heads, attend, 0)
+    stores = []
+    for i, (v, h) in enumerate(((n1, h_n1), (kv_all, h_kv_all), (q_all, h_q_all), (probs, h_probs))):
+        c = pltpu.make_async_copy(v, h, store.at[i])
+        c.start()
+        stores.append(c)
     fourth(3)
     third(4)
     fetches.append(fetch(3, w_o))
+    rest_all.wait()
+    rest_load = pltpu.make_async_copy(g_rest, rest, load.at[4])
+    rest_load.start()
 
     fetches[3].wait()
+    rest_load.wait()
     z_acc = jnp.zeros((rows, 256), f32)
     pair_lane = lax.broadcasted_iota(jnp.int32, (rows, 256), 1)
     mine = pair_lane // 128 == lax.broadcasted_iota(jnp.int32, (rows, 256), 0) // half
@@ -869,7 +924,7 @@
     spread = Spread(None, lambda rank: columns(attn, rank), sum_send, sum_recv, 1)
     for d in (5, 6, 7, 4, 1, 2, 3, 0):
         at = pl.ds(pl.multiple_of((tp ^ d) * part, part), part)
-        total = dot_nt(z_acc, wide[at, 256:512])
+        total = dot_nt(z_acc, rest[pl.ds(2 * (tp ^ d), 2), :, :, 256:512].reshape(part, 256))
         for e in range(experts):
             total = total + dot(chosen[e], w_o[e, :, at]) * gates[:, e : e + 1]
         if d:
@@ -900,6 +955,8 @@
     tp_wait(2)
     for t in range(4, len(kinds)):
         finish(t)
+    for c in stores:
+        c.wait()
     for c in started:
         c.wait_send()
     for t, c in enumerate(staying):
@@ -912,13 +969,17 @@
             pl.when(condition)(c.wait_send)
     scatter.sent()
     spread.sent()
-    for c in tp_all:
+    for c in tp_all + [rest_all]:
         c.sent()
+    for d in range(1, 8):
+        rest_copy(d, me, me ^ (2 * d), s_rest).wait_send()
+        rest_copy(8 + d, me ^ (2 * d), core).wait_send()
+    rest_copy(8, me, core, s_rest).wait_send()
 
 
 def attention(shards_in, tp_shards, small):
     s_q, s_kv, s_o, s_gu, s_d = shards_in
-    tokens, cotangent, s_wide = tp_shards
+    tokens, cotangent, s_wide, s_rest = tp_shards
     rows, part = tokens.shape
     model = part * N_TP
     experts, _, width = s_q.shape
@@ -932,30 +993,35 @@
     gathered = (grown(s_q, 1), grown(s_kv, 0), grown(s_o, 2), grown(s_gu, 1), grown(s_d, 2))
     wide_mid = shape((s_wide.shape[0] * N_TP, s_wide.shape[1]), bf16)
     wide = grown(wide_mid, 0)
-    vmem_out = (
-        shape((rows, model), bf16),
-        shape((rows, model), bf16),
+    rest = shape((N_CTX, N_TP) + s_rest.shape, bf16)
+    kept = (
         shape((rows, model), bf16),
         shape((PAST + 1, 2, half, 2 * width), bf16),
         shape((2 * heads, rows, HEAD_DIM), bf16),
         shape((2 * heads, rows, (PAST + 1) * half), bf16),
+    )
+    vmem_out = (
+        shape((rows, model), bf16),
+        shape((rows, model), bf16),
         shape((2, rows, width), bf16),
         shape((rows, 128), bf16),
         shape((rows, 128), bf16),
         shape((rows, 128), bf16),
         shape((rows, 128), f32),
     )
-    any_out = gathered + (wide, wide_mid, shape((rows, model), bf16))
+    any_out = gathered + (wide, wide_mid, shape((rows, model), bf16), rest) + kept
     return pl.pallas_call(
         attention_kernel,
         out_shape=any_out + vmem_out,
-        in_specs=[ANY] * 8 + [VMEM] * len(small),
+        in_specs=[ANY] * 9 + [VMEM] * len(small),
         out_specs=tuple([ANY] * len(any_out) + [VMEM] * len(vmem_out)),
-        scratch_shapes=[
+        scratch_shapes=[pltpu.VMEM(a.shape, bf16) for a in kept]
+        + [
             pltpu.VMEM(gathered[0].shape, bf16),
             pltpu.VMEM(gathered[1].shape, bf16),
             pltpu.VMEM(gathered[2].shape, bf16),
             pltpu.VMEM(wide.shape, bf16),
+            pltpu.VMEM(rest.shape, bf16),
             pltpu.VMEM((N_TP, rows, part), bf16),
             pltpu.VMEM((rows, part), bf16),
             pltpu.VMEM((rows, part), f32),
@@ -963,12 +1029,15 @@
             pltpu.SemaphoreType.DMA((10, 25)),
             pltpu.SemaphoreType.DMA((10, 25)),
             pltpu.SemaphoreType.DMA((10,)),
-            pltpu.SemaphoreType.DMA((3, N_TP)),
-            pltpu.SemaphoreType.DMA((3, N_TP)),
-            pltpu.SemaphoreType.DMA((3,)),
+            pltpu.SemaphoreType.DMA((4, N_TP)),
+            pltpu.SemaphoreType.DMA((4, N_TP)),
+            pltpu.SemaphoreType.DMA((4,)),
             pltpu.SemaphoreType.DMA((14,)),
             pltpu.SemaphoreType.DMA((PAST + 1,)),
+            pltpu.SemaphoreType.DMA((5,)),
             pltpu.SemaphoreType.DMA((4,)),
+            pltpu.SemaphoreType.DMA((16,)),
+            pltpu.SemaphoreType.DMA((16,)),
             pltpu.SemaphoreType.DMA((2, N_TP)),
             pltpu.SemaphoreType.DMA((2, N_TP)),
         ],
@@ -981,9 +1050,9 @@
 
 def backward_kernel(
     dx1, dx1_own, ob, gates, z_q, z_kv, z_sum, table, gain, router, b_q, b_kv, a_o, ff_parts, ff_own,
-    h_q, h_kv, h_o, h_wide, h_x0, h_n1, h_n2, h_dy, h_kv_all, h_q_all, h_probs,
+    h_q, h_kv, h_o, h_wide, h_rest, h_x0, h_n1, h_n2, h_dy, h_kv_all, h_q_all, h_probs,
     mixed, grad_tokens, wide_a, wide_b, heads_out,
-    w_q, w_kv, w_o, wide, x0, n1, n2, dy, kv_all, q_all, probs, dob, dkv, dkv_held, dq, dkv_own, dn, parts, relay, own, held, ff_held, ff_relay,
+    w_q, w_kv, w_o, wide, rest, x0, n1, n2, dy, kv_all, q_all, probs, dob, dkv, dkv_held, dq, dkv_own, dn, parts, relay, own, held, ff_held, ff_relay,
     z_part, z_held, z_done, dots, tails, a_src, b_src, heads_src, a_core, b_core, heads_core, a_held, b_held, heads_held,
     load, tp_send, tp_recv, core_send, core_recv, kv_send, kv_recv, ctx_send, ctx_recv,
 ):
@@ -1001,7 +1070,7 @@
     loads = []
     for i, (h, w) in enumerate(
         (
-            (h_wide, wide),
+            (h_rest, rest),
             (h_o, w_o),
             (h_kv_all, kv_all),
             (h_probs, probs),
@@ -1012,6 +1081,7 @@
             (h_n1, n1),
             (h_kv, w_kv),
             (h_x0, x0),
+            (h_wide, wide),
         )
     ):
         c = pltpu.make_async_copy(h, w, load.at[i])
@@ -1032,7 +1102,7 @@
     loads[0].wait()
     pair_lane = lax.broadcasted_iota(jnp.int32, (rows, 256), 1)
     mine = pair_lane // 128 == lax.broadcasted_iota(jnp.int32, (rows, 256), 0) // half
-    dz_o = dot(dx1[...], wide[:, 256:512])
+    dz_o = dot(dx1[...], rest[:, 256:512])
     loads[1].wait()
     g = [jnp.zeros((rows, width), f32), jnp.zeros((rows, width), f32)]
     g_ao = jnp.zeros((256, width), f32)
@@ -1121,6 +1191,7 @@
 
     ff.relay()
     loads[5].wait()
+    loads[11].wait()
     dz_q = jnp.zeros((rows, 128), f32)
     g_bq = jnp.zeros((128, width), f32)
     chosen = []
@@ -1137,7 +1208,7 @@
     z_part[:, :128] = dz_q
     for j in range(N_TP):
         at = slice(part * j, part * j + part)
-        total = dot_nt(dz_q, wide[at, 512:640]) + dot_nt(d_logits, router[at, :])
+        total = dot_nt(dz_q, wide[at, :128]) + dot_nt(d_logits, router[at, :])
         for e in range(experts):
             total = total + dot_nt(chosen[e], w_q[e, at, :])
         dn[j] = total
@@ -1244,7 +1315,7 @@
             finish_z()
         peer = tp ^ d
         at = pl.ds(pl.multiple_of(peer * part, part), part)
-        total = dn[peer] + dot_nt(dz_kv, wide[at, 640:704]) + dot_nt(dkv_own[...], w_kv[at, :])
+        total = dn[peer] + dot_nt(dz_kv, wide[at, 128:192]) + dot_nt(dkv_own[...], w_kv[at, :])
         scaled = total * gain[:, at]
         along = along + jnp.sum(scaled * x0[:, at].astype(f32), axis=1, keepdims=True)
         if d:
@@ -1304,7 +1375,7 @@
 
 def backward(vmem, hbm):
     dx1 = vmem[0]
-    w_q, w_kv, w_o, wide, x0, n1, n2, dy, kv_all, q_all, probs = hbm
+    w_q = hbm[0]
     rows, model = dx1.shape
     part = model // N_TP
     width = w_q.shape[2]
@@ -1328,8 +1399,8 @@
         ]
         + [
             pltpu.VMEM((2 * heads, rows, HEAD_DIM), bf16),
-            pltpu.VMEM(kv_all.shape, bf16),
-            pltpu.VMEM((8,) + kv_all.shape[1:], bf16),
+            pltpu.VMEM(hbm[9].shape, bf16),
+            pltpu.VMEM((8,) + hbm[9].shape[1:], bf16),
             pltpu.VMEM((2, rows, width), bf16),
             pltpu.VMEM((rows, 2 * width), bf16),
             pltpu.VMEM((N_TP, rows, part), f32),
@@ -1450,8 +1521,8 @@
     )
     router_wide = jnp.pad(router_attn, ((0, 0), (0, 128 - experts)))
     (
-        w_query, w_key_value, w_out, w_gate_up, w_down, wide, _, dy,
-        x0, sum_out, n1, kv_all, q_all, probs, ob, z_o_gated, z_q, z_kv, gates,
+        w_query, w_key_value, w_out, w_gate_up, w_down, wide, _, dy, rest,
+        n1, kv_all, q_all, probs, x0, sum_out, ob, z_o_gated, z_q, z_kv, gates,
     ) = attention(
         [
             w_query,
@@ -1460,7 +1531,7 @@
             gate_up_columns(w_gate_up[:, :, 0], w_gate_up[:, :, 1]),
             w_down,
         ],
-        [tokens.reshape(rows, part), cotangent.reshape(rows, part), wide_cols],
+        [tokens.reshape(rows, part), cotangent.reshape(rows, part), wide_cols[:, 512:], wide_cols[:, :512]],
         [
             norm1_gain[None],
             router_wide,
@@ -1477,16 +1548,23 @@
         axis=2,
     ).reshape(seqs, 2 * experts * rank, 2 * hidden)
     a_d = jnp.pad(ffn_low[:, 2 * experts :].reshape(seqs, experts * rank, hidden), ((0, 0), (64, 0), (0, 0)))
+    rest = rest.reshape(model, 512)
     ff_parts, ff_own, dx1b, dx1_own, n2, z_sum, gu_sum, d_sum = feed_forward(
-        x0, sum_out, dy, norm2_gain[None], wide,
-        jnp.pad(router_ffn, ((0, 0), (0, 128 - experts))),
-        table, b_gu.reshape(256, 2 * hidden), a_d.reshape(256, hidden), z_o_gated, w_gate_up, w_down,
+        [
+            norm2_gain[None],
+            jnp.pad(router_ffn, ((0, 0), (0, 128 - experts))),
+            table,
+            b_gu.reshape(256, 2 * hidden),
+            a_d.reshape(256, hidden),
+            z_o_gated,
+        ],
+        [x0, sum_out, rest, dy, w_gate_up, w_down],
     )
     mixed, grad_tokens, wide_a, wide_b, head_sum = backward(
         [
             dx1b, dx1_own, ob, gates, z_q, z_kv, z_sum, table, norm1_gain[None], router_wide, b_q, b_kv_wide, a_o_wide, ff_parts, ff_own,
         ],
-        [w_query, w_key_value, w_out, wide, x0, n1, n2, dy, kv_all, q_all, probs],
+        [w_query, w_key_value, w_out, wide, rest, x0, n1, n2, dy, kv_all, q_all, probs],
     )
     grad_wide = jnp.concatenate([wide_a, wide_b[:, : 704 - 512]], axis=1).T
     back_order = np.argsort(np.array([q * wide_slots + s for q, s in order]))

time: 353 us -> 344 us (0.975)
  Pallas kernels: 327 us -> 317 us
    pallas_call x1, Pallas kernels: 194 us -> 187 us  [attention(): pl.pallas_call(attention_kernel, out_shape=any_out + vmem_out, in_specs=[...]
where the time goes in v6:
time: 344 us
  Pallas kernels  317 us (92%)
  local copies, waits for them, and re-layouts  14.6 us (4%)
  other arithmetic  10.7 us (3%)
    pallas_call x1, Pallas kernels, attention(): pl.pallas_call(attention_kernel, out_shape=any_out + vmem_out, in_specs=[...  187 us
    pallas_call x1, Pallas kernels, backward(): pl.pallas_call(backward_kernel, out_shape=(shape((rows, part), bf16), sha...  65.6 us
    pallas_call x1, Pallas kernels, feed_forward(): pl.pallas_call(ffn_kernel, out_shape=(shape((N_TP, rows, part), bf16), sh...  64.2 us

profile of v6, /device:TPU:1, one launch (start us, length us, event | category | flops | bytes accessed | tf_op | source)
XLA Modules:
  0.0 343.5 jit_solution(12405270848661269459)
XLA Ops:
  0.7 0.9 multiply_reduce_fusion
  1.6 0.8 fusion.15
  3.2 0.8 fusion.22
  4.1 0.8 convert_reduce_fusion
  5.0 1.0 concatenate.24.table
  7.0 0.6 broadcast_in_dim.94.k_doc
  7.7 0.6 pad_maximum_fusion.8
  8.3 0.7 pad.68
  12.2 1.3 add_add_fusion.s_gu
  13.8 0.9 pad.67.router
  14.7 0.7 copy.103
  15.4 187.2 %attention.1 = (bf16[4,2048,256]{2,1,0:T(8,128)(2,1)}, bf16[2048,512]{1,0:T(8,128)(2,1)}, bf16[4,256,2048]{2,1,0:T(8,128)(2,1)}, bf16[4,2048,1408]{2,1,0:T(8,128...) custom-call(bf16[4,128,256]{2,1,0:T(8,128)(2,1)} %s_q.1, ...), custom_call_target="tpu_custom_call" | custom-call | tf_op jit(solution)/shard_map/attention/pallas_call | solution.py:1013
  203.1 0.9 copy.84
  204.0 0.8 pad.62
  205.1 0.9 pad.53.router
  206.0 64.2 %feed_forward.1 = (bf16[8,256,256]{2,1,0:T(8,128)(2,1)}, f32[256,256]{1,0:T(8,128)}, bf16[256,2048]{1,0:T(8,128)(2,1)}, f32[256,256]{1,0:T(8,128)}, bf16[256,204...) custom-call(f32[1,2048]{1,0:T(1,128)} %bitcast.106, ...), custom_call_target="tpu_custom_call" | custom-call | tf_op jit(solution)/shard_map/feed_forward/pallas_call | solution.py:502
  270.2 1.1 convert_element_type.97
  271.7 1.1 pad_maximum_fusion.1
  272.8 65.6 %backward.1 = (bf16[256,256]{1,0:T(8,128)(2,1)}, bf16[256,256]{1,0:T(8,128)(2,1)}, f32[16,512]{1,0:T(8,128)}, f32[16,256]{1,0:T(8,128)}, bf16[2,8,32,256]{3,2,1,0:T(8,128)(2,1)}) custom-call(bf16[256,2048]{1,0:T(8,128)(2,1)} %get-tuple-element.44.dx1, f32[256,256]{1,0:T(8,128)} %get-tuple-element.45.dx1_own, bf16[2,256,256]{2,1,0:T(8,128)(2,1)} %get-tuple-element.46.ob, ...), custom_call_target="tpu_custom_call" | custom-call | tf_op jit(solution)/shard_map/backward/pallas_call | solution.py:1386
  338.4 1.0 convert_bitcast_fusion
  339.6 0.7 pad_maximum_fusion.5
  341.2 1.0 copy.96
  342.2 0.7 copy.108
  342.9 0.7 copy.109
  (93 shorter events, 7.4 us)
Async XLA Ops:
  0.6 5.4 %copy-start.14 = (s32[2]{0:T(128)S(1)}, s32[2]{0:T(128)}, u32[]{:S(2)}) copy-start(s32[2]{0:T(128)} %param.40) | copy-start | bytes 28
  0.6 5.4 %copy-start.3 = (f32[2,10,16,256]{3,2,1,0:T(8,128)S(1)}, f32[2,10,16,256]{3,2,1,0:T(8,128)}, u32[]{:S(2)}) copy-start(f32[2,10,16,256]{3,2,1,0:T(8,128)} %param.35) | copy-start | bytes 983044
  5.0 4.0 %copy-start.4 = (f32[2,22,16,16]{1,3,2,0:T(8,128)S(1)}, f32[2,22,16,16]{1,3,2,0:T(8,128)}, u32[]{:S(2)}) copy-start(f32[2,22,16,16]{1,3,2,0:T(8,128)} %param.34) | copy-start | bytes 135172
  6.1 3.3 copy-start.13
  6.1 5.2 %copy-start = (bf16[4,128,2,704]{1,3,2,0:T(8,128)(2,1)S(1)}, bf16[4,128,2,704]{1,3,2,0:T(8,128)(2,1)}, u32[]{:S(2)}) copy-start(bf16[4,128,2,704]{1,3,2,0:T(8,128)(2,1)} %param.32) | copy-start | bytes 4325380
  12.2 1.3 copy-start.9
  13.5 1.2 copy-start.5
  15.4 187.3 %copy-start.1 = (f32[2,12,16,704]{3,2,1,0:T(8,128)S(1)}, f32[2,12,16,704]{3,2,1,0:T(8,128)}, u32[]{:S(2)}) copy-start(f32[2,12,16,704]{3,2,1,0:T(8,128)} %param.36) | copy-start | bytes 3244036
  203.1 1.7 copy-start.10
  270.2 1.3 copy-start.2
  339.4 0.9 copy-start.8
  339.4 0.9 copy-start.11
  339.5 1.0 copy-start.12
  340.5 1.7 copy-start.7
  340.5 2.3 copy-start.6

commit v7 on v6

--- a/solution.py
+++ b/solution.py
@@ -634,7 +634,7 @@
         c.start()
         started.append(c)
 
-    cuts = [2, 2, 3, 3, 3, 3, 3, 2, 2, 2]
+    cuts = [2, 2, 3, 3, 3, 3, 3, 3, 2, 2]
 
     def arrive(t, item):
         cut = cuts[t]

time: 344 us -> 347 us (level)
    pallas_call x1, Pallas kernels: 187 us -> 191 us  [attention(): pl.pallas_call(attention_kernel, out_shape=any_out + vmem_out, in_specs=[...]
where the time goes in v7:
time: 347 us
  Pallas kernels  320 us (92%)
  local copies, waits for them, and re-layouts  14.6 us (4%)
  other arithmetic  10.7 us (3%)
    pallas_call x1, Pallas kernels, attention(): pl.pallas_call(attention_kernel, out_shape=any_out + vmem_out, in_specs=[...  191 us
    pallas_call x1, Pallas kernels, backward(): pl.pallas_call(backward_kernel, out_shape=(shape((rows, part), bf16), sha...  66.3 us
    pallas_call x1, Pallas kernels, feed_forward(): pl.pallas_call(ffn_kernel, out_shape=(shape((N_TP, rows, part), bf16), sh...  62.8 us

profile of v7, /device:TPU:1, one launch (start us, length us, event | category | flops | bytes accessed | tf_op | source)
XLA Modules:
  0.0 346.8 jit_solution(13146526214205733499)
XLA Ops:
  0.7 0.9 multiply_reduce_fusion
  1.6 0.8 fusion.15
  3.2 0.8 fusion.22
  4.1 0.8 convert_reduce_fusion
  5.0 1.0 concatenate.24.table
  7.0 0.6 broadcast_in_dim.94.k_doc
  7.7 0.6 pad_maximum_fusion.8
  8.3 0.7 pad.68
  12.2 1.3 add_add_fusion.s_gu
  13.8 0.9 pad.67.router
  14.7 0.7 copy.103
  15.4 191.1 %attention.1 = (bf16[4,2048,256]{2,1,0:T(8,128)(2,1)}, bf16[2048,512]{1,0:T(8,128)(2,1)}, bf16[4,256,2048]{2,1,0:T(8,128)(2,1)}, bf16[4,2048,1408]{2,1,0:T(8,128...) custom-call(bf16[4,128,256]{2,1,0:T(8,128)(2,1)} %s_q.1, ...), custom_call_target="tpu_custom_call" | custom-call | tf_op jit(solution)/shard_map/attention/pallas_call | solution.py:1013
  206.9 0.9 copy.84
  207.9 0.8 pad.62
  209.0 0.9 pad.53.router
  209.9 62.8 %feed_forward.1 = (bf16[8,256,256]{2,1,0:T(8,128)(2,1)}, f32[256,256]{1,0:T(8,128)}, bf16[256,2048]{1,0:T(8,128)(2,1)}, f32[256,256]{1,0:T(8,128)}, bf16[256,204...) custom-call(f32[1,2048]{1,0:T(1,128)} %bitcast.106, ...), custom_call_target="tpu_custom_call" | custom-call | tf_op jit(solution)/shard_map/feed_forward/pallas_call | solution.py:502
  272.7 1.1 convert_element_type.97
  274.2 1.1 pad_maximum_fusion.1
  275.3 66.3 %backward.1 = (bf16[256,256]{1,0:T(8,128)(2,1)}, bf16[256,256]{1,0:T(8,128)(2,1)}, f32[16,512]{1,0:T(8,128)}, f32[16,256]{1,0:T(8,128)}, bf16[2,8,32,256]{3,2,1,0:T(8,128)(2,1)}) custom-call(bf16[256,2048]{1,0:T(8,128)(2,1)} %get-tuple-element.44.dx1, f32[256,256]{1,0:T(8,128)} %get-tuple-element.45.dx1_own, bf16[2,256,256]{2,1,0:T(8,128)(2,1)} %get-tuple-element.46.ob, ...), custom_call_target="tpu_custom_call" | custom-call | tf_op jit(solution)/shard_map/backward/pallas_call | solution.py:1386
  341.6 1.0 convert_bitcast_fusion
  342.8 0.7 pad_maximum_fusion.5
  344.5 1.0 copy.96
  345.4 0.7 copy.108
  346.1 0.7 copy.109
  (93 shorter events, 7.4 us)
Async XLA Ops:
  0.6 5.4 %copy-start.14 = (s32[2]{0:T(128)S(1)}, s32[2]{0:T(128)}, u32[]{:S(2)}) copy-start(s32[2]{0:T(128)} %param.40) | copy-start | bytes 28
  0.6 5.4 %copy-start.3 = (f32[2,10,16,256]{3,2,1,0:T(8,128)S(1)}, f32[2,10,16,256]{3,2,1,0:T(8,128)}, u32[]{:S(2)}) copy-start(f32[2,10,16,256]{3,2,1,0:T(8,128)} %param.35) | copy-start | bytes 983044
  5.0 4.0 %copy-start.4 = (f32[2,22,16,16]{1,3,2,0:T(8,128)S(1)}, f32[2,22,16,16]{1,3,2,0:T(8,128)}, u32[]{:S(2)}) copy-start(f32[2,22,16,16]{1,3,2,0:T(8,128)} %param.34) | copy-start | bytes 135172
  6.1 3.3 copy-start.13
  6.1 5.2 %copy-start = (bf16[4,128,2,704]{1,3,2,0:T(8,128)(2,1)S(1)}, bf16[4,128,2,704]{1,3,2,0:T(8,128)(2,1)}, u32[]{:S(2)}) copy-start(bf16[4,128,2,704]{1,3,2,0:T(8,128)(2,1)} %param.32) | copy-start | bytes 4325380
  12.2 1.3 copy-start.9
  13.5 1.2 copy-start.5
  15.4 191.1 %copy-start.1 = (f32[2,12,16,704]{3,2,1,0:T(8,128)S(1)}, f32[2,12,16,704]{3,2,1,0:T(8,128)}, u32[]{:S(2)}) copy-start(f32[2,12,16,704]{3,2,1,0:T(8,128)} %param.36) | copy-start | bytes 3244036
  206.9 1.7 copy-start.10
  272.7 1.3 copy-start.2
  342.7 0.9 copy-start.8
  342.7 0.9 copy-start.11
  342.7 1.0 copy-start.12
  343.7 1.7 copy-start.7
  343.8 2.3 copy-start.6
